TPU v7x, 256 devices: a whole 4x4x8 slice. The times are simulated.
256 devices in a mesh: frow: 16 (over z_hi, y), fcol: 16 (over z_lo, x, core).
Axes of the slice: x: 4, y: 4, z: 8 (z_hi: 4, z_lo: 2; z = z_hi * 2 + z_lo), core: 2. Of those that a mesh axis runs over, the one named last changes fastest.
Arguments:
- image: bfloat16 [2, 8192, 8192], P(None, 'frow', 'fcol'), may hold values from -6 to 6
- window_rows: float32 [8192], P('frow'), may hold values from 0.1 to 1.9
- window_cols: float32 [8192], P('fcol'), may hold values from 0.1 to 1.9
- w_terms: float32 [2], replicated, may hold values from 20 to 200
- facet_row_offset: int32 [16], replicated, may hold values from 0 to 65535
- facet_col_offset: int32 [16], replicated, may hold values from 0 to 65535
- band_offset: int32 [2], replicated, may hold values from 0 to 65535
- sub_row_offset: int32 [2], replicated, may hold values from 0 to 65535
- sub_column: int32 [2], replicated, may hold values from 0 to 1, as said below
Outputs:
- subgrids: float32 [2, 2, 512, 512], P(None, None, 'frow', 'fcol')
Inputs may be any that keep to these rules, and one draw needn't show every extreme that they name: `sub_column`: every subgrid column holds exactly 1 subgrids.
All inputs are finite; a program needn't handle non-finite values.
Results may differ from a plain program's by a relative error of at most 0.0052.
Values sent between devices are 32-bit elements; how exact they have to be, the bound alone decides.
No kernel may reach another device: no remote copies, remote signals or barrier semaphores. Data moves between devices by JAX's collectives and lax.ppermute only.
A program may use at most 64 MiB of HBM per device.

v0:
```python
import math

import jax
import jax.numpy as jnp
from jax import lax
from jax.sharding import Mesh
from jax.sharding import PartitionSpec as P

SG = 512
IMAGE = 65536
FCOL = ("fcol_0", "fcol_1", "fcol_2")


def cut_along(shard, dim, count):
    before, after = (shard.shape[:dim], shard.shape[dim + 1 :])
    return jnp.moveaxis(shard.reshape(*before, count, -1, *after), dim, 0)


def sent_and_summed(shard, axis, dim):
    count = lax.axis_size(axis)
    pieces = lax.all_to_all(cut_along(shard, dim, count), axis, 0, 0, tiled=True)
    return jnp.sum(pieces, axis=0)


def summed_rows(shard, axes, dim):
    far, near = axes
    pieces = cut_along(shard, dim, lax.axis_size(far))
    nearer = sent_and_summed(pieces, near, dim + 1)
    arrived = lax.all_to_all(nearer, far, split_axis=0, concat_axis=0, tiled=True)
    return arrived.sum(axis=0)


def phase_index(first, second):
    high = first * (second // 256) % 256 * 256
    return (high + first * (second % 256)) % 65536


def dft_table(coords, freqs):
    angle = phase_index(coords, freqs).astype(jnp.float32) * (2.0 * math.pi / IMAGE)
    return (jnp.cos(angle).astype(jnp.bfloat16), (-jnp.sin(angle)).astype(jnp.bfloat16))


def coord_unit(coords):
    return (coords % IMAGE).astype(jnp.float32) / IMAGE - 0.5


def block_table(table_re, table_im):
    upper = jnp.concatenate([table_re, table_im], axis=1)
    lower = jnp.concatenate([-table_im, table_re], axis=1)
    return jnp.concatenate([upper, lower], axis=0)


def local(
    image,
    window_rows,
    window_cols,
    w_terms,
    facet_row_offset,
    facet_col_offset,
    band_offset,
    sub_row_offset,
    sub_column,
):
    facet = image.shape[1]
    column_count = band_offset.shape[0]
    sub_count = sub_row_offset.shape[0]
    frow_index = lax.axis_index("frow")
    fcol_index = lax.axis_index(FCOL)
    freq_base = jnp.arange(SG, dtype=jnp.int32)
    gcol = facet_col_offset[fcol_index] + jnp.arange(image.shape[2], dtype=jnp.int32)
    mcoord = coord_unit(gcol)
    row_base = facet_row_offset[frow_index]
    row_ids = row_base + jnp.arange(facet, dtype=jnp.int32)
    radius = coord_unit(row_ids)[:, None] ** 2 + mcoord[None, :] ** 2
    scale = window_rows[:, None] * window_cols[None, :]
    first = image[0].astype(jnp.float32) * scale
    second = image[1].astype(jnp.float32) * scale
    prepared = []
    for column in range(column_count):
        angle = w_terms[column] * radius
        cosine = jnp.cos(angle)
        sine = jnp.sin(angle)
        prep_re = (first * cosine - second * sine).astype(jnp.bfloat16)
        prep_im = (first * sine + second * cosine).astype(jnp.bfloat16)
        prepared.append(jnp.concatenate([prep_re, prep_im], axis=1))
    band_dev = SG // lax.axis_size(FCOL)
    freqs = jnp.arange(band_dev * lax.axis_size(FCOL), dtype=jnp.int32)
    outputs = []
    for column in range(column_count):
        table_re, table_im = dft_table(gcol[:, None], band_offset[column] + freqs[None, :])
        whole_table = block_table(table_re, table_im)
        product = lax.dot_general(
            whole_table,
            prepared[column],
            (((0,), (1,)), ((), ())),
            preferred_element_type=jnp.float32,
        )
        outputs.append(product.reshape(2, band_dev * lax.axis_size(FCOL), facet).transpose(1, 0, 2))
    summed = summed_rows(jnp.stack(outputs, axis=1), (("fcol_0", "fcol_1"), "fcol_2"), 0)
    banded = (summed / math.sqrt(facet * lax.axis_size(FCOL))).astype(jnp.bfloat16)
    chosen = jnp.take(banded, sub_column, axis=1)
    right_side = chosen.transpose(1, 2, 3, 0).reshape(sub_count, 2 * facet, band_dev)
    table_re, table_im = dft_table(
        row_ids[None, :, None], sub_row_offset[:, None, None] + freq_base[None, None, :]
    )
    left_real = jnp.concatenate([table_re, -table_im], axis=1)
    left_imag = jnp.concatenate([table_im, table_re], axis=1)
    left_side = jnp.stack([left_real, left_imag], axis=2)
    term = jnp.einsum("kxcu,kxv->kcuv", left_side, right_side, preferred_element_type=jnp.float32)
    term = term * (1.0 / math.sqrt(facet * lax.axis_size("frow")))
    return sent_and_summed(term, "frow", 2)


def solution(mesh):
    torus = Mesh(
        mesh.devices.reshape(mesh.shape["frow"], 2, 4, 2), ("frow", "fcol_0", "fcol_1", "fcol_2")
    )
    placed = (P(None, "frow", FCOL), P("frow"), P(FCOL), P(), P(), P(), P(), P(), P())
    return jax.shard_map(
        local, mesh=torus, in_specs=placed, out_specs=P(None, None, "frow", FCOL), check_vma=False
    )
```

profile of v0, /device:TPU:32, one launch (start us, length us, event | category | flops | bytes accessed | tf_op | source)
XLA Modules:
  0.0 116.2 jit_solution(7191070569073293390)
XLA Ops:
  0.0 0.0 copy-start.4
  0.0 0.0 copy-start
  0.0 1.4 %dynamic_slice.7 = s32[1]{0:T(128)} dynamic-slice(s32[16]{0:T(128)} %param.14, s32[]{:T(128)S(6)} %select_n.131), dynamic_slice_sizes={1} | dynamic-slice | bytes 12 | tf_op jit(solution)/shard_map/dynamic_slice | solution.py:70
  1.4 0.6 iota_add_fusion.3
  2.0 1.3 %fusion.92 = (s32[1]{0:T(128)}, s32[1]{0:T(128)}) fusion(s32[2]{0:T(128)} %param.15), kind=kLoop, calls=%fused_computation.163 | loop fusion | bytes 16 | tf_op jit(solution)/shard_map/slice | solution.py:90
  3.4 0.7 add_select_fusion.10
  4.0 0.6 add_select_fusion.6
  4.7 9.7 %negate_convert_fusion.2 = (bf16[512,512]{1,0:T(8,128)(2,1)S(1)}, bf16[512,512]{1,0:T(8,128)(2,1)S(1)}, bf16[512,512]{1,0:T(8,128)(2,1)S(1)}, bf16[512,512]{1,0:T(8,128)(2,1)S(1)}) fusion(s32[512]{0:T(512)S(1)} %get-tuple-element.27, s32[512]{0:T(512)S(1)} %get-tuple-element.28, s32[512]{0:T(512)S(1)} %iota_add_fusion.3, s32[512]{0:T(512)S(1)} %get-tuple-element.29, ...), kind=kLoop, calls=%fused_computation.102 | loop fusion | flops 16252928 | bytes 2107392 | tf_op jit(solution)/shard_map/convert_element_type | solution.py:40
  14.4 10.2 %fusion.69 = (bf16[512,512]{1,0:T(8,128)(2,1)}, bf16[512,512]{1,0:T(8,128)(2,1)}) fusion(s32[512]{0:T(512)S(1)} %get-tuple-element.27, s32[512]{0:T(512)S(1)} %get-tuple-element.28, s32[512]{0:T(512)S(1)} %iota_add_fusion.3, s32[512]{0:T(512)S(1)} %get-tuple-element.29, s32[512]{0:T(512)S(1)} %get-tuple-element.30), kind=kLoop, calls=%fused_computation.108 | loop fusion | flops 17301504 | bytes 1058816 | tf_op jit(solution)/shard_map/neg | solution.py:49
  24.6 0.0 copy-done.7
  24.6 0.6 dynamic_slice.6
  25.2 1.3 %fusion.76 = (f32[512]{0:T(512)S(1)}, f32[512]{0:T(512)S(1)}) fusion(s32[]{:T(128)} %bitcast, s32[]{:T(128)} %bitcast.4), kind=kLoop, calls=%fused_computation.139 | loop fusion | flops 16384 | bytes 4104 | tf_op jit(solution)/shard_map/integer_pow | solution.py:74
  26.5 0.0 copy-done.3
  26.5 0.6 fusion.91
  27.1 0.0 copy-done.5
  27.1 0.0 copy-done.4
  27.1 0.0 copy-done
  27.1 9.8 %fusion.42 = (bf16[512,512]{1,0:T(8,128)(2,1)S(1)}, bf16[512,512]{1,0:T(8,128)(2,1)S(1)}, bf16[512,512]{1,0:T(8,128)(2,1)S(1)}, bf16[512,512]{1,0:T(8,128)(2,1)S(1)}) fusion(f32[512]{0:T(512)S(1)} %get-tuple-element.32, f32[512]{0:T(512)S(1)} %get-tuple-element.31, f32[]{:T(128)} %bitcast.7, f32[512]{0:T(512)S(1)} %copy-done.4, f32[512]{0:T(512)S(1)} %copy-done.5, ...), kind=kLoop, calls=%fused_computation.74 | loop fusion | flops 6291456 | bytes 3153928 | tf_op jit(solution)/shard_map/convert_element_type | solution.py:83
  36.8 0.0 copy-done.2
  36.8 1.3 %fusion.10 = f32[1024,512]{1,0:T(8,128)S(1)} fusion(bf16[512,512]{1,0:T(8,128)(2,1)S(1)} %get-tuple-element.14, bf16[512,512]{1,0:T(8,128)(2,1)S(1)} %copy-done.2, bf16[512,512]{1,0:T(8,128)(2,1)S(1)} %get-tuple-element.13, bf16[512,512]{1,0:T(8,128)(2,1)S(1)} %get-tuple-element.8, bf16[512,512]{1,0:T(8,128)(2,1)S(1)} %get-tuple-element.5), kind=kOutput, calls=%fused_computation.20 | convolution fusion | flops 1084227584 | bytes 4718592 | tf_op jit(solution)/shard_map/dot_general | solution.py:92
  38.2 1.3 %fusion.18 = f32[1024,512]{1,0:T(8,128)S(1)} fusion(bf16[512,512]{1,0:T(8,128)(2,1)S(1)} %get-tuple-element.17, bf16[512,512]{1,0:T(8,128)(2,1)S(1)} %copy-done.1, bf16[512,512]{1,0:T(8,128)(2,1)S(1)} %get-tuple-element.18, bf16[512,512]{1,0:T(8,128)(2,1)S(1)} %get-tuple-element.6, bf16[512,512]{1,0:T(8,128)(2,1)S(1)} %get-tuple-element.7), kind=kOutput, calls=%fused_computation.28 | convolution fusion | flops 1084227584 | bytes 4718592 | tf_op jit(solution)/shard_map/dot_general | solution.py:92
  39.5 0.8 maximum_bitcast_fusion
  40.3 0.8 copy.31
  41.1 8.2 %all_to_all.15 = f32[2,8,32,2,2,512]{5,2,1,4,3,0:T(8,128)} all-to-all(f32[2,8,32,2,2,512]{5,2,1,4,3,0:T(8,128)S(1)} %copy.31), channel_id=1, replica_groups=mesh['frow'=16,'fcol_0'=2,'fcol_1'=4,'fcol_2'=2] {'fcol_2'}, dimensions={0} | all-to-all | bytes 8388608 | tf_op jit(solution)/shard_map/all_to_all | solution.py:21
  49.2 2.9 %reduce_sum.27 = f32[8,32,2,2,512]{4,1,0,3,2:T(8,128)S(1)} reduce(f32[2,8,32,2,2,512]{5,2,1,4,3,0:T(8,128)} %all_to_all.15, f32[]{:T(128)} %constant.163.clone.1), dimensions={0}, to_apply=%region_0.1 | reduce | flops 524288 | bytes 6291460 | tf_op jit(solution)/shard_map/reduce_sum | solution.py:22
  52.1 1.5 %copy.33 = f32[8,32,2,2,512]{4,1,3,2,0:T(8,128)} copy(f32[8,32,2,2,512]{4,1,0,3,2:T(8,128)S(1)} %reduce_sum.27) | data formatting | bytes 4194304 | tf_op jit(solution)/shard_map/reduce_sum | solution.py:22
  53.7 5.9 %all-to-all-start.1 = ((f32[8,32,2,2,512]{4,1,3,2,0:T(8,128)}), f32[8,32,2,2,512]{4,1,3,2,0:T(8,128)S(1)}, u32[]{:S(2)}, u32[]{:S(2)}) async-start(f32[8,32,2,2,512]{4,1,3,2,0:T(8,128)} %copy.33), calls=%async_computation.1 | async-start | bytes 4194304 | tf_op jit(solution)/shard_map/all_to_all | solution.py:29
  59.6 0.6 iota_add_fusion.4
  60.3 0.1 and_select_fusion.1
  60.4 9.5 %fusion.68 = bf16[2,512,512]{2,1,0:T(8,128)(2,1)S(1)} fusion(s32[2,512]{1,0:T(2,128)S(1)} %get-tuple-element.26, s32[2,512]{1,0:T(2,128)S(1)} %get-tuple-element.25, s32[512]{0:T(512)S(1)} %iota_add_fusion.4), kind=kLoop, calls=%fused_computation.107 | loop fusion | flops 17301504 | bytes 1058816 | tf_op jit(solution)/shard_map/neg | solution.py:106
  69.9 10.1 %negate_convert_fusion = (bf16[2,512,512]{2,1,0:T(8,128)(2,1)S(1)}, bf16[2,512,512]{2,1,0:T(8,128)(2,1)S(1)}) fusion(s32[2,512]{1,0:T(2,128)S(1)} %get-tuple-element.26, s32[2,512]{1,0:T(2,128)S(1)} %get-tuple-element.25, s32[512]{0:T(512)S(1)} %iota_add_fusion.4), kind=kLoop, calls=%fused_computation.38 | loop fusion | flops 16252928 | bytes 2107392 | tf_op jit(solution)/shard_map/convert_element_type | solution.py:40
  80.0 2.4 %maximum_bitcast_fusion.1 = (bf16[2,1024,1,512]{3,1,2,0:T(8,128)(2,1)}, bf16[2,1024,1,512]{3,1,2,0:T(8,128)(2,1)}) fusion(bf16[2,512,512]{2,1,0:T(8,128)(2,1)S(1)} %fusion.68, bf16[2,512,512]{2,1,0:T(8,128)(2,1)S(1)} %get-tuple-element.12, bf16[2,512,512]{2,1,0:T(8,128)(2,1)S(1)} %get-tuple-element.11), kind=kLoop, calls=%fused_computation.36 | loop fusion | flops 8388608 | bytes 7340032 | tf_op jit(solution)/shard_map/stack | solution.py:108
  82.4 3.0 %all-to-all-done.1 = f32[8,32,2,2,512]{4,1,3,2,0:T(8,128)S(1)} async-done(((f32[8,32,2,2,512]{4,1,3,2,0:T(8,128)}), f32[8,32,2,2,512]{4,1,3,2,0:T(8,128)S(1)}, u32[]{:S(2)}, u32[]{:S(2)}) %all-to-all-start.1) | async-done | bytes 2097184 | tf_op jit(solution)/shard_map/all_to_all | solution.py:29
  85.3 0.2 reduce_sum.28
  85.6 0.6 gather_fusion
  86.2 0.1 select_bitcast_fusion
  86.2 0.1 copy.35
  86.4 0.1 reshape.286
  86.5 3.0 %fusion.38 = f32[2,2,512,32]{2,3,1,0:T(8,128)S(1)} fusion(bf16[2,1024,1,512]{3,1,2,0:T(8,128)(2,1)} %get-tuple-element.10, bf16[2,1024,1,512]{3,1,2,0:T(8,128)(2,1)} %get-tuple-element.9, bf16[2,1024,32,1]{1,2,0,3:T(8,128)(2,1)S(1)} %reshape.286), kind=kOutput, calls=%fused_computation.72 | convolution fusion | flops 142671872 | bytes 4587520 | tf_op jit(solution)/shard_map/kxcu,kxv->kcuv/dot_general | solution.py:109
  89.5 0.3 reshape.274
  89.8 0.3 copy.46
  90.1 0.5 reshape.288
  90.6 22.6 %all_to_all.16 = f32[16,1,4096]{2,1,0:T(1,128)S(1)} all-to-all(f32[16,1,4096]{2,1,0:T(1,128)S(1)} %reshape.288), channel_id=1, replica_groups=mesh['frow'=16,'fcol_0'=2,'fcol_1'=4,'fcol_2'=2] {'frow'}, dimensions={0} | all-to-all | bytes 524288 | tf_op jit(solution)/shard_map/all_to_all | solution.py:21
  113.2 0.5 broadcast.455
  113.7 1.3 %reduce = f32[16,4096]{1,0:T(8,128)S(1)} reduce(f32[16,1,4096]{2,1,0:T(1,128)S(1)} %all_to_all.16, f32[]{:T(128)} %broadcast.455), dimensions={1}, to_apply=%all_to_all.11.reduce_sub_computation | reduce | bytes 524292 | tf_op jit(solution)/shard_map/all_to_all | solution.py:21
  115.0 0.3 reshape.289
  115.4 0.1 bitcast_reduce_fusion
  115.5 0.7 copy.38
  (14 shorter events, 0.1 us)
Async XLA Ops:
  0.0 24.6 %copy-start.7 = (s32[16]{0:T(128)S(1)}, s32[16]{0:T(128)}, u32[]{:S(2)}) copy-start(s32[16]{0:T(128)} %param.13) | copy-start | bytes 196
  0.0 26.5 %copy-start.3 = (f32[2]{0:T(128)S(1)}, f32[2]{0:T(128)}, u32[]{:S(2)}) copy-start(f32[2]{0:T(128)} %param.12) | copy-start | bytes 28
  0.0 27.1 %copy-start.5 = (f32[512]{0:T(512)S(1)}, f32[512]{0:T(512)}, u32[]{:S(2)}) copy-start(f32[512]{0:T(512)} %param.10) | copy-start | bytes 6148
  0.0 27.1 %copy-start.4 = (f32[512]{0:T(512)S(1)}, f32[512]{0:T(512)}, u32[]{:S(2)}) copy-start(f32[512]{0:T(512)} %param.11) | copy-start | bytes 6148
  0.0 27.0 %copy-start = (bf16[2,512,512]{2,1,0:T(8,128)(2,1)S(1)}, bf16[2,512,512]{2,1,0:T(8,128)(2,1)}, u32[]{:S(2)}) copy-start(bf16[2,512,512]{2,1,0:T(8,128)(2,1)} %param.9) | copy-start | bytes 3145732
  24.6 12.2 %copy-start.2 = (bf16[512,512]{1,0:T(8,128)(2,1)S(1)}, bf16[512,512]{1,0:T(8,128)(2,1)}, u32[]{:S(2)}) copy-start(bf16[512,512]{1,0:T(8,128)(2,1)} %get-tuple-element.19) | copy-start | bytes 1572868
  36.8 1.3 %copy-start.1 = (bf16[512,512]{1,0:T(8,128)(2,1)S(1)}, bf16[512,512]{1,0:T(8,128)(2,1)}, u32[]{:S(2)}) copy-start(bf16[512,512]{1,0:T(8,128)(2,1)} %get-tuple-element.20) | copy-start | bytes 1572868
  53.7 6.6 %copy-start.8 = (s32[2]{0:T(128)S(1)}, s32[2]{0:T(128)}, u32[]{:S(2)}) copy-start(s32[2]{0:T(128)} %param.17) | copy-start | bytes 28
  53.7 6.6 %copy-start.6 = (s32[2]{0:T(128)S(1)}, s32[2]{0:T(128)}, u32[]{:S(2)}) copy-start(s32[2]{0:T(128)} %param.16) | copy-start | bytes 28
  53.7 31.7 %all-to-all-start.1 = ((f32[8,32,2,2,512]{4,1,3,2,0:T(8,128)}), f32[8,32,2,2,512]{4,1,3,2,0:T(8,128)S(1)}, u32[]{:S(2)}, u32[]{:S(2)}) async-start(f32[8,32,2,2,512]{4,1,3,2,0:T(8,128)} %copy.33), calls=%async_computation.1 | async-start | bytes 4194304 | tf_op jit(solution)/shard_map/all_to_all | solution.py:29
where the time goes:
time: 117 us; the launch traced here: 116 us
  other arithmetic  61 us (52%)
  blocking collectives  30.8 us (26%)
  local copies, waits for them, and re-layouts  9.63 us (8%)
  starting transfers between devices  5.89 us (5%)
  matrix products  5.61 us (5%)
  waiting for transfers between devices  2.99 us (3%)
    all_to_all x2, blocking collectives, sent_and_summed(): lax.all_to_all(cut_along(shard, dim, count), axis, 0, 0, tiled=True)  30.8 us
    convert_element_type x2, other arithmetic, dft_table(): (-jnp.sin(angle)).astype(jnp.bfloat16)  19.8 us
    neg x1, other arithmetic, block_table(): lower = jnp.concatenate([-table_im, table_re], axis=1)  10.2 us
    convert_element_type x1, other arithmetic, local(): prep_re = (first * cosine - second * sine).astype(jnp.bfloat16)  9.75 us
    neg x1, other arithmetic, local(): left_real = jnp.concatenate([table_re, -table_im], axis=1)  9.51 us
    all_to_all x1, starting transfers between devices, summed_rows(): lax.all_to_all(nearer, far, split_axis=0, concat_axis=0, tiled=True)  5.89 us
    dot_general x1, matrix products, local(): jnp.einsum('kxcu,kxv->kcuv', left_side, right_side, preferred_element_typ...  3.02 us
    all_to_all x1, waiting for transfers between devices, summed_rows(): lax.all_to_all(nearer, far, split_axis=0, concat_axis=0, tiled=True)  2.99 us
  transfers between devices with their start and end apart: 1, of which 1 were waited for; matrix products, arithmetic and copies ran while one was open for 20% of the time, Pallas kernels for 0%

commit v1 on v0

v1 whole, which is shorter than its diff:
```python
import functools
import math

import jax
import jax.numpy as jnp
from jax import lax
from jax.experimental import pallas as pl
from jax.experimental.pallas import tpu as pltpu
from jax.sharding import Mesh
from jax.sharding import PartitionSpec as P

IMAGE = 65536
F = 512
f32 = jnp.float32
bf16 = jnp.bfloat16
FROW = ("zh", "y")
FCOL = ("zl", "x", "c")
Z = ("zh", "zl")
PIO2 = (1.5703125, 4.837512969970703125e-4, 7.549789948768648e-8)
NT = (((1,), (1,)), ((), ()))
NN = (((1,), (0,)), ((), ()))


def sincos_of(r, q):
    z = r * r
    s = r + r * z * (-1.6666654611e-1 + z * (8.3321608736e-3 - 1.9515295891e-4 * z))
    c = 1.0 - 0.5 * z + z * z * (4.166664568298827e-2 + z * (-1.388731625493765e-3 + 2.443315711809948e-5 * z))
    odd = (q & 1) == 1
    cosine = jnp.where(odd, s, c)
    sine = jnp.where(odd, c, s)
    cosine = jnp.where(((q + 1) & 2) == 2, -cosine, cosine)
    sine = jnp.where((q & 2) == 2, -sine, sine)
    return cosine, sine


def turn(p):
    q = (p + 8192) >> 14
    r = (p - (q << 14)).astype(f32) * (2.0 * math.pi / IMAGE)
    c, s = sincos_of(r, q)
    return c, -s


def phase_index(first, second):
    high = ((first * (second >> 8)) & 255) << 8
    return (high + first * (second & 255)) & (IMAGE - 1)


def chirp(w, g):
    unit = (g & (IMAGE - 1)).astype(f32) * (1.0 / IMAGE) - 0.5
    angle = w * (unit * unit)
    n = jnp.floor(angle * (2.0 / math.pi) + 0.5)
    r = ((angle - n * PIO2[0]) - n * PIO2[1]) - n * PIO2[2]
    return sincos_of(r, n.astype(jnp.int32))


def times(a, b):
    return a[0] * b[0] - a[1] * b[1], a[0] * b[1] + a[1] * b[0]


def ids():
    return {name: lax.axis_index(name) for name in ("zh", "y", "zl", "x", "c")}


def outer(a, b):
    n = a[0].shape[1]
    big = [v[:, None, :] for v in a]
    small = [v[None, :, :] for v in b]
    return [v.reshape(-1, n) for v in times(big, small)]


def column_factors(at, w, band, offset, window):
    g = offset + lax.broadcasted_iota(jnp.int32, (1, F), 1)
    i = lax.broadcasted_iota(jnp.int32, (16, F), 0)
    zl = (at["zl"] + (i >> 3)) & 1
    x = (at["x"] + (i >> 1)) & 3
    c = (at["c"] + i) & 1
    coarse = turn(phase_index(g, band + ((zl * 4 + x) * 2 + c) * 32))
    wave = chirp(w, g)
    coarse = times(coarse, (wave[0] * window, wave[1] * window))
    fine = turn((g * lax.broadcasted_iota(jnp.int32, (32, F), 0)) & (IMAGE - 1))
    return coarse, fine


def column_table(factors, t):
    coarse, fine = factors
    re, im = outer([v[2 * t : 2 * t + 2] for v in coarse], fine)
    first = jnp.concatenate([re, im], axis=0).astype(bf16)
    second = jnp.concatenate([-im, re], axis=0).astype(bf16)
    return first, second


def scalars(at, w_terms, band_offset, sub_column):
    column = sub_column[at["c"]]
    return w_terms[column], band_offset[column]


def own_kernel(w_terms, fro, fco, bo, sro, sc, image, wrow, wcol, rt, g_out, w1, w2):
    at = ids()
    w, band = scalars(at, w_terms, bo, sc)
    me = (at["zl"] * 4 + at["x"]) * 2 + at["c"]
    factors = column_factors(at, w, band, fco[me], wcol[...])
    for t in range(8):
        rows = pl.ds(t * 128, 128)
        w1[rows, :], w2[rows, :] = column_table(factors, t)
    for n in range(4):
        rows = pl.ds(n * 256, 256)
        g_out[:, rows] = lax.dot_general(image[0], w1[rows, :], NT, preferred_element_type=f32) + lax.dot_general(
            image[1], w2[rows, :], NT, preferred_element_type=f32
        )
    g = fro[at["zh"] * 4 + at["y"]] + lax.broadcasted_iota(jnp.int32, (1, F), 1)
    i = lax.broadcasted_iota(jnp.int32, (16, F), 0)
    wave = chirp(w, g)
    window = wrow[...] * (1.0 / 8192.0)
    wave = (wave[0] * window, wave[1] * window)
    first = sro[at["c"]]
    fine = turn((g * lax.broadcasted_iota(jnp.int32, (32, F), 0)) & (IMAGE - 1))

    def coarse_rows(base):
        block = ((base + i) & 3) * 4 + ((at["y"] + (i >> 2)) & 3)
        return times(turn(phase_index(g, first + block * 32)), wave)

    plain = coarse_rows(at["zh"])
    moved = coarse_rows(at["zh"] + at["zl"])
    for part in range(4):
        re, im = outer(moved if part == 3 else plain, [v[part * 8 : part * 8 + 8] for v in fine])
        rt[pl.ds(part * 128, 128), pl.ds(0, F)] = re.astype(bf16)
        rt[pl.ds(part * 128, 128), pl.ds(F, F)] = im.astype(bf16)


def other_kernel(w_terms, fco, bo, sc, wcol, w1, w2):
    at = ids()
    w, band = scalars(at, w_terms, bo, sc)
    me = (at["zl"] * 4 + at["x"]) * 2 + (1 - at["c"])
    factors = column_factors(at, w, band, fco[me], wcol[...])
    for t in range(8):
        rows = pl.ds(t * 128, 128)
        w1[rows, :], w2[rows, :] = column_table(factors, t)


def sum_kernel(rt, g_own, w1, w2, image, *rest):
    xo, yo, z1, z2 = rest[0:4], rest[4:8], rest[8:10], rest[10:12]
    gg, im = rest[12:]
    im[0] = image[0].astype(bf16)
    im[1] = image[1].astype(bf16)
    sign = jnp.where(lax.broadcasted_iota(jnp.int32, (1, 128), 1) < 64, -1.0, 1.0)
    for n in range(4):
        rows = pl.ds(n * 256, 256)
        g = g_own[:, rows] + lax.dot_general(im[0], w1[rows, :], NT, preferred_element_type=f32)
        g = g + lax.dot_general(im[1], w2[rows, :], NT, preferred_element_type=f32)
        gg[pl.ds(0, F), rows] = g.astype(bf16)
        for h in range(2):
            half = pltpu.roll(g[:, h * 128 : h * 128 + 128], 64, 1) * sign
            gg[pl.ds(F, F), pl.ds(n * 256 + h * 128, 128)] = half.astype(bf16)
    for n in range(4):
        s = lax.dot_general(rt[...], gg[:, pl.ds(n * 256, 256)], NN, preferred_element_type=f32)
        for h in range(2):
            t = 2 * n + h
            zl, x = t // 4, t % 4
            piece = s[:, h * 128 : h * 128 + 128]
            xo[x][:, pl.ds(zl * 128, 128)] = piece[0:128]
            for y in range(4):
                yo[y][:, pl.ds(t * 128, 128)] = piece[128 + y * 32 : 160 + y * 32]
            z1[zl][:, pl.ds(x * 128, 128)] = piece[256:384]
            z2[zl][:, pl.ds(x * 128, 128)] = piece[384:512]


def shift(value, axis, step):
    n = lax.axis_size(axis)
    return lax.ppermute(value, axis, [(i, (i + step) % n) for i in range(n)])


def sent_round(pieces, axis):
    total = pieces[0]
    for step, piece in enumerate(pieces[1:], 1):
        total = total + shift(piece, axis, step)
    return total


def rows_of(value, count):
    size = value.shape[0] // count
    return [value[i * size : (i + 1) * size] for i in range(count)]


def cols_of(value, count):
    size = value.shape[1] // count
    return [value[:, i * size : (i + 1) * size] for i in range(count)]


def local(image, wrow, wcol, w_terms, fro, fco, bo, sro, sc):
    smem = pl.BlockSpec(memory_space=pltpu.SMEM)
    vmem = pl.BlockSpec(memory_space=pltpu.VMEM)
    params = pltpu.CompilerParams(vmem_limit_bytes=24 * 2**20)
    swap = [(0, 1), (1, 0)]
    window = wcol.reshape(1, F)
    other_window = lax.ppermute(window, "c", swap)
    other_image = lax.ppermute(image.astype(f32), "c", swap)
    table = jax.ShapeDtypeStruct((2 * F, F), bf16)
    rt, g_own = pl.pallas_call(
        own_kernel,
        out_shape=(jax.ShapeDtypeStruct((F, 2 * F), bf16), jax.ShapeDtypeStruct((F, 2 * F), f32)),
        in_specs=[smem] * 6 + [vmem] * 3,
        out_specs=(vmem, vmem),
        scratch_shapes=[pltpu.VMEM((2 * F, F), bf16)] * 2,
        compiler_params=params,
        cost_estimate=pl.CostEstimate(flops=2**30, bytes_accessed=4 * 2**20, transcendentals=0),
        name="own_facet",
    )(w_terms, fro, fco, bo, sro, sc, image, wrow.reshape(1, F), window)
    w1, w2 = pl.pallas_call(
        other_kernel,
        out_shape=(table, table),
        in_specs=[smem] * 4 + [vmem],
        out_specs=(vmem, vmem),
        compiler_params=params,
        cost_estimate=pl.CostEstimate(flops=2**22, bytes_accessed=2 * 2**20, transcendentals=0),
        name="other_table",
    )(w_terms, fco, bo, sc, other_window)
    shapes = [(128, 256)] * 4 + [(32, 1024)] * 4 + [(128, 512)] * 4
    pieces = pl.pallas_call(
        sum_kernel,
        out_shape=[jax.ShapeDtypeStruct(s, f32) for s in shapes],
        in_specs=[vmem] * 5,
        out_specs=[vmem] * 12,
        scratch_shapes=[pltpu.VMEM((2 * F, 2 * F), bf16), pltpu.VMEM((2, F, F), bf16)],
        compiler_params=params,
        cost_estimate=pl.CostEstimate(flops=2**31, bytes_accessed=9 * 2**20, transcendentals=0),
        name="two_stages",
    )(rt, g_own, w1, w2, other_image)
    xs, ys, z1, z2 = pieces[0:4], pieces[4:8], pieces[8:10], pieces[10:12]
    nearby = [(z, (z + 1 if z % 2 else z - 1) % 8) for z in range(8)]
    part_z1 = sent_round(z1, "zl")
    part_z2 = z2[0] + lax.ppermute(z2[1], Z, nearby)
    part_x = sent_round(xs, "x")
    part_y = sent_round(ys, "y")
    part_z1 = sent_round(cols_of(part_z1, 4), "x")
    part_z2 = sent_round(rows_of(part_z2, 4), "y")
    part_x = sent_round(cols_of(part_x, 2), "zl")
    part_y = sent_round(cols_of(part_y, 2), "zl")
    part_x = sent_round(rows_of(part_x, 4), "y")
    part_z1 = sent_round(rows_of(part_z1, 4), "y")
    part_y = sent_round(cols_of(part_y, 4), "x")
    part_z2 = sent_round(cols_of(part_z2, 4), "x")
    part_z2 = jnp.where(lax.axis_index("zl") == 1, jnp.roll(part_z2, 8, axis=0), part_z2)
    whole = jnp.stack([v.reshape(4, 8, 2, 2, 32) for v in (part_x, part_y, part_z1, part_z2)], axis=1)
    whole = whole.reshape(4, 32, 2, 2, 32)
    core = "c"

    def routed(value, step, cross):
        if not (step or cross):
            return value
        perm = [(z * 2 + c, (z + step) % 4 * 2 + (c ^ cross)) for z in range(4) for c in range(2)]
        return lax.ppermute(value, ("zh", core), perm)

    sums = [sum(routed(whole[r, :, :, cross], r, cross) for r in range(4)) for cross in (0, 1)]
    mine, theirs = [v.transpose(1, 0, 2) for v in sums]
    first = lax.axis_index(core) == 0
    return jnp.stack([jnp.where(first, mine, theirs), jnp.where(first, theirs, mine)])


def solution(mesh):
    torus = Mesh(mesh.devices.reshape(4, 4, 2, 4, 2), ("zh", "y", "zl", "x", "c"))
    placed = (P(None, FROW, FCOL), P(FROW), P(FCOL), P(), P(), P(), P(), P(), P())
    return jax.shard_map(local, mesh=torus, in_specs=placed, out_specs=P(None, None, FROW, FCOL), check_vma=False)
```

time: 117 us -> 87.9 us (0.75)
  other arithmetic: 61 us -> 2.63 us
  starting transfers between devices: 5.89 us -> 59.1 us
  blocking collectives: 30.8 us -> 0 us
  waiting for transfers between devices: 2.99 us -> 18 us
  local copies, waits for them, and re-layouts: 9.63 us -> 0.58 us
  Pallas kernels: 0 us -> 6.3 us
  matrix products: 5.61 us -> 0 us
    ppermute x0 -> x37, starting transfers between devices: none -> 59.1 us  [the longest x27 41 us: shift(): return lax.ppermute(value, axis, [(i, (i + step) % n) for i in range(n)])]
    all_to_all x2 -> x0, blocking collectives: 30.8 us -> none  [sent_and_summed(): lax.all_to_all(cut_along(shard, dim, count), axis, 0, 0, tiled=True)]
    convert_element_type x4 -> x1, other arithmetic: 29.6 us -> 1.58 us  [local(): other_image = lax.ppermute(image.astype(f32), 'c', swap)]
    neg x2 -> x0, other arithmetic: 19.7 us -> none  [the longest x1 10.2 us: block_table(): lower = jnp.concatenate([-table_im, table_re], axis=1)]
    ppermute x0 -> x37, waiting for transfers between devices: none -> 18 us  [the longest x27 11.2 us: shift(): return lax.ppermute(value, axis, [(i, (i + step) % n) for i in range(n)])]
    pallas_call x0 -> x3, Pallas kernels: none -> 6.3 us  [the longest x1 2.82 us: local(): pl.pallas_call(own_kernel, out_shape=(jax.ShapeDtypeStruct((F, 2 * F), bf...]
    all_to_all x1 -> x0, starting transfers between devices: 5.89 us -> none  [summed_rows(): lax.all_to_all(nearer, far, split_axis=0, concat_axis=0, tiled=True)]
    dot_general x3 -> x0, matrix products: 5.61 us -> none  [the longest x1 3.02 us: local(): jnp.einsum('kxcu,kxv->kcuv', left_side, right_side, preferred_element_typ...]
  transfers between devices with their start and end apart: 1 -> 37, of which waited for: 1 -> 12; matrix products, arithmetic and copies ran while one was open for 20% -> 1% of each run, Pallas kernels for 0% -> 4%
where the time goes in v1:
time: 87.9 us; the launch traced here: 87 us
  starting transfers between devices  59.1 us (67%)
  waiting for transfers between devices  18 us (20%)
  Pallas kernels  6.3 us (7%)
  other arithmetic  2.63 us (3%)
    ppermute x27, starting transfers between devices, shift(): return lax.ppermute(value, axis, [(i, (i + step) % n) for i in range(n)])  41 us
    ppermute x7, starting transfers between devices, routed(): return lax.ppermute(value, ('zh', core), perm)  13.8 us
    ppermute x27, waiting for transfers between devices, shift(): return lax.ppermute(value, axis, [(i, (i + step) % n) for i in range(n)])  11.2 us
    ppermute x7, waiting for transfers between devices, routed(): return lax.ppermute(value, ('zh', core), perm)  6.01 us
    ppermute x1, starting transfers between devices, local(): part_z2 = z2[0] + lax.ppermute(z2[1], Z, nearby)  3.72 us
    pallas_call x1, Pallas kernels, local(): pl.pallas_call(own_kernel, out_shape=(jax.ShapeDtypeStruct((F, 2 * F), bf...  2.82 us
    pallas_call x1, Pallas kernels, local(): pl.pallas_call(sum_kernel, out_shape=[jax.ShapeDtypeStruct(s, f32) for s...  2.39 us
  transfers between devices with their start and end apart: 37, of which 12 were waited for; matrix products, arithmetic and copies ran while one was open for 1% of the time, Pallas kernels for 4%

profile of v1, /device:TPU:32, one launch (start us, length us, event | category | flops | bytes accessed | tf_op | source)
XLA Modules:
  0.0 87.0 jit_solution(5379791854800949370)
XLA Ops:
  0.1 1.6 %convert_element_type.3 = f32[2,512,512]{2,1,0:T(8,128)S(1)} convert(bf16[2,512,512]{2,1,0:T(8,128)(2,1)} %image.1) | non-fusion elementwise | flops 524288 | bytes 3145728 | tf_op jit(solution)/shard_map/convert_element_type | solution.py:196
  1.8 0.5 collective-permute-start
  2.3 2.8 %own_facet.1 = (bf16[512,1024]{1,0:T(8,128)(2,1)S(1)}, f32[512,1024]{1,0:T(8,128)S(1)}) custom-call(f32[2]{0:T(128)S(1)} %copy-done.5, s32[16]{0:T(128)S(1)} %copy-done.3, s32[16]{0:T(128)S(1)} %copy-done.6, s32[2]{0:T(128)S(1)} %copy-done.7, s32[2]{0:T(128)S(1)} %copy-done.4, s32[2]{0:T(128)S(1)} %copy-done.8, bf16[2,512,512]{2,1,0:T(8,128)(2,1)S(1)} %copy-done, ...), custom_call_target="tpu_custom_call" | custom-call | flops 1073741824 | bytes 4194304 | tf_op jit(solution)/shard_map/own_facet/pallas_call | solution.py:198
  5.1 0.8 collective-permute-done.wcol
  5.9 1.1 %other_table.1 = (bf16[1024,512]{1,0:T(8,128)(2,1)S(1)}, bf16[1024,512]{1,0:T(8,128)(2,1)S(1)}) custom-call(f32[2]{0:T(128)S(1)} %copy-done.5, s32[16]{0:T(128)S(1)} %copy-done.6, s32[2]{0:T(128)S(1)} %copy-done.7, s32[2]{0:T(128)S(1)} %copy-done.8, f32[1,512]{1,0:T(1,128)S(1)} %collective-permute-done.wcol), custom_call_target="tpu_custom_call" | custom-call | flops 4194304 | bytes 2097152 | tf_op jit(solution)/shard_map/other_table/pallas_call | solution.py:208
  7.0 2.4 %two_stages.1 = (f32[128,256]{1,0:T(8,128)S(1)}, f32[128,256]{1,0:T(8,128)S(1)}, f32[128,256]{1,0:T(8,128)S(1)}, f32[128,256]{1,0:T(8,128)S(1)}, f32[32,1024]{1,...) custom-call(bf16[512,1024]{1,0:T(8,128)(2,1)S(1)} %get-tuple-element, ...), custom_call_target="tpu_custom_call" | custom-call | flops 2147483648 | bytes 9437184 | tf_op jit(solution)/shard_map/two_stages/pallas_call | solution.py:218
  9.4 1.6 %collective-permute-start.2 = (f32[128,256]{1,0:T(8,128)S(1)}, f32[128,256]{1,0:T(8,128)S(1)}, u32[]{:S(2)}, u32[]{:S(2)}) collective-permute-start(f32[128,256]{1,0:T(8,128)S(1)} %get-tuple-element.26), channel_id=1, source_target_pairs={{0,2},{2,4},{4,6},{6,0},{1,3},{3,5},{5,7},{7,1},{8,10},{10,12},{12... | collective-permute-start | bytes 393224 | tf_op jit(solution)/shard_map/ppermute | solution.py:169
  11.0 2.7 %collective-permute-start.3 = (f32[128,256]{1,0:T(8,128)S(1)}, f32[128,256]{1,0:T(8,128)S(1)}, u32[]{:S(2)}, u32[]{:S(2)}) collective-permute-start(f32[128,256]{1,0:T(8,128)S(1)} %get-tuple-element.27), channel_id=1, source_target_pairs={{0,4},{2,6},{4,0},{6,2},{1,5},{3,7},{5,1},{7,3},{8,12},{10,14},{12... | collective-permute-start | bytes 393224 | tf_op jit(solution)/shard_map/ppermute | solution.py:169
  13.7 1.4 %collective-permute-start.4 = (f32[128,256]{1,0:T(8,128)S(1)}, f32[128,256]{1,0:T(8,128)S(1)}, u32[]{:S(2)}, u32[]{:S(2)}) collective-permute-start(f32[128,256]{1,0:T(8,128)S(1)} %get-tuple-element.28), channel_id=1, source_target_pairs={{0,6},{2,0},{4,2},{6,4},{1,7},{3,1},{5,3},{7,5},{8,14},{10,8},{12,... | collective-permute-start | bytes 393224 | tf_op jit(solution)/shard_map/ppermute | solution.py:169
  15.2 1.6 %collective-permute-start.9 = (f32[32,1024]{1,0:T(8,128)S(1)}, f32[32,1024]{1,0:T(8,128)S(1)}, u32[]{:S(2)}, u32[]{:S(2)}) collective-permute-start(f32[32,1024]{1,0:T(8,128)S(1)} %get-tuple-element.30), channel_id=1, source_target_pairs={{0,16},{16,32},{32,48},{48,0},{1,17},{17,33},{33,49},{49,1},{2,18}... | collective-permute-start | bytes 393224 | tf_op jit(solution)/shard_map/ppermute | solution.py:169
  16.7 2.9 %collective-permute-start.10 = (f32[32,1024]{1,0:T(8,128)S(1)}, f32[32,1024]{1,0:T(8,128)S(1)}, u32[]{:S(2)}, u32[]{:S(2)}) collective-permute-start(f32[32,1024]{1,0:T(8,128)S(1)} %get-tuple-element.31), channel_id=1, source_target_pairs={{0,32},{16,48},{32,0},{48,16},{1,33},{17,49},{33,1},{49,17},{2,34}... | collective-permute-start | bytes 393224 | tf_op jit(solution)/shard_map/ppermute | solution.py:169
  19.6 1.3 %collective-permute-start.11 = (f32[32,1024]{1,0:T(8,128)S(1)}, f32[32,1024]{1,0:T(8,128)S(1)}, u32[]{:S(2)}, u32[]{:S(2)}) collective-permute-start(f32[32,1024]{1,0:T(8,128)S(1)} %get-tuple-element.32), channel_id=1, source_target_pairs={{0,48},{16,0},{32,16},{48,32},{1,49},{17,1},{33,17},{49,33},{2,50}... | collective-permute-start | bytes 393224 | tf_op jit(solution)/shard_map/ppermute | solution.py:169
  21.1 3.7 %collective-permute-start.23 = (f32[128,512]{1,0:T(8,128)S(1)}, f32[128,512]{1,0:T(8,128)S(1)}, u32[]{:S(2)}, u32[]{:S(2)}) collective-permute-start(f32[128,512]{1,0:T(8,128)S(1)} %get-tuple-element.36), channel_id=1, source_target_pairs={{0,200},{8,64},{64,8},{72,128},{128,72},{136,192},{192,136},{200,0... | collective-permute-start | bytes 786440 | tf_op jit(solution)/shard_map/ppermute | solution.py:231
  24.9 3.2 %collective-permute-start.5 = (f32[128,128]{1,0:T(8,128)S(1)}, f32[128,128]{1,0:T(8,128)S(1)}, u32[]{:S(2)}, u32[]{:S(2)}) collective-permute-start(f32[128,128]{1,0:T(8,128)S(1)} %slice.155), channel_id=1, source_target_pairs={{0,8},{8,0},{1,9},{9,1},{2,10},{10,2},{3,11},{11,3},{4,12},{12,4},... | collective-permute-start | bytes 196616 | tf_op jit(solution)/shard_map/ppermute | solution.py:169
  28.2 0.3 collective-permute-start.12
  28.5 1.9 %collective-permute-done.5 = f32[128,128]{1,0:T(8,128)S(1)} collective-permute-done((f32[128,128]{1,0:T(8,128)S(1)}, f32[128,128]{1,0:T(8,128)S(1)}, u32[]{:S(2)}, u32[]{:S(2)}) %collective-permute-start.5) | collective-permute-done | bytes 65568 | tf_op jit(solution)/shard_map/ppermute | solution.py:169
  30.4 1.3 %collective-permute-start.6 = (f32[32,128]{1,0:T(8,128)S(1)}, f32[32,128]{1,0:T(8,128)S(1)}, u32[]{:S(2)}, u32[]{:S(2)}) collective-permute-start(f32[32,128]{1,0:T(8,128)S(1)} %get-tuple-element.53), channel_id=1, source_target_pairs={{0,16},{16,32},{32,48},{48,0},{1,17},{17,33},{33,49},{49,1},{2,18}... | collective-permute-start | bytes 49160 | tf_op jit(solution)/shard_map/ppermute | solution.py:169
  31.6 2.1 %collective-permute-start.8 = (f32[32,128]{1,0:T(8,128)S(1)}, f32[32,128]{1,0:T(8,128)S(1)}, u32[]{:S(2)}, u32[]{:S(2)}) collective-permute-start(f32[32,128]{1,0:T(8,128)S(1)} %get-tuple-element.54), channel_id=1, source_target_pairs={{0,48},{16,0},{32,16},{48,32},{1,49},{17,1},{33,17},{49,33},{2,50}... | collective-permute-start | bytes 49160 | tf_op jit(solution)/shard_map/ppermute | solution.py:169
  33.7 1.6 %collective-permute-start.7 = (f32[32,128]{1,0:T(8,128)S(1)}, f32[32,128]{1,0:T(8,128)S(1)}, u32[]{:S(2)}, u32[]{:S(2)}) collective-permute-start(f32[32,128]{1,0:T(8,128)S(1)} %get-tuple-element.55), channel_id=1, source_target_pairs={{0,32},{16,48},{32,0},{48,16},{1,33},{17,49},{33,1},{49,17},{2,34}... | collective-permute-start | bytes 49160 | tf_op jit(solution)/shard_map/ppermute | solution.py:169
  35.4 0.6 collective-permute-start.13
  36.0 2.6 %collective-permute-start.15 = (f32[32,128]{1,0:T(8,128)S(1)}, f32[32,128]{1,0:T(8,128)S(1)}, u32[]{:S(2)}, u32[]{:S(2)}) collective-permute-start(f32[32,128]{1,0:T(8,128)S(1)} %get-tuple-element.57), channel_id=1, source_target_pairs={{0,6},{2,0},{4,2},{6,4},{1,7},{3,1},{5,3},{7,5},{8,14},{10,8},{12,... | collective-permute-start | bytes 49160 | tf_op jit(solution)/shard_map/ppermute | solution.py:169
  38.7 0.3 collective-permute-done.7
  38.9 1.3 %collective-permute-start.14 = (f32[32,128]{1,0:T(8,128)S(1)}, f32[32,128]{1,0:T(8,128)S(1)}, u32[]{:S(2)}, u32[]{:S(2)}) collective-permute-start(f32[32,128]{1,0:T(8,128)S(1)} %get-tuple-element.58), channel_id=1, source_target_pairs={{0,4},{2,6},{4,0},{6,2},{1,5},{3,7},{5,1},{7,3},{8,12},{10,14},{12... | collective-permute-start | bytes 49160 | tf_op jit(solution)/shard_map/ppermute | solution.py:169
  40.2 0.2 collective-permute-done.13
  40.4 3.8 %collective-permute-done.14 = f32[32,128]{1,0:T(8,128)S(1)} collective-permute-done((f32[32,128]{1,0:T(8,128)S(1)}, f32[32,128]{1,0:T(8,128)S(1)}, u32[]{:S(2)}, u32[]{:S(2)}) %collective-permute-start.14) | collective-permute-done | bytes 16416 | tf_op jit(solution)/shard_map/ppermute | solution.py:169
  44.5 0.5 collective-permute-start.24
  45.0 2.9 %collective-permute-start.26 = (f32[32,512]{1,0:T(8,128)S(1)}, f32[32,512]{1,0:T(8,128)S(1)}, u32[]{:S(2)}, u32[]{:S(2)}) collective-permute-start(f32[32,512]{1,0:T(8,128)S(1)} %get-tuple-element.51), channel_id=1, source_target_pairs={{0,48},{16,0},{32,16},{48,32},{1,49},{17,1},{33,17},{49,33},{2,50}... | collective-permute-start | bytes 196616 | tf_op jit(solution)/shard_map/ppermute | solution.py:169
  47.8 0.4 collective-permute-start.25
  48.3 0.4 collective-permute-start.17
  48.7 2.9 %collective-permute-start.19 = (f32[128,128]{1,0:T(8,128)S(1)}, f32[128,128]{1,0:T(8,128)S(1)}, u32[]{:S(2)}, u32[]{:S(2)}) collective-permute-start(f32[128,128]{1,0:T(8,128)S(1)} %get-tuple-element.48), channel_id=1, source_target_pairs={{0,6},{2,0},{4,2},{6,4},{1,7},{3,1},{5,3},{7,5},{8,14},{10,8},{12,... | collective-permute-start | bytes 196616 | tf_op jit(solution)/shard_map/ppermute | solution.py:169
  51.6 0.4 collective-permute-start.18
  52.0 1.6 %collective-permute-done.25 = f32[32,512]{1,0:T(8,128)S(1)} collective-permute-done((f32[32,512]{1,0:T(8,128)S(1)}, f32[32,512]{1,0:T(8,128)S(1)}, u32[]{:S(2)}, u32[]{:S(2)}) %collective-permute-start.25) | collective-permute-done | bytes 65568 | tf_op jit(solution)/shard_map/ppermute | solution.py:169
  53.6 0.7 collective-permute-start.27
  54.3 2.6 %collective-permute-start.29 = (f32[32,128]{1,0:T(8,128)S(1)}, f32[32,128]{1,0:T(8,128)S(1)}, u32[]{:S(2)}, u32[]{:S(2)}) collective-permute-start(f32[32,128]{1,0:T(8,128)S(1)} %get-tuple-element.63), channel_id=1, source_target_pairs={{0,6},{2,0},{4,2},{6,4},{1,7},{3,1},{5,3},{7,5},{8,14},{10,8},{12,... | collective-permute-start | bytes 49160 | tf_op jit(solution)/shard_map/ppermute | solution.py:169
  56.9 0.4 collective-permute-start.28
  57.5 0.7 collective-permute-start.20
  58.2 2.6 %collective-permute-start.22 = (f32[32,128]{1,0:T(8,128)S(1)}, f32[32,128]{1,0:T(8,128)S(1)}, u32[]{:S(2)}, u32[]{:S(2)}) collective-permute-start(f32[32,128]{1,0:T(8,128)S(1)} %get-tuple-element.60), channel_id=1, source_target_pairs={{0,48},{16,0},{32,16},{48,32},{1,49},{17,1},{33,17},{49,33},{2,50}... | collective-permute-start | bytes 49160 | tf_op jit(solution)/shard_map/ppermute | solution.py:169
  60.8 1.9 %collective-permute-start.21 = (f32[32,128]{1,0:T(8,128)S(1)}, f32[32,128]{1,0:T(8,128)S(1)}, u32[]{:S(2)}, u32[]{:S(2)}) collective-permute-start(f32[32,128]{1,0:T(8,128)S(1)} %get-tuple-element.61), channel_id=1, source_target_pairs={{0,32},{16,48},{32,0},{48,16},{1,33},{17,49},{33,1},{49,17},{2,34}... | collective-permute-start | bytes 49160 | tf_op jit(solution)/shard_map/ppermute | solution.py:169
  62.8 3.3 %collective-permute-done.21 = f32[32,128]{1,0:T(8,128)S(1)} collective-permute-done((f32[32,128]{1,0:T(8,128)S(1)}, f32[32,128]{1,0:T(8,128)S(1)}, u32[]{:S(2)}, u32[]{:S(2)}) %collective-permute-start.21) | collective-permute-done | bytes 16416 | tf_op jit(solution)/shard_map/ppermute | solution.py:169
  66.3 0.1 pad_maximum_fusion
  66.6 3.8 %collective-permute-start.36 = (f32[32,2,32]{2,0,1:T(8,128)S(1)}, f32[32,2,32]{2,0,1:T(8,128)S(1)}, u32[]{:S(2)}, u32[]{:S(2)}) collective-permute-start(f32[32,2,32]{2,0,1:T(8,128)S(1)} %get-tuple-element.41), channel_id=1, source_target_pairs={{0,193},{1,192},{64,1},{65,0},{128,65},{129,64},{192,129},{193,128... | collective-permute-start | bytes 24584 | tf_op jit(solution)/shard_map/ppermute | solution.py:251
  70.4 3.3 %collective-permute-start.35 = (f32[32,2,32]{2,0,1:T(8,128)S(1)}, f32[32,2,32]{2,0,1:T(8,128)S(1)}, u32[]{:S(2)}, u32[]{:S(2)}) collective-permute-start(f32[32,2,32]{2,0,1:T(8,128)S(1)} %get-tuple-element.42), channel_id=1, source_target_pairs={{0,129},{1,128},{64,193},{65,192},{128,1},{129,0},{192,65},{193,64... | collective-permute-start | bytes 24584 | tf_op jit(solution)/shard_map/ppermute | solution.py:251
  73.7 2.8 %collective-permute-start.33 = (f32[32,2,32]{2,0,1:T(8,128)S(1)}, f32[32,2,32]{2,0,1:T(8,128)S(1)}, u32[]{:S(2)}, u32[]{:S(2)}) collective-permute-start(f32[32,2,32]{2,0,1:T(8,128)S(1)} %get-tuple-element.43), channel_id=1, source_target_pairs={{0,1},{1,0},{64,65},{65,64},{128,129},{129,128},{192,193},{193,192... | collective-permute-start | bytes 24584 | tf_op jit(solution)/shard_map/ppermute | solution.py:251
  76.5 3.8 %collective-permute-start.31 = (f32[32,2,32]{2,0,1:T(8,128)S(1)}, f32[32,2,32]{2,0,1:T(8,128)S(1)}, u32[]{:S(2)}, u32[]{:S(2)}) collective-permute-start(f32[32,2,32]{2,0,1:T(8,128)S(1)} %get-tuple-element.45), channel_id=1, source_target_pairs={{0,128},{1,129},{64,192},{65,193},{128,0},{129,1},{192,64},{193,65... | collective-permute-start | bytes 24584 | tf_op jit(solution)/shard_map/ppermute | solution.py:251
  80.3 1.1 %collective-permute-done.32 = f32[32,2,32]{2,0,1:T(8,128)S(1)} collective-permute-done((f32[32,2,32]{2,0,1:T(8,128)S(1)}, f32[32,2,32]{2,0,1:T(8,128)S(1)}, u32[]{:S(2)}, u32[]{:S(2)}) %collective-permute-start.32) | collective-permute-done | bytes 8224 | tf_op jit(solution)/shard_map/ppermute | solution.py:251
  81.5 2.8 %collective-permute-done.31 = f32[32,2,32]{2,0,1:T(8,128)S(1)} collective-permute-done((f32[32,2,32]{2,0,1:T(8,128)S(1)}, f32[32,2,32]{2,0,1:T(8,128)S(1)}, u32[]{:S(2)}, u32[]{:S(2)}) %collective-permute-start.31) | collective-permute-done | bytes 8224 | tf_op jit(solution)/shard_map/ppermute | solution.py:251
  84.3 2.0 %collective-permute-done.30 = f32[32,2,32]{2,0,1:T(8,128)S(1)} collective-permute-done((f32[32,2,32]{2,0,1:T(8,128)S(1)}, f32[32,2,32]{2,0,1:T(8,128)S(1)}, u32[]{:S(2)}, u32[]{:S(2)}) %collective-permute-start.30) | collective-permute-done | bytes 8224 | tf_op jit(solution)/shard_map/ppermute | solution.py:251
  86.4 0.6 pad_maximum_fusion.1
  (81 shorter events, 1.4 us)
Async XLA Ops:
  0.0 2.3 %copy-start = (bf16[2,512,512]{2,1,0:T(8,128)(2,1)S(1)}, bf16[2,512,512]{2,1,0:T(8,128)(2,1)}, u32[]{:S(2)}) copy-start(bf16[2,512,512]{2,1,0:T(8,128)(2,1)} %image.1) | copy-start | bytes 3145732
  0.0 1.8 %copy-start.2 = (f32[512]{0:T(512)S(1)}, f32[512]{0:T(512)}, u32[]{:S(2)}) copy-start(f32[512]{0:T(512)} %param.11) | copy-start | bytes 6148
  0.0 2.3 %copy-start.8 = (s32[2]{0:T(128)S(1)}, s32[2]{0:T(128)}, u32[]{:S(2)}) copy-start(s32[2]{0:T(128)} %sc.3) | copy-start | bytes 28
  0.0 2.3 %copy-start.7 = (s32[2]{0:T(128)S(1)}, s32[2]{0:T(128)}, u32[]{:S(2)}) copy-start(s32[2]{0:T(128)} %bo.3) | copy-start | bytes 28
  0.0 2.2 %copy-start.6 = (s32[16]{0:T(128)S(1)}, s32[16]{0:T(128)}, u32[]{:S(2)}) copy-start(s32[16]{0:T(128)} %fco.3) | copy-start | bytes 196
  0.0 2.2 %copy-start.5 = (f32[2]{0:T(128)S(1)}, f32[2]{0:T(128)}, u32[]{:S(2)}) copy-start(f32[2]{0:T(128)} %w_terms.3) | copy-start | bytes 28
  0.0 2.2 %copy-start.4 = (s32[2]{0:T(128)S(1)}, s32[2]{0:T(128)}, u32[]{:S(2)}) copy-start(s32[2]{0:T(128)} %sro.1) | copy-start | bytes 28
  0.0 2.2 %copy-start.3 = (s32[16]{0:T(128)S(1)}, s32[16]{0:T(128)}, u32[]{:S(2)}) copy-start(s32[16]{0:T(128)} %fro.1) | copy-start | bytes 196
  0.1 2.2 %copy-start.1 = (f32[512]{0:T(512)S(1)}, f32[512]{0:T(512)}, u32[]{:S(2)}) copy-start(f32[512]{0:T(512)} %param.10) | copy-start | bytes 6148
  1.7 5.4 %collective-permute-start.1 = (f32[2,512,512]{2,1,0:T(8,128)S(1)}, f32[2,512,512]{2,1,0:T(8,128)S(1)}, u32[]{:S(2)}, u32[]{:S(2)}) collective-permute-start(f32[2,512,512]{2,1,0:T(8,128)S(1)} %convert_element_type.3), channel_id=1, source_target_pairs={{0,1},{1,0},{2,3},{3,2},{4,5},{5,4},{6,7},{7,6},{8,9},{9,8},{10,11... | collective-permute-start | bytes 6291464 | tf_op jit(solution)/shard_map/ppermute | solution.py:196
  1.8 4.1 %collective-permute-start = (f32[1,512]{1,0:T(1,128)S(1)}, f32[1,512]{1,0:T(1,128)S(1)}, u32[]{:S(2)}, u32[]{:S(2)}) collective-permute-start(f32[1,512]{1,0:T(1,128)S(1)} %bitcast.37), channel_id=1, source_target_pairs={{0,1},{1,0},{2,3},{3,2},{4,5},{5,4},{6,7},{7,6},{8,9},{9,8},{10,11... | collective-permute-start | bytes 6152 | tf_op jit(solution)/shard_map/ppermute | solution.py:195
  9.4 10.2 %collective-permute-start.2 = (f32[128,256]{1,0:T(8,128)S(1)}, f32[128,256]{1,0:T(8,128)S(1)}, u32[]{:S(2)}, u32[]{:S(2)}) collective-permute-start(f32[128,256]{1,0:T(8,128)S(1)} %get-tuple-element.26), channel_id=1, source_target_pairs={{0,2},{2,4},{4,6},{6,0},{1,3},{3,5},{5,7},{7,1},{8,10},{10,12},{12... | collective-permute-start | bytes 393224 | tf_op jit(solution)/shard_map/ppermute | solution.py:169
  11.0 10.0 %collective-permute-start.3 = (f32[128,256]{1,0:T(8,128)S(1)}, f32[128,256]{1,0:T(8,128)S(1)}, u32[]{:S(2)}, u32[]{:S(2)}) collective-permute-start(f32[128,256]{1,0:T(8,128)S(1)} %get-tuple-element.27), channel_id=1, source_target_pairs={{0,4},{2,6},{4,0},{6,2},{1,5},{3,7},{5,1},{7,3},{8,12},{10,14},{12... | collective-permute-start | bytes 393224 | tf_op jit(solution)/shard_map/ppermute | solution.py:169
  13.7 7.4 %collective-permute-start.4 = (f32[128,256]{1,0:T(8,128)S(1)}, f32[128,256]{1,0:T(8,128)S(1)}, u32[]{:S(2)}, u32[]{:S(2)}) collective-permute-start(f32[128,256]{1,0:T(8,128)S(1)} %get-tuple-element.28), channel_id=1, source_target_pairs={{0,6},{2,0},{4,2},{6,4},{1,7},{3,1},{5,3},{7,5},{8,14},{10,8},{12,... | collective-permute-start | bytes 393224 | tf_op jit(solution)/shard_map/ppermute | solution.py:169
  15.2 9.7 %collective-permute-start.9 = (f32[32,1024]{1,0:T(8,128)S(1)}, f32[32,1024]{1,0:T(8,128)S(1)}, u32[]{:S(2)}, u32[]{:S(2)}) collective-permute-start(f32[32,1024]{1,0:T(8,128)S(1)} %get-tuple-element.30), channel_id=1, source_target_pairs={{0,16},{16,32},{32,48},{48,0},{1,17},{17,33},{33,49},{49,1},{2,18}... | collective-permute-start | bytes 393224 | tf_op jit(solution)/shard_map/ppermute | solution.py:169
  16.7 11.4 %collective-permute-start.10 = (f32[32,1024]{1,0:T(8,128)S(1)}, f32[32,1024]{1,0:T(8,128)S(1)}, u32[]{:S(2)}, u32[]{:S(2)}) collective-permute-start(f32[32,1024]{1,0:T(8,128)S(1)} %get-tuple-element.31), channel_id=1, source_target_pairs={{0,32},{16,48},{32,0},{48,16},{1,33},{17,49},{33,1},{49,17},{2,34}... | collective-permute-start | bytes 393224 | tf_op jit(solution)/shard_map/ppermute | solution.py:169
  19.6 8.5 %collective-permute-start.11 = (f32[32,1024]{1,0:T(8,128)S(1)}, f32[32,1024]{1,0:T(8,128)S(1)}, u32[]{:S(2)}, u32[]{:S(2)}) collective-permute-start(f32[32,1024]{1,0:T(8,128)S(1)} %get-tuple-element.32), channel_id=1, source_target_pairs={{0,48},{16,0},{32,16},{48,32},{1,49},{17,1},{33,17},{49,33},{2,50}... | collective-permute-start | bytes 393224 | tf_op jit(solution)/shard_map/ppermute | solution.py:169
  21.0 27.3 %collective-permute-start.16 = (f32[128,512]{1,0:T(8,128)S(1)}, f32[128,512]{1,0:T(8,128)S(1)}, u32[]{:S(2)}, u32[]{:S(2)}) collective-permute-start(f32[128,512]{1,0:T(8,128)S(1)} %get-tuple-element.34), channel_id=1, source_target_pairs={{0,8},{8,0},{1,9},{9,1},{2,10},{10,2},{3,11},{11,3},{4,12},{12,4},... | collective-permute-start | bytes 786440 | tf_op jit(solution)/shard_map/ppermute | solution.py:169
  21.1 23.3 %collective-permute-start.23 = (f32[128,512]{1,0:T(8,128)S(1)}, f32[128,512]{1,0:T(8,128)S(1)}, u32[]{:S(2)}, u32[]{:S(2)}) collective-permute-start(f32[128,512]{1,0:T(8,128)S(1)} %get-tuple-element.36), channel_id=1, source_target_pairs={{0,200},{8,64},{64,8},{72,128},{128,72},{136,192},{192,136},{200,0... | collective-permute-start | bytes 786440 | tf_op jit(solution)/shard_map/ppermute | solution.py:231
  24.9 5.5 %collective-permute-start.5 = (f32[128,128]{1,0:T(8,128)S(1)}, f32[128,128]{1,0:T(8,128)S(1)}, u32[]{:S(2)}, u32[]{:S(2)}) collective-permute-start(f32[128,128]{1,0:T(8,128)S(1)} %slice.155), channel_id=1, source_target_pairs={{0,8},{8,0},{1,9},{9,1},{2,10},{10,2},{3,11},{11,3},{4,12},{12,4},... | collective-permute-start | bytes 196616 | tf_op jit(solution)/shard_map/ppermute | solution.py:169
  28.2 5.5 %collective-permute-start.12 = (f32[32,512]{1,0:T(8,128)S(1)}, f32[32,512]{1,0:T(8,128)S(1)}, u32[]{:S(2)}, u32[]{:S(2)}) collective-permute-start(f32[32,512]{1,0:T(8,128)S(1)} %slice.161), channel_id=1, source_target_pairs={{0,8},{8,0},{1,9},{9,1},{2,10},{10,2},{3,11},{11,3},{4,12},{12,4},... | collective-permute-start | bytes 196616 | tf_op jit(solution)/shard_map/ppermute | solution.py:169
  30.4 5.0 %collective-permute-start.6 = (f32[32,128]{1,0:T(8,128)S(1)}, f32[32,128]{1,0:T(8,128)S(1)}, u32[]{:S(2)}, u32[]{:S(2)}) collective-permute-start(f32[32,128]{1,0:T(8,128)S(1)} %get-tuple-element.53), channel_id=1, source_target_pairs={{0,16},{16,32},{32,48},{48,0},{1,17},{17,33},{33,49},{49,1},{2,18}... | collective-permute-start | bytes 49160 | tf_op jit(solution)/shard_map/ppermute | solution.py:169
  31.6 4.4 %collective-permute-start.8 = (f32[32,128]{1,0:T(8,128)S(1)}, f32[32,128]{1,0:T(8,128)S(1)}, u32[]{:S(2)}, u32[]{:S(2)}) collective-permute-start(f32[32,128]{1,0:T(8,128)S(1)} %get-tuple-element.54), channel_id=1, source_target_pairs={{0,48},{16,0},{32,16},{48,32},{1,49},{17,1},{33,17},{49,33},{2,50}... | collective-permute-start | bytes 49160 | tf_op jit(solution)/shard_map/ppermute | solution.py:169
  33.7 5.2 %collective-permute-start.7 = (f32[32,128]{1,0:T(8,128)S(1)}, f32[32,128]{1,0:T(8,128)S(1)}, u32[]{:S(2)}, u32[]{:S(2)}) collective-permute-start(f32[32,128]{1,0:T(8,128)S(1)} %get-tuple-element.55), channel_id=1, source_target_pairs={{0,32},{16,48},{32,0},{48,16},{1,33},{17,49},{33,1},{49,17},{2,34}... | collective-permute-start | bytes 49160 | tf_op jit(solution)/shard_map/ppermute | solution.py:169
  35.4 4.9 %collective-permute-start.13 = (f32[32,128]{1,0:T(8,128)S(1)}, f32[32,128]{1,0:T(8,128)S(1)}, u32[]{:S(2)}, u32[]{:S(2)}) collective-permute-start(f32[32,128]{1,0:T(8,128)S(1)} %get-tuple-element.56), channel_id=1, source_target_pairs={{0,2},{2,4},{4,6},{6,0},{1,3},{3,5},{5,7},{7,1},{8,10},{10,12},{12... | collective-permute-start | bytes 49160 | tf_op jit(solution)/shard_map/ppermute | solution.py:169
  36.0 4.4 %collective-permute-start.15 = (f32[32,128]{1,0:T(8,128)S(1)}, f32[32,128]{1,0:T(8,128)S(1)}, u32[]{:S(2)}, u32[]{:S(2)}) collective-permute-start(f32[32,128]{1,0:T(8,128)S(1)} %get-tuple-element.57), channel_id=1, source_target_pairs={{0,6},{2,0},{4,2},{6,4},{1,7},{3,1},{5,3},{7,5},{8,14},{10,8},{12,... | collective-permute-start | bytes 49160 | tf_op jit(solution)/shard_map/ppermute | solution.py:169
  38.9 5.2 %collective-permute-start.14 = (f32[32,128]{1,0:T(8,128)S(1)}, f32[32,128]{1,0:T(8,128)S(1)}, u32[]{:S(2)}, u32[]{:S(2)}) collective-permute-start(f32[32,128]{1,0:T(8,128)S(1)} %get-tuple-element.58), channel_id=1, source_target_pairs={{0,4},{2,6},{4,0},{6,2},{1,5},{3,7},{5,1},{7,3},{8,12},{10,14},{12... | collective-permute-start | bytes 49160 | tf_op jit(solution)/shard_map/ppermute | solution.py:169
  44.5 7.1 %collective-permute-start.24 = (f32[32,512]{1,0:T(8,128)S(1)}, f32[32,512]{1,0:T(8,128)S(1)}, u32[]{:S(2)}, u32[]{:S(2)}) collective-permute-start(f32[32,512]{1,0:T(8,128)S(1)} %get-tuple-element.50), channel_id=1, source_target_pairs={{0,16},{16,32},{32,48},{48,0},{1,17},{17,33},{33,49},{49,1},{2,18}... | collective-permute-start | bytes 196616 | tf_op jit(solution)/shard_map/ppermute | solution.py:169
  45.0 7.1 %collective-permute-start.26 = (f32[32,512]{1,0:T(8,128)S(1)}, f32[32,512]{1,0:T(8,128)S(1)}, u32[]{:S(2)}, u32[]{:S(2)}) collective-permute-start(f32[32,512]{1,0:T(8,128)S(1)} %get-tuple-element.51), channel_id=1, source_target_pairs={{0,48},{16,0},{32,16},{48,32},{1,49},{17,1},{33,17},{49,33},{2,50}... | collective-permute-start | bytes 196616 | tf_op jit(solution)/shard_map/ppermute | solution.py:169
  47.8 5.8 %collective-permute-start.25 = (f32[32,512]{1,0:T(8,128)S(1)}, f32[32,512]{1,0:T(8,128)S(1)}, u32[]{:S(2)}, u32[]{:S(2)}) collective-permute-start(f32[32,512]{1,0:T(8,128)S(1)} %get-tuple-element.52), channel_id=1, source_target_pairs={{0,32},{16,48},{32,0},{48,16},{1,33},{17,49},{33,1},{49,17},{2,34}... | collective-permute-start | bytes 196616 | tf_op jit(solution)/shard_map/ppermute | solution.py:169
  48.3 8.6 %collective-permute-start.17 = (f32[128,128]{1,0:T(8,128)S(1)}, f32[128,128]{1,0:T(8,128)S(1)}, u32[]{:S(2)}, u32[]{:S(2)}) collective-permute-start(f32[128,128]{1,0:T(8,128)S(1)} %get-tuple-element.47), channel_id=1, source_target_pairs={{0,2},{2,4},{4,6},{6,0},{1,3},{3,5},{5,7},{7,1},{8,10},{10,12},{12... | collective-permute-start | bytes 196616 | tf_op jit(solution)/shard_map/ppermute | solution.py:169
  48.7 8.6 %collective-permute-start.19 = (f32[128,128]{1,0:T(8,128)S(1)}, f32[128,128]{1,0:T(8,128)S(1)}, u32[]{:S(2)}, u32[]{:S(2)}) collective-permute-start(f32[128,128]{1,0:T(8,128)S(1)} %get-tuple-element.48), channel_id=1, source_target_pairs={{0,6},{2,0},{4,2},{6,4},{1,7},{3,1},{5,3},{7,5},{8,14},{10,8},{12,... | collective-permute-start | bytes 196616 | tf_op jit(solution)/shard_map/ppermute | solution.py:169
  51.6 5.8 %collective-permute-start.18 = (f32[128,128]{1,0:T(8,128)S(1)}, f32[128,128]{1,0:T(8,128)S(1)}, u32[]{:S(2)}, u32[]{:S(2)}) collective-permute-start(f32[128,128]{1,0:T(8,128)S(1)} %get-tuple-element.49), channel_id=1, source_target_pairs={{0,4},{2,6},{4,0},{6,2},{1,5},{3,7},{5,1},{7,3},{8,12},{10,14},{12... | collective-permute-start | bytes 196616 | tf_op jit(solution)/shard_map/ppermute | solution.py:169
  53.6 7.1 %collective-permute-start.27 = (f32[32,128]{1,0:T(8,128)S(1)}, f32[32,128]{1,0:T(8,128)S(1)}, u32[]{:S(2)}, u32[]{:S(2)}) collective-permute-start(f32[32,128]{1,0:T(8,128)S(1)} %get-tuple-element.62), channel_id=1, source_target_pairs={{0,2},{2,4},{4,6},{6,0},{1,3},{3,5},{5,7},{7,1},{8,10},{10,12},{12... | collective-permute-start | bytes 49160 | tf_op jit(solution)/shard_map/ppermute | solution.py:169
  54.3 8.4 %collective-permute-start.29 = (f32[32,128]{1,0:T(8,128)S(1)}, f32[32,128]{1,0:T(8,128)S(1)}, u32[]{:S(2)}, u32[]{:S(2)}) collective-permute-start(f32[32,128]{1,0:T(8,128)S(1)} %get-tuple-element.63), channel_id=1, source_target_pairs={{0,6},{2,0},{4,2},{6,4},{1,7},{3,1},{5,3},{7,5},{8,14},{10,8},{12,... | collective-permute-start | bytes 49160 | tf_op jit(solution)/shard_map/ppermute | solution.py:169
  56.9 5.8 %collective-permute-start.28 = (f32[32,128]{1,0:T(8,128)S(1)}, f32[32,128]{1,0:T(8,128)S(1)}, u32[]{:S(2)}, u32[]{:S(2)}) collective-permute-start(f32[32,128]{1,0:T(8,128)S(1)} %get-tuple-element.64), channel_id=1, source_target_pairs={{0,4},{2,6},{4,0},{6,2},{1,5},{3,7},{5,1},{7,3},{8,12},{10,14},{12... | collective-permute-start | bytes 49160 | tf_op jit(solution)/shard_map/ppermute | solution.py:169
  57.5 5.3 %collective-permute-start.20 = (f32[32,128]{1,0:T(8,128)S(1)}, f32[32,128]{1,0:T(8,128)S(1)}, u32[]{:S(2)}, u32[]{:S(2)}) collective-permute-start(f32[32,128]{1,0:T(8,128)S(1)} %get-tuple-element.59), channel_id=1, source_target_pairs={{0,16},{16,32},{32,48},{48,0},{1,17},{17,33},{33,49},{49,1},{2,18}... | collective-permute-start | bytes 49160 | tf_op jit(solution)/shard_map/ppermute | solution.py:169
  58.2 4.6 %collective-permute-start.22 = (f32[32,128]{1,0:T(8,128)S(1)}, f32[32,128]{1,0:T(8,128)S(1)}, u32[]{:S(2)}, u32[]{:S(2)}) collective-permute-start(f32[32,128]{1,0:T(8,128)S(1)} %get-tuple-element.60), channel_id=1, source_target_pairs={{0,48},{16,0},{32,16},{48,32},{1,49},{17,1},{33,17},{49,33},{2,50}... | collective-permute-start | bytes 49160 | tf_op jit(solution)/shard_map/ppermute | solution.py:169
  60.8 5.2 %collective-permute-start.21 = (f32[32,128]{1,0:T(8,128)S(1)}, f32[32,128]{1,0:T(8,128)S(1)}, u32[]{:S(2)}, u32[]{:S(2)}) collective-permute-start(f32[32,128]{1,0:T(8,128)S(1)} %get-tuple-element.61), channel_id=1, source_target_pairs={{0,32},{16,48},{32,0},{48,16},{1,33},{17,49},{33,1},{49,17},{2,34}... | collective-permute-start | bytes 49160 | tf_op jit(solution)/shard_map/ppermute | solution.py:169
  66.5 10.0 %collective-permute-start.34 = (f32[32,2,32]{2,0,1:T(8,128)S(1)}, f32[32,2,32]{2,0,1:T(8,128)S(1)}, u32[]{:S(2)}, u32[]{:S(2)}) collective-permute-start(f32[32,2,32]{2,0,1:T(8,128)S(1)} %get-tuple-element.40), channel_id=1, source_target_pairs={{0,65},{1,64},{64,129},{65,128},{128,193},{129,192},{192,1},{193,0... | collective-permute-start | bytes 24584 | tf_op jit(solution)/shard_map/ppermute | solution.py:251
  66.6 13.7 %collective-permute-start.36 = (f32[32,2,32]{2,0,1:T(8,128)S(1)}, f32[32,2,32]{2,0,1:T(8,128)S(1)}, u32[]{:S(2)}, u32[]{:S(2)}) collective-permute-start(f32[32,2,32]{2,0,1:T(8,128)S(1)} %get-tuple-element.41), channel_id=1, source_target_pairs={{0,193},{1,192},{64,1},{65,0},{128,65},{129,64},{192,129},{193,128... | collective-permute-start | bytes 24584 | tf_op jit(solution)/shard_map/ppermute | solution.py:251
  70.4 9.9 %collective-permute-start.35 = (f32[32,2,32]{2,0,1:T(8,128)S(1)}, f32[32,2,32]{2,0,1:T(8,128)S(1)}, u32[]{:S(2)}, u32[]{:S(2)}) collective-permute-start(f32[32,2,32]{2,0,1:T(8,128)S(1)} %get-tuple-element.42), channel_id=1, source_target_pairs={{0,129},{1,128},{64,193},{65,192},{128,1},{129,0},{192,65},{193,64... | collective-permute-start | bytes 24584 | tf_op jit(solution)/shard_map/ppermute | solution.py:251
  73.7 6.6 %collective-permute-start.33 = (f32[32,2,32]{2,0,1:T(8,128)S(1)}, f32[32,2,32]{2,0,1:T(8,128)S(1)}, u32[]{:S(2)}, u32[]{:S(2)}) collective-permute-start(f32[32,2,32]{2,0,1:T(8,128)S(1)} %get-tuple-element.43), channel_id=1, source_target_pairs={{0,1},{1,0},{64,65},{65,64},{128,129},{129,128},{192,193},{193,192... | collective-permute-start | bytes 24584 | tf_op jit(solution)/shard_map/ppermute | solution.py:251
  76.5 5.0 %collective-permute-start.32 = (f32[32,2,32]{2,0,1:T(8,128)S(1)}, f32[32,2,32]{2,0,1:T(8,128)S(1)}, u32[]{:S(2)}, u32[]{:S(2)}) collective-permute-start(f32[32,2,32]{2,0,1:T(8,128)S(1)} %get-tuple-element.44), channel_id=1, source_target_pairs={{0,192},{1,193},{64,0},{65,1},{128,64},{129,65},{192,128},{193,129... | collective-permute-start | bytes 24584 | tf_op jit(solution)/shard_map/ppermute | solution.py:251
  76.5 7.8 %collective-permute-start.31 = (f32[32,2,32]{2,0,1:T(8,128)S(1)}, f32[32,2,32]{2,0,1:T(8,128)S(1)}, u32[]{:S(2)}, u32[]{:S(2)}) collective-permute-start(f32[32,2,32]{2,0,1:T(8,128)S(1)} %get-tuple-element.45), channel_id=1, source_target_pairs={{0,128},{1,129},{64,192},{65,193},{128,0},{129,1},{192,64},{193,65... | collective-permute-start | bytes 24584 | tf_op jit(solution)/shard_map/ppermute | solution.py:251
  80.3 6.0 %collective-permute-start.30 = (f32[32,2,32]{2,0,1:T(8,128)S(1)}, f32[32,2,32]{2,0,1:T(8,128)S(1)}, u32[]{:S(2)}, u32[]{:S(2)}) collective-permute-start(f32[32,2,32]{2,0,1:T(8,128)S(1)} %get-tuple-element.46), channel_id=1, source_target_pairs={{0,64},{1,65},{64,128},{65,129},{128,192},{129,193},{192,0},{193,1... | collective-permute-start | bytes 24584 | tf_op jit(solution)/shard_map/ppermute | solution.py:251

commit v2 on v1

v2 whole, which is shorter than its diff:
```python
import itertools
import math

import jax
import jax.numpy as jnp
from jax import lax
from jax.experimental import pallas as pl
from jax.experimental.pallas import tpu as pltpu
from jax.sharding import Mesh
from jax.sharding import PartitionSpec as P

IMAGE = 65536
F = 512
f32 = jnp.float32
bf16 = jnp.bfloat16
FROW = ("zh", "y")
FCOL = ("zl", "x", "c")
Z = ("zh", "zl")
PIO2 = (1.5703125, 4.837512969970703125e-4, 7.549789948768648e-8)
NT = (((1,), (1,)), ((), ()))
NN = (((1,), (0,)), ((), ()))


def sincos_of(r, q):
    z = r * r
    s = r + r * z * (-1.6666654611e-1 + z * (8.3321608736e-3 - 1.9515295891e-4 * z))
    c = 1.0 - 0.5 * z + z * z * (4.166664568298827e-2 + z * (-1.388731625493765e-3 + 2.443315711809948e-5 * z))
    odd = (q & 1) == 1
    cosine = jnp.where(odd, s, c)
    sine = jnp.where(odd, c, s)
    cosine = jnp.where(((q + 1) & 2) == 2, -cosine, cosine)
    sine = jnp.where((q & 2) == 2, -sine, sine)
    return cosine, sine


def turn(p):
    q = (p + 8192) >> 14
    r = (p - (q << 14)).astype(f32) * (2.0 * math.pi / IMAGE)
    c, s = sincos_of(r, q)
    return c, -s


def phase_index(first, second):
    high = ((first * (second >> 8)) & 255) << 8
    return (high + first * (second & 255)) & (IMAGE - 1)


def chirp(w, g):
    unit = (g & (IMAGE - 1)).astype(f32) * (1.0 / IMAGE) - 0.5
    angle = w * (unit * unit)
    n = jnp.floor(angle * (2.0 / math.pi) + 0.5)
    r = ((angle - n * PIO2[0]) - n * PIO2[1]) - n * PIO2[2]
    return sincos_of(r, n.astype(jnp.int32))


def times(a, b):
    return a[0] * b[0] - a[1] * b[1], a[0] * b[1] + a[1] * b[0]


def ids():
    return {name: lax.axis_index(name) for name in ("zh", "y", "zl", "x", "c")}


def outer(a, b):
    n = a[0].shape[1]
    big = [v[:, None, :] for v in a]
    small = [v[None, :, :] for v in b]
    return [v.reshape(-1, n) for v in times(big, small)]


def gray(i):
    return i ^ (i >> 1)


def near(own, high, low, core):
    low_first = high | (low << 1)
    high_first = low | (high << 1)
    return gray(gray(own) ^ jnp.where(core == 0, low_first, high_first))


def per_sub(sub, values):
    return jnp.where(sub == 0, values[0], values[1])


def column_factors(at, w_terms, bo, sc, offset, window):
    g = offset + lax.broadcasted_iota(jnp.int32, (1, F), 1)
    i = lax.broadcasted_iota(jnp.int32, (16, F), 0)
    x = near(at["x"], i >> 3, (i >> 2) & 1, at["c"])
    sub = (i >> 1) & 1
    zl = at["zl"] ^ (i & 1)
    band = per_sub(sub, [bo[sc[k]] for k in range(2)])
    coarse = turn(phase_index(g, band + ((zl * 4 + x) * 2 + at["c"]) * 32))
    waves = [chirp(w_terms[sc[k]], g) for k in range(2)]
    wave = [per_sub(sub, [v[part] * window for v in waves]) for part in range(2)]
    coarse = times(coarse, wave)
    fine = turn((g * lax.broadcasted_iota(jnp.int32, (32, F), 0)) & (IMAGE - 1))
    return coarse, fine


def column_table(factors, t):
    coarse, fine = factors
    first, second = [], []
    for zl in range(2):
        row = 2 * t + zl
        re, im = outer([v[row : row + 1] for v in coarse], fine)
        first += [re, im]
        second += [-im, re]
    return [jnp.concatenate(v, axis=0).astype(bf16) for v in (first, second)]


def own_kernel(w_terms, fro, fco, bo, sro, sc, image, wrow, wcol, rt, g_out, w1, w2):
    at = ids()
    me = (at["zl"] * 4 + at["x"]) * 2 + at["c"]
    factors = column_factors(at, w_terms, bo, sc, fco[me], wcol[...])
    for t in range(8):
        rows = pl.ds(t * 128, 128)
        w1[rows, :], w2[rows, :] = column_table(factors, t)
    for n in range(4):
        rows = pl.ds(n * 256, 256)
        g_out[:, rows] = lax.dot_general(image[0], w1[rows, :], NT, preferred_element_type=f32) + lax.dot_general(
            image[1], w2[rows, :], NT, preferred_element_type=f32
        )
    g = fro[at["zh"] * 4 + at["y"]] + lax.broadcasted_iota(jnp.int32, (1, F), 1)
    i = lax.broadcasted_iota(jnp.int32, (16, F), 0)
    window = wrow[...] * (1.0 / 8192.0)
    fine = turn((g * lax.broadcasted_iota(jnp.int32, (32, F), 0)) & (IMAGE - 1))
    y = near(at["y"], i >> 3, (i >> 2) & 1, at["c"])
    zh = near(at["zh"], (i >> 1) & 1, i & 1, at["c"])
    for k in range(2):
        wave = [v * window for v in chirp(w_terms[sc[k]], g)]
        coarse = times(turn(phase_index(g, sro[k] + (zh * 4 + y) * 32)), wave)
        for part in range(2):
            re, im = outer(coarse, [v[part * 16 : part * 16 + 16] for v in fine])
            rt[k, pl.ds(part * 256, 256), pl.ds(0, F)] = re.astype(bf16)
            rt[k, pl.ds(part * 256, 256), pl.ds(F, F)] = im.astype(bf16)


def other_kernel(w_terms, fco, bo, sc, wcol, w1, w2):
    at = ids()
    me = (at["zl"] * 4 + at["x"]) * 2 + (1 - at["c"])
    factors = column_factors(at, w_terms, bo, sc, fco[me], wcol[...])
    for t in range(8):
        rows = pl.ds(t * 128, 128)
        w1[rows, :], w2[rows, :] = column_table(factors, t)


def sum_kernel(rt, g_own, w1, w2, image, a_keep, a_send, b_keep, b_send, gg, im):
    im[0] = image[0].astype(bf16)
    im[1] = image[1].astype(bf16)
    imag = (lax.broadcasted_iota(jnp.int32, (F, 128), 1) & 32) == 32
    for n in range(4):
        rows = pl.ds(n * 256, 256)
        g = g_own[:, rows] + lax.dot_general(im[0], w1[rows, :], NT, preferred_element_type=f32)
        g = g + lax.dot_general(im[1], w2[rows, :], NT, preferred_element_type=f32)
        for k in range(2):
            tile = g[:, k * 128 : k * 128 + 128]
            turned = jnp.where(imag, pltpu.roll(tile, 32, 1), -pltpu.roll(tile, 96, 1))
            cols = pl.ds(n * 128, 128)
            gg[k, pl.ds(0, F), cols] = tile.astype(bf16)
            gg[k, pl.ds(F, F), cols] = turned.astype(bf16)
    for k in range(2):
        for half in range(2):
            s = lax.dot_general(rt[k], gg[k, :, pl.ds(half * 256, 256)], NN, preferred_element_type=f32)
            a_out = a_send if half else a_keep
            for low in range(2):
                tile = s[:, low * 128 : low * 128 + 128]
                a_out[:, pl.ds(low * 256 + k * 128, 128)] = tile[0:256]
                cols = pl.ds(half * 512 + low * 256 + k * 128, 128)
                b_keep[:, cols] = tile[256:384]
                b_send[:, cols] = tile[384:512]


def partner(place, bit):
    zh, y, zl, x, c = place
    if bit[0] == "z":
        if bit == "zl":
            return zh, y, zl ^ 1, x, c
        return gray(gray(zh) ^ "ab".index(bit[1]) + 1), y, zl, x, c
    flip = "ab".index(bit[1]) + 1
    if bit[0] == "x":
        return zh, y, zl, gray(gray(x) ^ flip), c
    return zh, gray(gray(y) ^ flip), zl, x, c


def swapped(value, axis, order):
    sizes = (4, 4, 2, 4, 2)
    places = list(itertools.product(*map(range, sizes)))
    number = {place: i for i, place in enumerate(places)}
    perm = [(i, number[partner(p, axis + order[p[-1]])]) for i, p in enumerate(places)]
    return lax.ppermute(value, ("zh", "y", "zl", "x", "c"), perm)


def local(image, wrow, wcol, w_terms, fro, fco, bo, sro, sc):
    smem = pl.BlockSpec(memory_space=pltpu.SMEM)
    vmem = pl.BlockSpec(memory_space=pltpu.VMEM)
    params = pltpu.CompilerParams(vmem_limit_bytes=24 * 2**20)
    swap = [(0, 1), (1, 0)]
    window = wcol.reshape(1, F)
    other_window = lax.ppermute(window, "c", swap)
    other_image = lax.ppermute(image.astype(f32), "c", swap)
    table = jax.ShapeDtypeStruct((2 * F, F), bf16)
    rt, g_own = pl.pallas_call(
        own_kernel,
        out_shape=(jax.ShapeDtypeStruct((2, F, 2 * F), bf16), jax.ShapeDtypeStruct((F, 2 * F), f32)),
        in_specs=[smem] * 6 + [vmem] * 3,
        out_specs=(vmem, vmem),
        scratch_shapes=[pltpu.VMEM((2 * F, F), bf16)] * 2,
        compiler_params=params,
        cost_estimate=pl.CostEstimate(flops=2**30, bytes_accessed=4 * 2**20, transcendentals=0),
        name="own_facet",
    )(w_terms, fro, fco, bo, sro, sc, image, wrow.reshape(1, F), window)
    w1, w2 = pl.pallas_call(
        other_kernel,
        out_shape=(table, table),
        in_specs=[smem] * 4 + [vmem],
        out_specs=(vmem, vmem),
        compiler_params=params,
        cost_estimate=pl.CostEstimate(flops=2**22, bytes_accessed=2 * 2**20, transcendentals=0),
        name="other_table",
    )(w_terms, fco, bo, sc, other_window)
    shapes = [(256, 512)] * 2 + [(128, 1024)] * 2
    a_keep, a_send, b_keep, b_send = pl.pallas_call(
        sum_kernel,
        out_shape=[jax.ShapeDtypeStruct(s, f32) for s in shapes],
        in_specs=[vmem] * 5,
        out_specs=[vmem] * 4,
        scratch_shapes=[pltpu.VMEM((2, 2 * F, F), bf16), pltpu.VMEM((2, F, F), bf16)],
        compiler_params=params,
        cost_estimate=pl.CostEstimate(flops=2**31, bytes_accessed=9 * 2**20, transcendentals=0),
        name="two_stages",
    )(rt, g_own, w1, w2, other_image)
    a = a_keep + swapped(a_send, "x", "ab")
    b = b_keep + swapped(b_send, "y", "ab")
    a = a[:128] + swapped(a[128:], "y", "ab")
    b = b[:, :512] + swapped(b[:, 512:], "x", "ab")
    whole = jnp.stack([a.reshape(2, 64, 512), b.reshape(2, 64, 512)], axis=1).reshape(256, 512)
    whole = whole[:, :256] + swapped(whole[:, 256:], "x", "ba")
    whole = whole[:128] + swapped(whole[128:], "y", "ba")
    whole = whole.reshape(2, 2, 2, 16, 256)
    whole = whole[:, 0] + swapped(whole[:, 1], "z", "ab")
    whole = whole[:, 0] + swapped(whole[:, 1], "z", "ba")
    whole = whole.reshape(32, 2, 2, 64)
    whole = whole[:, :, 0] + swapped(whole[:, :, 1], "z", "ll")
    return whole.reshape(32, 2, 2, 32).transpose(1, 2, 0, 3)


def solution(mesh):
    torus = Mesh(mesh.devices.reshape(4, 4, 2, 4, 2), ("zh", "y", "zl", "x", "c"))
    placed = (P(None, FROW, FCOL), P(FROW), P(FCOL), P(), P(), P(), P(), P(), P())
    return jax.shard_map(local, mesh=torus, in_specs=placed, out_specs=P(None, None, FROW, FCOL), check_vma=False)
```

time: 87.9 us -> 60.1 us (0.68)
  starting transfers between devices: 59.1 us -> 22.1 us
  waiting for transfers between devices: 18 us -> 27.6 us
    ppermute x35 -> x9, starting transfers between devices: 58.5 us -> 21.6 us  [swapped(): return lax.ppermute(value, ('zh', 'y', 'zl', 'x', 'c'), perm)]
    ppermute x35 -> x9, waiting for transfers between devices: 17.2 us -> 27.2 us  [swapped(): return lax.ppermute(value, ('zh', 'y', 'zl', 'x', 'c'), perm)]
  transfers between devices with their start and end apart: 37 -> 11, of which waited for: 12 -> 9; matrix products, arithmetic and copies ran while one was open for 1% -> 0% of each run, Pallas kernels for 4% -> 7%
where the time goes in v2:
time: 60.1 us; the launch traced here: 59.8 us
  waiting for transfers between devices  27.6 us (46%)
  starting transfers between devices  22.1 us (37%)
  Pallas kernels  6.86 us (11%)
  other arithmetic  1.94 us (3%)
  local copies, waits for them, and re-layouts  1.01 us (2%)
    ppermute x9, waiting for transfers between devices, swapped(): return lax.ppermute(value, ('zh', 'y', 'zl', 'x', 'c'), perm)  27.2 us
    ppermute x9, starting transfers between devices, swapped(): return lax.ppermute(value, ('zh', 'y', 'zl', 'x', 'c'), perm)  21.6 us
    pallas_call x1, Pallas kernels, local(): pl.pallas_call(own_kernel, out_shape=(jax.ShapeDtypeStruct((2, F, 2 * F),...  3.22 us
    pallas_call x1, Pallas kernels, local(): pl.pallas_call(sum_kernel, out_shape=[jax.ShapeDtypeStruct(s, f32) for s...  2.53 us
    convert_element_type x1, other arithmetic, local(): other_image = lax.ppermute(image.astype(f32), 'c', swap)  1.58 us
  transfers between devices with their start and end apart: 11, of which 9 were waited for; matrix products, arithmetic and copies ran while one was open for 0% of the time, Pallas kernels for 7%

profile of v2, /device:TPU:32, one launch (start us, length us, event | category | flops | bytes accessed | tf_op | source)
XLA Modules:
  0.0 59.8 jit_solution(6329256349822688005)
XLA Ops:
  0.0 0.0 copy-start
  0.0 0.0 copy-start.7
  0.0 0.0 copy-start.6
  0.0 0.0 copy-start.5
  0.0 0.0 copy-start.4
  0.0 0.0 copy-start.3
  0.1 0.0 copy-start.1
  0.1 1.6 %convert_element_type.3 = f32[2,512,512]{2,1,0:T(8,128)S(1)} convert(bf16[2,512,512]{2,1,0:T(8,128)(2,1)} %image.1) | non-fusion elementwise | flops 524288 | bytes 3145728 | tf_op jit(solution)/shard_map/convert_element_type | solution.py:200
  1.7 0.1 collective-permute-start.1
  1.8 0.0 copy-done.2
  1.8 0.5 collective-permute-start
  2.3 0.0 copy-done
  2.3 0.0 copy-done.8
  2.3 0.0 copy-done.7
  2.3 0.0 copy-done.6
  2.3 0.0 copy-done.5
  2.3 0.0 copy-done.4
  2.3 0.0 copy-done.3
  2.3 0.0 copy-done.1
  2.3 3.2 %own_facet.1 = (bf16[2,512,1024]{2,1,0:T(8,128)(2,1)S(1)}, f32[512,1024]{1,0:T(8,128)S(1)}) custom-call(f32[2]{0:T(128)S(1)} %copy-done.5, s32[16]{0:T(128)S(1)} %copy-done.3, s32[16]{0:T(128)S(1)} %copy-done.6, s32[2]{0:T(128)S(1)} %copy-done.7, s32[2]{0:T(128)S(1)} %copy-done.4, s32[2]{0:T(128)S(1)} %copy-done.8, bf16[2,512,512]{2,1,0:T(8,128)(2,1)S(1)} %copy-done, ...), custom_call_target="tpu_custom_call" | custom-call | flops 1073741824 | bytes 4194304 | tf_op jit(solution)/shard_map/own_facet/pallas_call | solution.py:202
  5.5 0.4 collective-permute-done.wcol
  5.9 1.1 %other_table.1 = (bf16[1024,512]{1,0:T(8,128)(2,1)S(1)}, bf16[1024,512]{1,0:T(8,128)(2,1)S(1)}) custom-call(f32[2]{0:T(128)S(1)} %copy-done.5, s32[16]{0:T(128)S(1)} %copy-done.6, s32[2]{0:T(128)S(1)} %copy-done.7, s32[2]{0:T(128)S(1)} %copy-done.8, f32[1,512]{1,0:T(1,128)S(1)} %collective-permute-done.wcol), custom_call_target="tpu_custom_call" | custom-call | flops 4194304 | bytes 2097152 | tf_op jit(solution)/shard_map/other_table/pallas_call | solution.py:212
  7.0 0.0 collective-permute-done.1.image
  7.0 2.5 %two_stages.1 = (f32[256,512]{1,0:T(8,128)S(1)}, f32[256,512]{1,0:T(8,128)S(1)}, f32[128,1024]{1,0:T(8,128)S(1)}, f32[128,1024]{1,0:T(8,128)S(1)}) custom-call(bf16[2,512,1024]{2,1,0:T(8,128)(2,1)S(1)} %get-tuple-element.13.rt, f32[512,1024]{1,0:T(8,128)S(1)} %get-tuple-element.14.g_own, bf16[1024,512]{1,0:T(8,128)(2,1)S(1)} %get-tuple-element.15.w1, ...), custom_call_target="tpu_custom_call" | custom-call | flops 2147483648 | bytes 9437184 | tf_op jit(solution)/shard_map/two_stages/pallas_call | solution.py:222
  9.6 1.6 %collective-permute-start.2 = (f32[256,512]{1,0:T(8,128)S(1)}, f32[256,512]{1,0:T(8,128)S(1)}, u32[]{:S(2)}, u32[]{:S(2)}) collective-permute-start(f32[256,512]{1,0:T(8,128)S(1)} %get-tuple-element.18), channel_id=1, source_target_pairs={{0,2},{1,7},{2,0},{3,5},{4,6},{5,3},{6,4},{7,1},{8,10},{9,15},{10,... | collective-permute-start | bytes 1572872 | tf_op jit(solution)/shard_map/ppermute | solution.py:190
  11.1 1.6 %collective-permute-start.4 = (f32[128,1024]{1,0:T(8,128)S(1)}, f32[128,1024]{1,0:T(8,128)S(1)}, u32[]{:S(2)}, u32[]{:S(2)}) collective-permute-start(f32[128,1024]{1,0:T(8,128)S(1)} %get-tuple-element.20), channel_id=1, source_target_pairs={{0,16},{1,49},{2,18},{3,51},{4,20},{5,53},{6,22},{7,55},{8,24},{9,... | collective-permute-start | bytes 1572872 | tf_op jit(solution)/shard_map/ppermute | solution.py:190
  12.7 6.1 %collective-permute-done.2 = f32[256,512]{1,0:T(8,128)S(1)} collective-permute-done((f32[256,512]{1,0:T(8,128)S(1)}, f32[256,512]{1,0:T(8,128)S(1)}, u32[]{:S(2)}, u32[]{:S(2)}) %collective-permute-start.2) | collective-permute-done | bytes 524320 | tf_op jit(solution)/shard_map/ppermute | solution.py:190
  18.8 0.1 add.27
  18.9 1.7 %collective-permute-start.3 = (f32[128,512]{1,0:T(8,128)S(1)}, f32[128,512]{1,0:T(8,128)S(1)}, u32[]{:S(2)}, u32[]{:S(2)}) collective-permute-start(f32[128,512]{1,0:T(8,128)S(1)} %slice.57), channel_id=1, source_target_pairs={{0,16},{1,49},{2,18},{3,51},{4,20},{5,53},{6,22},{7,55},{8,24},{9,... | collective-permute-start | bytes 786440 | tf_op jit(solution)/shard_map/ppermute | solution.py:190
  20.6 0.0 collective-permute-done.4
  20.6 0.1 add.29
  20.7 1.6 %collective-permute-start.5 = (f32[128,512]{1,0:T(8,128)S(1)}, f32[128,512]{1,0:T(8,128)S(1)}, u32[]{:S(2)}, u32[]{:S(2)}) collective-permute-start(f32[128,512]{1,0:T(8,128)S(1)} %slice.59), channel_id=1, source_target_pairs={{0,2},{1,7},{2,0},{3,5},{4,6},{5,3},{6,4},{7,1},{8,10},{9,15},{10,... | collective-permute-start | bytes 786440 | tf_op jit(solution)/shard_map/ppermute | solution.py:190
  22.3 3.1 %collective-permute-done.3 = f32[128,512]{1,0:T(8,128)S(1)} collective-permute-done((f32[128,512]{1,0:T(8,128)S(1)}, f32[128,512]{1,0:T(8,128)S(1)}, u32[]{:S(2)}, u32[]{:S(2)}) %collective-permute-start.3) | collective-permute-done | bytes 262176 | tf_op jit(solution)/shard_map/ppermute | solution.py:190
  25.4 1.7 %collective-permute-done.5 = f32[128,512]{1,0:T(8,128)S(1)} collective-permute-done((f32[128,512]{1,0:T(8,128)S(1)}, f32[128,512]{1,0:T(8,128)S(1)}, u32[]{:S(2)}, u32[]{:S(2)}) %collective-permute-start.5) | collective-permute-done | bytes 262176 | tf_op jit(solution)/shard_map/ppermute | solution.py:190
  27.3 2.8 %collective-permute-start.6 = (f32[256,256]{1,0:T(8,128)S(1)}, f32[256,256]{1,0:T(8,128)S(1)}, u32[]{:S(2)}, u32[]{:S(2)}) collective-permute-start(f32[256,256]{1,0:T(8,128)S(1)} %slice.61), channel_id=1, source_target_pairs={{0,6},{1,3},{2,4},{3,1},{4,2},{5,7},{6,0},{7,5},{8,14},{9,11},{10,... | collective-permute-start | bytes 786440 | tf_op jit(solution)/shard_map/ppermute | solution.py:190
  30.1 4.8 %collective-permute-done.6 = f32[256,256]{1,0:T(8,128)S(1)} collective-permute-done((f32[256,256]{1,0:T(8,128)S(1)}, f32[256,256]{1,0:T(8,128)S(1)}, u32[]{:S(2)}, u32[]{:S(2)}) %collective-permute-start.6) | collective-permute-done | bytes 262176 | tf_op jit(solution)/shard_map/ppermute | solution.py:190
  35.0 2.8 %collective-permute-start.7 = (f32[128,256]{1,0:T(8,128)S(1)}, f32[128,256]{1,0:T(8,128)S(1)}, u32[]{:S(2)}, u32[]{:S(2)}) collective-permute-start(f32[128,256]{1,0:T(8,128)S(1)} %slice.63), channel_id=1, source_target_pairs={{0,48},{1,17},{2,50},{3,19},{4,52},{5,21},{6,54},{7,23},{8,56},{9,... | collective-permute-start | bytes 393224 | tf_op jit(solution)/shard_map/ppermute | solution.py:190
  37.8 3.5 %collective-permute-done.7 = f32[128,256]{1,0:T(8,128)S(1)} collective-permute-done((f32[128,256]{1,0:T(8,128)S(1)}, f32[128,256]{1,0:T(8,128)S(1)}, u32[]{:S(2)}, u32[]{:S(2)}) %collective-permute-start.7) | collective-permute-done | bytes 131104 | tf_op jit(solution)/shard_map/ppermute | solution.py:190
  41.3 3.4 %collective-permute-start.8 = (f32[2,2,16,256]{3,2,0,1:T(8,128)S(1)}, f32[2,2,16,256]{3,2,0,1:T(8,128)S(1)}, u32[]{:S(2)}, u32[]{:S(2)}) collective-permute-start(f32[2,2,16,256]{3,2,0,1:T(8,128)S(1)} %bitcast.40), channel_id=1, source_target_pairs={{0,64},{1,193},{2,66},{3,195},{4,68},{5,197},{6,70},{7,199},{8,72}... | collective-permute-start | bytes 196616 | tf_op jit(solution)/shard_map/ppermute | solution.py:190
  44.7 2.2 %collective-permute-done.8 = f32[2,2,16,256]{3,2,0,1:T(8,128)S(1)} collective-permute-done((f32[2,2,16,256]{3,2,0,1:T(8,128)S(1)}, f32[2,2,16,256]{3,2,0,1:T(8,128)S(1)}, u32[]{:S(2)}, u32[]{:S(2)}) %collective-permute-start.8) | collective-permute-done | bytes 65568 | tf_op jit(solution)/shard_map/ppermute | solution.py:190
  47.0 5.8 %collective-permute-start.9 = (f32[2,16,256]{2,1,0:T(8,128)S(1)}, f32[2,16,256]{2,1,0:T(8,128)S(1)}, u32[]{:S(2)}, u32[]{:S(2)}) collective-permute-start(f32[2,16,256]{2,1,0:T(8,128)S(1)} %slice_bitcast_fusion), channel_id=1, source_target_pairs={{0,192},{1,65},{2,194},{3,67},{4,196},{5,69},{6,198},{7,71},{8,200... | collective-permute-start | bytes 98312 | tf_op jit(solution)/shard_map/ppermute | solution.py:190
  52.8 2.1 %collective-permute-done.9 = f32[2,16,256]{2,1,0:T(8,128)S(1)} collective-permute-done((f32[2,16,256]{2,1,0:T(8,128)S(1)}, f32[2,16,256]{2,1,0:T(8,128)S(1)}, u32[]{:S(2)}, u32[]{:S(2)}) %collective-permute-start.9) | collective-permute-done | bytes 32800 | tf_op jit(solution)/shard_map/ppermute | solution.py:190
  54.9 0.1 reshape.22
  55.0 0.1 fusion.3
  55.1 0.3 collective-permute-start.10
  55.4 3.7 %collective-permute-done.10 = f32[32,2,64]{2,1,0:T(2,128)S(1)} collective-permute-done((f32[32,2,64]{2,1,0:T(2,128)S(1)}, f32[32,2,64]{2,1,0:T(2,128)S(1)}, u32[]{:S(2)}, u32[]{:S(2)}) %collective-permute-start.10) | collective-permute-done | bytes 16416 | tf_op jit(solution)/shard_map/ppermute | solution.py:190
  59.1 0.1 reshape.23
  59.2 0.6 %copy.24 = f32[2,2,32,32]{3,2,1,0:T(8,128)} copy(f32[2,2,32,32]{3,1,2,0:T(2,128)S(1)} %bitcast.38) | data formatting | bytes 32768 | tf_op jit(solution)/shard_map/transpose | solution.py:244
  (18 shorter events, 0.3 us)
Async XLA Ops:
  0.0 2.3 %copy-start = (bf16[2,512,512]{2,1,0:T(8,128)(2,1)S(1)}, bf16[2,512,512]{2,1,0:T(8,128)(2,1)}, u32[]{:S(2)}) copy-start(bf16[2,512,512]{2,1,0:T(8,128)(2,1)} %image.1) | copy-start | bytes 3145732
  0.0 1.8 %copy-start.2 = (f32[512]{0:T(512)S(1)}, f32[512]{0:T(512)}, u32[]{:S(2)}) copy-start(f32[512]{0:T(512)} %param.11) | copy-start | bytes 6148
  0.0 2.3 %copy-start.8 = (s32[2]{0:T(128)S(1)}, s32[2]{0:T(128)}, u32[]{:S(2)}) copy-start(s32[2]{0:T(128)} %sc.3) | copy-start | bytes 28
  0.0 2.3 %copy-start.7 = (s32[2]{0:T(128)S(1)}, s32[2]{0:T(128)}, u32[]{:S(2)}) copy-start(s32[2]{0:T(128)} %bo.3) | copy-start | bytes 28
  0.0 2.2 %copy-start.6 = (s32[16]{0:T(128)S(1)}, s32[16]{0:T(128)}, u32[]{:S(2)}) copy-start(s32[16]{0:T(128)} %fco.3) | copy-start | bytes 196
  0.0 2.2 %copy-start.5 = (f32[2]{0:T(128)S(1)}, f32[2]{0:T(128)}, u32[]{:S(2)}) copy-start(f32[2]{0:T(128)} %w_terms.3) | copy-start | bytes 28
  0.0 2.2 %copy-start.4 = (s32[2]{0:T(128)S(1)}, s32[2]{0:T(128)}, u32[]{:S(2)}) copy-start(s32[2]{0:T(128)} %sro.1) | copy-start | bytes 28
  0.0 2.2 %copy-start.3 = (s32[16]{0:T(128)S(1)}, s32[16]{0:T(128)}, u32[]{:S(2)}) copy-start(s32[16]{0:T(128)} %fro.1) | copy-start | bytes 196
  0.1 2.2 %copy-start.1 = (f32[512]{0:T(512)S(1)}, f32[512]{0:T(512)}, u32[]{:S(2)}) copy-start(f32[512]{0:T(512)} %param.10) | copy-start | bytes 6148
  1.7 5.4 %collective-permute-start.1 = (f32[2,512,512]{2,1,0:T(8,128)S(1)}, f32[2,512,512]{2,1,0:T(8,128)S(1)}, u32[]{:S(2)}, u32[]{:S(2)}) collective-permute-start(f32[2,512,512]{2,1,0:T(8,128)S(1)} %convert_element_type.3), channel_id=1, source_target_pairs={{0,1},{1,0},{2,3},{3,2},{4,5},{5,4},{6,7},{7,6},{8,9},{9,8},{10,11... | collective-permute-start | bytes 6291464 | tf_op jit(solution)/shard_map/ppermute | solution.py:200
  1.8 4.1 %collective-permute-start = (f32[1,512]{1,0:T(1,128)S(1)}, f32[1,512]{1,0:T(1,128)S(1)}, u32[]{:S(2)}, u32[]{:S(2)}) collective-permute-start(f32[1,512]{1,0:T(1,128)S(1)} %bitcast.31), channel_id=1, source_target_pairs={{0,1},{1,0},{2,3},{3,2},{4,5},{5,4},{6,7},{7,6},{8,9},{9,8},{10,11... | collective-permute-start | bytes 6152 | tf_op jit(solution)/shard_map/ppermute | solution.py:199
  9.6 9.3 %collective-permute-start.2 = (f32[256,512]{1,0:T(8,128)S(1)}, f32[256,512]{1,0:T(8,128)S(1)}, u32[]{:S(2)}, u32[]{:S(2)}) collective-permute-start(f32[256,512]{1,0:T(8,128)S(1)} %get-tuple-element.18), channel_id=1, source_target_pairs={{0,2},{1,7},{2,0},{3,5},{4,6},{5,3},{6,4},{7,1},{8,10},{9,15},{10,... | collective-permute-start | bytes 1572872 | tf_op jit(solution)/shard_map/ppermute | solution.py:190
  11.1 9.5 %collective-permute-start.4 = (f32[128,1024]{1,0:T(8,128)S(1)}, f32[128,1024]{1,0:T(8,128)S(1)}, u32[]{:S(2)}, u32[]{:S(2)}) collective-permute-start(f32[128,1024]{1,0:T(8,128)S(1)} %get-tuple-element.20), channel_id=1, source_target_pairs={{0,16},{1,49},{2,18},{3,51},{4,20},{5,53},{6,22},{7,55},{8,24},{9,... | collective-permute-start | bytes 1572872 | tf_op jit(solution)/shard_map/ppermute | solution.py:190
  18.9 6.5 %collective-permute-start.3 = (f32[128,512]{1,0:T(8,128)S(1)}, f32[128,512]{1,0:T(8,128)S(1)}, u32[]{:S(2)}, u32[]{:S(2)}) collective-permute-start(f32[128,512]{1,0:T(8,128)S(1)} %slice.57), channel_id=1, source_target_pairs={{0,16},{1,49},{2,18},{3,51},{4,20},{5,53},{6,22},{7,55},{8,24},{9,... | collective-permute-start | bytes 786440 | tf_op jit(solution)/shard_map/ppermute | solution.py:190
  20.7 6.5 %collective-permute-start.5 = (f32[128,512]{1,0:T(8,128)S(1)}, f32[128,512]{1,0:T(8,128)S(1)}, u32[]{:S(2)}, u32[]{:S(2)}) collective-permute-start(f32[128,512]{1,0:T(8,128)S(1)} %slice.59), channel_id=1, source_target_pairs={{0,2},{1,7},{2,0},{3,5},{4,6},{5,3},{6,4},{7,1},{8,10},{9,15},{10,... | collective-permute-start | bytes 786440 | tf_op jit(solution)/shard_map/ppermute | solution.py:190
  27.3 7.7 %collective-permute-start.6 = (f32[256,256]{1,0:T(8,128)S(1)}, f32[256,256]{1,0:T(8,128)S(1)}, u32[]{:S(2)}, u32[]{:S(2)}) collective-permute-start(f32[256,256]{1,0:T(8,128)S(1)} %slice.61), channel_id=1, source_target_pairs={{0,6},{1,3},{2,4},{3,1},{4,2},{5,7},{6,0},{7,5},{8,14},{9,11},{10,... | collective-permute-start | bytes 786440 | tf_op jit(solution)/shard_map/ppermute | solution.py:190
  35.0 6.3 %collective-permute-start.7 = (f32[128,256]{1,0:T(8,128)S(1)}, f32[128,256]{1,0:T(8,128)S(1)}, u32[]{:S(2)}, u32[]{:S(2)}) collective-permute-start(f32[128,256]{1,0:T(8,128)S(1)} %slice.63), channel_id=1, source_target_pairs={{0,48},{1,17},{2,50},{3,19},{4,52},{5,21},{6,54},{7,23},{8,56},{9,... | collective-permute-start | bytes 393224 | tf_op jit(solution)/shard_map/ppermute | solution.py:190
  41.3 5.6 %collective-permute-start.8 = (f32[2,2,16,256]{3,2,0,1:T(8,128)S(1)}, f32[2,2,16,256]{3,2,0,1:T(8,128)S(1)}, u32[]{:S(2)}, u32[]{:S(2)}) collective-permute-start(f32[2,2,16,256]{3,2,0,1:T(8,128)S(1)} %bitcast.40), channel_id=1, source_target_pairs={{0,64},{1,193},{2,66},{3,195},{4,68},{5,197},{6,70},{7,199},{8,72}... | collective-permute-start | bytes 196616 | tf_op jit(solution)/shard_map/ppermute | solution.py:190
  47.0 7.9 %collective-permute-start.9 = (f32[2,16,256]{2,1,0:T(8,128)S(1)}, f32[2,16,256]{2,1,0:T(8,128)S(1)}, u32[]{:S(2)}, u32[]{:S(2)}) collective-permute-start(f32[2,16,256]{2,1,0:T(8,128)S(1)} %slice_bitcast_fusion), channel_id=1, source_target_pairs={{0,192},{1,65},{2,194},{3,67},{4,196},{5,69},{6,198},{7,71},{8,200... | collective-permute-start | bytes 98312 | tf_op jit(solution)/shard_map/ppermute | solution.py:190
  55.1 4.0 %collective-permute-start.10 = (f32[32,2,64]{2,1,0:T(2,128)S(1)}, f32[32,2,64]{2,1,0:T(2,128)S(1)}, u32[]{:S(2)}, u32[]{:S(2)}) collective-permute-start(f32[32,2,64]{2,1,0:T(2,128)S(1)} %bitcast.41), channel_id=1, source_target_pairs={{0,8},{1,9},{2,10},{3,11},{4,12},{5,13},{6,14},{7,15},{8,0},{9,1},... | collective-permute-start | bytes 49160 | tf_op jit(solution)/shard_map/ppermute | solution.py:190

commit v3 on v2

--- a/solution.py
+++ b/solution.py
@@ -87,7 +87,7 @@
     i = lax.broadcasted_iota(jnp.int32, (16, F), 0)
     x = near(at["x"], i >> 3, (i >> 2) & 1, at["c"])
     sub = (i >> 1) & 1
-    zl = at["zl"] ^ (i & 1)
+    zl = i & 1
     band = per_sub(sub, [bo[sc[k]] for k in range(2)])
     coarse = turn(phase_index(g, band + ((zl * 4 + x) * 2 + at["c"]) * 32))
     waves = [chirp(w_terms[sc[k]], g) for k in range(2)]
@@ -125,14 +125,13 @@
     window = wrow[...] * (1.0 / 8192.0)
     fine = turn((g * lax.broadcasted_iota(jnp.int32, (32, F), 0)) & (IMAGE - 1))
     y = near(at["y"], i >> 3, (i >> 2) & 1, at["c"])
-    zh = near(at["zh"], (i >> 1) & 1, i & 1, at["c"])
+    zh = i & 3
     for k in range(2):
         wave = [v * window for v in chirp(w_terms[sc[k]], g)]
         coarse = times(turn(phase_index(g, sro[k] + (zh * 4 + y) * 32)), wave)
-        for part in range(2):
-            re, im = outer(coarse, [v[part * 16 : part * 16 + 16] for v in fine])
-            rt[k, pl.ds(part * 256, 256), pl.ds(0, F)] = re.astype(bf16)
-            rt[k, pl.ds(part * 256, 256), pl.ds(F, F)] = im.astype(bf16)
+        re, im = outer(coarse, fine)
+        rt[k, :, pl.ds(0, F)] = re.astype(bf16)
+        rt[k, :, pl.ds(F, F)] = im.astype(bf16)
 
 
 def other_kernel(w_terms, fco, bo, sc, wcol, w1, w2):
@@ -144,7 +143,7 @@
         w1[rows, :], w2[rows, :] = column_table(factors, t)
 
 
-def sum_kernel(rt, g_own, w1, w2, image, a_keep, a_send, b_keep, b_send, gg, im):
+def sum_kernel(rt, g_own, w1, w2, image, keep, to_x, to_y, to_xy, gg, im):
     im[0] = image[0].astype(bf16)
     im[1] = image[1].astype(bf16)
     imag = (lax.broadcasted_iota(jnp.int32, (F, 128), 1) & 32) == 32
@@ -161,33 +160,86 @@
     for k in range(2):
         for half in range(2):
             s = lax.dot_general(rt[k], gg[k, :, pl.ds(half * 256, 256)], NN, preferred_element_type=f32)
-            a_out = a_send if half else a_keep
             for low in range(2):
                 tile = s[:, low * 128 : low * 128 + 128]
-                a_out[:, pl.ds(low * 256 + k * 128, 128)] = tile[0:256]
-                cols = pl.ds(half * 512 + low * 256 + k * 128, 128)
-                b_keep[:, cols] = tile[256:384]
-                b_send[:, cols] = tile[384:512]
-
-
-def partner(place, bit):
-    zh, y, zl, x, c = place
-    if bit[0] == "z":
-        if bit == "zl":
-            return zh, y, zl ^ 1, x, c
-        return gray(gray(zh) ^ "ab".index(bit[1]) + 1), y, zl, x, c
-    flip = "ab".index(bit[1]) + 1
-    if bit[0] == "x":
-        return zh, y, zl, gray(gray(x) ^ flip), c
-    return zh, gray(gray(y) ^ flip), zl, x, c
-
-
-def swapped(value, axis, order):
-    sizes = (4, 4, 2, 4, 2)
-    places = list(itertools.product(*map(range, sizes)))
+                cols = pl.ds(low * 256 + k * 128, 128)
+                (to_x if half else keep)[:, cols] = tile[:256]
+                (to_xy if half else to_y)[:, cols] = tile[256:]
+
+
+def swapped(value, axes, second):
+    places = list(itertools.product(*map(range, (4, 4, 2, 4, 2))))
     number = {place: i for i, place in enumerate(places)}
-    perm = [(i, number[partner(p, axis + order[p[-1]])]) for i, p in enumerate(places)]
+    perm = []
+    for i, (zh, y, zl, x, c) in enumerate(places):
+        flip = 1 + (c ^ second)
+        if "x" in axes:
+            x = gray(gray(x) ^ flip)
+        if "y" in axes:
+            y = gray(gray(y) ^ flip)
+        perm.append((i, number[zh, y, zl, x, c]))
     return lax.ppermute(value, ("zh", "y", "zl", "x", "c"), perm)
+
+
+def arrived(pieces, second):
+    return [pieces[0]] + [swapped(v, axes, second) for v, axes in zip(pieces[1:], ("x", "y", "xy"))]
+
+
+def cut_kernel(own, by_x, by_y, by_xy, keep, to_x, to_y, to_xy):
+    for y in range(2):
+        for x in range(2):
+            rows, cols = pl.ds(y * 128, 128), pl.ds(x * 256, 256)
+            total = (own[rows, cols] + by_x[rows, cols]) + (by_y[rows, cols] + by_xy[rows, cols])
+            ((keep, to_x), (to_y, to_xy))[y][x][...] = total
+
+
+def pack_kernel(own, by_x, by_y, by_xy, out):
+    low = lax.broadcasted_iota(jnp.int32, (128, 128), 1) < 64
+    total = (own[...] + by_x[...]) + (by_y[...] + by_xy[...])
+    one, two = total[:, :128], total[:, 128:]
+    left = jnp.where(low, one, pltpu.roll(two, 64, 1))
+    right = jnp.where(low, pltpu.roll(one, 64, 1), two)
+    for zh in range(4):
+        rows = slice(zh * 32, zh * 32 + 32)
+        out[2 * zh] = left[rows]
+        out[2 * zh + 1] = right[rows]
+
+
+def last_kernel(pieces, out):
+    total = jnp.sum(pieces[...], axis=0)
+    for k in range(2):
+        for c in range(2):
+            out[k, c] = total[:, (2 * k + c) * 32 : (2 * k + c) * 32 + 32]
+
+
+def spread(pieces):
+    vmem = pl.BlockSpec(memory_space=pltpu.VMEM)
+    params = pltpu.CompilerParams(vmem_limit_bytes=8 * 2**20)
+    pieces = pl.pallas_call(
+        cut_kernel,
+        out_shape=[jax.ShapeDtypeStruct((128, 256), f32)] * 4,
+        in_specs=[vmem] * 4,
+        out_specs=[vmem] * 4,
+        compiler_params=params,
+        name="cut",
+    )(*arrived(pieces, 0))
+    packed = pl.pallas_call(
+        pack_kernel,
+        out_shape=jax.ShapeDtypeStruct((8, 32, 128), f32),
+        in_specs=[vmem] * 4,
+        out_specs=vmem,
+        compiler_params=params,
+        name="pack",
+    )(*arrived(pieces, 1))
+    blocks = lax.all_to_all(packed, ("zh", "zl"), 0, 0, tiled=True)
+    return pl.pallas_call(
+        last_kernel,
+        out_shape=jax.ShapeDtypeStruct((2, 2, 32, 32), f32),
+        in_specs=[vmem],
+        out_specs=vmem,
+        compiler_params=params,
+        name="last_sum",
+    )(blocks)
 
 
 def local(image, wrow, wcol, w_terms, fro, fco, bo, sro, sc):
@@ -218,10 +270,9 @@
         cost_estimate=pl.CostEstimate(flops=2**22, bytes_accessed=2 * 2**20, transcendentals=0),
         name="other_table",
     )(w_terms, fco, bo, sc, other_window)
-    shapes = [(256, 512)] * 2 + [(128, 1024)] * 2
-    a_keep, a_send, b_keep, b_send = pl.pallas_call(
+    pieces = pl.pallas_call(
         sum_kernel,
-        out_shape=[jax.ShapeDtypeStruct(s, f32) for s in shapes],
+        out_shape=[jax.ShapeDtypeStruct((256, 512), f32)] * 4,
         in_specs=[vmem] * 5,
         out_specs=[vmem] * 4,
         scratch_shapes=[pltpu.VMEM((2, 2 * F, F), bf16), pltpu.VMEM((2, F, F), bf16)],
@@ -229,19 +280,7 @@
         cost_estimate=pl.CostEstimate(flops=2**31, bytes_accessed=9 * 2**20, transcendentals=0),
         name="two_stages",
     )(rt, g_own, w1, w2, other_image)
-    a = a_keep + swapped(a_send, "x", "ab")
-    b = b_keep + swapped(b_send, "y", "ab")
-    a = a[:128] + swapped(a[128:], "y", "ab")
-    b = b[:, :512] + swapped(b[:, 512:], "x", "ab")
-    whole = jnp.stack([a.reshape(2, 64, 512), b.reshape(2, 64, 512)], axis=1).reshape(256, 512)
-    whole = whole[:, :256] + swapped(whole[:, 256:], "x", "ba")
-    whole = whole[:128] + swapped(whole[128:], "y", "ba")
-    whole = whole.reshape(2, 2, 2, 16, 256)
-    whole = whole[:, 0] + swapped(whole[:, 1], "z", "ab")
-    whole = whole[:, 0] + swapped(whole[:, 1], "z", "ba")
-    whole = whole.reshape(32, 2, 2, 64)
-    whole = whole[:, :, 0] + swapped(whole[:, :, 1], "z", "ll")
-    return whole.reshape(32, 2, 2, 32).transpose(1, 2, 0, 3)
+    return spread(pieces)
 
 
 def solution(mesh):

time: 60.1 us -> 56.5 us (0.940)
  blocking collectives: 0 us -> 16 us
  starting transfers between devices: 22.1 us -> 10.2 us
  waiting for transfers between devices: 27.6 us -> 20.5 us
  Pallas kernels: 6.86 us -> 7.96 us
  local copies, waits for them, and re-layouts: 1.01 us -> 0.04 us
    all_to_all x0 -> x1, blocking collectives: none -> 16 us  [spread(): blocks = lax.all_to_all(packed, ('zh', 'zl'), 0, 0, tiled=True)]
    ppermute x9 -> x6, starting transfers between devices: 21.6 us -> 9.57 us  [swapped(): return lax.ppermute(value, ('zh', 'y', 'zl', 'x', 'c'), perm)]
    ppermute x9 -> x6, waiting for transfers between devices: 27.2 us -> 20.3 us  [swapped(): return lax.ppermute(value, ('zh', 'y', 'zl', 'x', 'c'), perm)]
    pallas_call x1 -> x4, Pallas kernels: 2.53 us -> 3.47 us  [the longest x1 2.53 us: local(): pl.pallas_call(sum_kernel, out_shape=[jax.ShapeDtypeStruct((256, 512), f3...]
    transpose x1 -> x0, local copies, waits for them, and re-layouts: 0.63 us -> none  [local(): return whole.reshape(32, 2, 2, 32).transpose(1, 2, 0, 3)]
  transfers between devices with their start and end apart: 11 -> 8, of which waited for: 9 -> 6; matrix products, arithmetic and copies ran while one was open for 0% -> 0% of each run, Pallas kernels for 7% -> 8%
where the time goes in v3:
time: 56.5 us; the launch traced here: 56.4 us
  waiting for transfers between devices  20.5 us (36%)
  blocking collectives  16 us (28%)
  starting transfers between devices  10.2 us (18%)
  Pallas kernels  7.96 us (14%)
  other arithmetic  1.58 us (3%)
    ppermute x6, waiting for transfers between devices, swapped(): return lax.ppermute(value, ('zh', 'y', 'zl', 'x', 'c'), perm)  20.3 us
    all_to_all x1, blocking collectives, spread(): blocks = lax.all_to_all(packed, ('zh', 'zl'), 0, 0, tiled=True)  16 us
    ppermute x6, starting transfers between devices, swapped(): return lax.ppermute(value, ('zh', 'y', 'zl', 'x', 'c'), perm)  9.57 us
    pallas_call x1, Pallas kernels, local(): pl.pallas_call(own_kernel, out_shape=(jax.ShapeDtypeStruct((2, F, 2 * F),...  3.37 us
    pallas_call x1, Pallas kernels, local(): pl.pallas_call(sum_kernel, out_shape=[jax.ShapeDtypeStruct((256, 512), f3...  2.53 us
    convert_element_type x1, other arithmetic, local(): other_image = lax.ppermute(image.astype(f32), 'c', swap)  1.58 us
  transfers between devices with their start and end apart: 8, of which 6 were waited for; matrix products, arithmetic and copies ran while one was open for 0% of the time, Pallas kernels for 8%

profile of v3, /device:TPU:32, one launch (start us, length us, event | category | flops | bytes accessed | tf_op | source)
XLA Modules:
  0.0 56.4 jit_solution(16632524716197080580)
XLA Ops:
  0.0 0.0 copy-start
  0.0 0.0 copy-start.2
  0.0 0.0 copy-start.8
  0.0 0.0 copy-start.7
  0.0 0.0 copy-start.6
  0.0 0.0 copy-start.5
  0.0 0.0 copy-start.4
  0.0 0.0 copy-start.3
  0.1 0.0 copy-start.1
  0.1 1.6 %convert_element_type.3 = f32[2,512,512]{2,1,0:T(8,128)S(1)} convert(bf16[2,512,512]{2,1,0:T(8,128)(2,1)} %image.1) | non-fusion elementwise | flops 524288 | bytes 3145728 | tf_op jit(solution)/shard_map/convert_element_type | solution.py:252
  1.7 0.1 collective-permute-start.1
  1.8 0.0 copy-done.2
  1.8 0.5 collective-permute-start
  2.3 0.0 copy-done
  2.3 0.0 copy-done.8
  2.3 0.0 copy-done.7
  2.3 0.0 copy-done.6
  2.3 0.0 copy-done.5
  2.3 0.0 copy-done.4
  2.3 0.0 copy-done.3
  2.3 0.0 copy-done.1
  2.3 3.4 %own_facet.1 = (bf16[2,512,1024]{2,1,0:T(8,128)(2,1)S(1)}, f32[512,1024]{1,0:T(8,128)S(1)}) custom-call(f32[2]{0:T(128)S(1)} %copy-done.5, s32[16]{0:T(128)S(1)} %copy-done.3, s32[16]{0:T(128)S(1)} %copy-done.6, s32[2]{0:T(128)S(1)} %copy-done.7, s32[2]{0:T(128)S(1)} %copy-done.4, s32[2]{0:T(128)S(1)} %copy-done.8, bf16[2,512,512]{2,1,0:T(8,128)(2,1)S(1)} %copy-done, ...), custom_call_target="tpu_custom_call" | custom-call | flops 1073741824 | bytes 4194304 | tf_op jit(solution)/shard_map/own_facet/pallas_call | solution.py:254
  5.7 0.2 collective-permute-done.wcol
  5.9 1.1 %other_table.1 = (bf16[1024,512]{1,0:T(8,128)(2,1)S(1)}, bf16[1024,512]{1,0:T(8,128)(2,1)S(1)}) custom-call(f32[2]{0:T(128)S(1)} %copy-done.5, s32[16]{0:T(128)S(1)} %copy-done.6, s32[2]{0:T(128)S(1)} %copy-done.7, s32[2]{0:T(128)S(1)} %copy-done.8, f32[1,512]{1,0:T(1,128)S(1)} %collective-permute-done.wcol), custom_call_target="tpu_custom_call" | custom-call | flops 4194304 | bytes 2097152 | tf_op jit(solution)/shard_map/other_table/pallas_call | solution.py:264
  7.0 0.0 collective-permute-done.1.image
  7.0 2.5 %two_stages.1 = (f32[256,512]{1,0:T(8,128)S(1)}, f32[256,512]{1,0:T(8,128)S(1)}, f32[256,512]{1,0:T(8,128)S(1)}, f32[256,512]{1,0:T(8,128)S(1)}) custom-call(bf16[2,512,1024]{2,1,0:T(8,128)(2,1)S(1)} %get-tuple-element.17.rt, f32[512,1024]{1,0:T(8,128)S(1)} %get-tuple-element.18.g_own, bf16[1024,512]{1,0:T(8,128)(2,1)S(1)} %get-tuple-element.19.w1, ...), custom_call_target="tpu_custom_call" | custom-call | flops 2147483648 | bytes 9437184 | tf_op jit(solution)/shard_map/two_stages/pallas_call | solution.py:273
  9.6 1.6 %collective-permute-start.2 = (f32[256,512]{1,0:T(8,128)S(1)}, f32[256,512]{1,0:T(8,128)S(1)}, u32[]{:S(2)}, u32[]{:S(2)}) collective-permute-start(f32[256,512]{1,0:T(8,128)S(1)} %get-tuple-element.22), channel_id=1, source_target_pairs={{0,2},{1,7},{2,0},{3,5},{4,6},{5,3},{6,4},{7,1},{8,10},{9,15},{10,... | collective-permute-start | bytes 1572872 | tf_op jit(solution)/shard_map/ppermute | solution.py:181
  11.1 1.6 %collective-permute-start.3 = (f32[256,512]{1,0:T(8,128)S(1)}, f32[256,512]{1,0:T(8,128)S(1)}, u32[]{:S(2)}, u32[]{:S(2)}) collective-permute-start(f32[256,512]{1,0:T(8,128)S(1)} %get-tuple-element.23), channel_id=1, source_target_pairs={{0,16},{1,49},{2,18},{3,51},{4,20},{5,53},{6,22},{7,55},{8,24},{9,... | collective-permute-start | bytes 1572872 | tf_op jit(solution)/shard_map/ppermute | solution.py:181
  12.7 0.4 collective-permute-start.4
  13.1 5.7 %collective-permute-done.2.by_x = f32[256,512]{1,0:T(8,128)S(1)} collective-permute-done((f32[256,512]{1,0:T(8,128)S(1)}, f32[256,512]{1,0:T(8,128)S(1)}, u32[]{:S(2)}, u32[]{:S(2)}) %collective-permute-start.2) | collective-permute-done | bytes 524320 | tf_op jit(solution)/shard_map/ppermute | solution.py:181
  18.8 7.1 %collective-permute-done.3.by_y = f32[256,512]{1,0:T(8,128)S(1)} collective-permute-done((f32[256,512]{1,0:T(8,128)S(1)}, f32[256,512]{1,0:T(8,128)S(1)}, u32[]{:S(2)}, u32[]{:S(2)}) %collective-permute-start.3) | collective-permute-done | bytes 524320 | tf_op jit(solution)/shard_map/ppermute | solution.py:181
  25.9 0.0 collective-permute-done.4.by_xy
  25.9 0.1 cut.1
  26.1 2.4 %collective-permute-start.5 = (f32[128,256]{1,0:T(8,128)S(1)}, f32[128,256]{1,0:T(8,128)S(1)}, u32[]{:S(2)}, u32[]{:S(2)}) collective-permute-start(f32[128,256]{1,0:T(8,128)S(1)} %get-tuple-element.26), channel_id=1, source_target_pairs={{0,6},{1,3},{2,4},{3,1},{4,2},{5,7},{6,0},{7,5},{8,14},{9,11},{10,... | collective-permute-start | bytes 393224 | tf_op jit(solution)/shard_map/ppermute | solution.py:181
  28.4 2.8 %collective-permute-start.6 = (f32[128,256]{1,0:T(8,128)S(1)}, f32[128,256]{1,0:T(8,128)S(1)}, u32[]{:S(2)}, u32[]{:S(2)}) collective-permute-start(f32[128,256]{1,0:T(8,128)S(1)} %get-tuple-element.27), channel_id=1, source_target_pairs={{0,48},{1,17},{2,50},{3,19},{4,52},{5,21},{6,54},{7,23},{8,56},{9,... | collective-permute-start | bytes 393224 | tf_op jit(solution)/shard_map/ppermute | solution.py:181
  31.3 0.8 %collective-permute-start.7 = (f32[128,256]{1,0:T(8,128)S(1)}, f32[128,256]{1,0:T(8,128)S(1)}, u32[]{:S(2)}, u32[]{:S(2)}) collective-permute-start(f32[128,256]{1,0:T(8,128)S(1)} %get-tuple-element.28), channel_id=1, source_target_pairs={{0,54},{1,19},{2,52},{3,17},{4,50},{5,23},{6,48},{7,21},{8,62},{9,... | collective-permute-start | bytes 393224 | tf_op jit(solution)/shard_map/ppermute | solution.py:181
  32.1 0.3 collective-permute-done.5.by_x
  32.3 2.3 %collective-permute-done.6.by_y = f32[128,256]{1,0:T(8,128)S(1)} collective-permute-done((f32[128,256]{1,0:T(8,128)S(1)}, f32[128,256]{1,0:T(8,128)S(1)}, u32[]{:S(2)}, u32[]{:S(2)}) %collective-permute-start.6) | collective-permute-done | bytes 131104 | tf_op jit(solution)/shard_map/ppermute | solution.py:181
  34.6 4.9 %collective-permute-done.7.by_xy = f32[128,256]{1,0:T(8,128)S(1)} collective-permute-done((f32[128,256]{1,0:T(8,128)S(1)}, f32[128,256]{1,0:T(8,128)S(1)}, u32[]{:S(2)}, u32[]{:S(2)}) %collective-permute-start.7) | collective-permute-done | bytes 131104 | tf_op jit(solution)/shard_map/ppermute | solution.py:181
  39.6 0.1 pack.1
  39.7 16.0 %all_to_all.5.pieces = f32[8,32,128]{2,1,0:T(8,128)S(1)} all-to-all(f32[8,32,128]{2,1,0:T(8,128)S(1)} %pack.1), channel_id=1, replica_groups=mesh['zh'=4,'y'=4,'zl'=2,'x'=4,'c'=2] {'zh','zl'}, dimensions={0} | all-to-all | bytes 262144 | tf_op jit(solution)/shard_map/all_to_all | solution.py:234
  55.7 0.7 %last_sum.1 = f32[2,2,32,32]{3,2,1,0:T(8,128)} custom-call(f32[8,32,128]{2,1,0:T(8,128)S(1)} %all_to_all.5.pieces), custom_call_target="tpu_custom_call" | custom-call | tf_op jit(solution)/shard_map/last_sum/pallas_call | solution.py:235
Async XLA Ops:
  0.0 2.3 %copy-start = (bf16[2,512,512]{2,1,0:T(8,128)(2,1)S(1)}, bf16[2,512,512]{2,1,0:T(8,128)(2,1)}, u32[]{:S(2)}) copy-start(bf16[2,512,512]{2,1,0:T(8,128)(2,1)} %image.1) | copy-start | bytes 3145732
  0.0 1.8 %copy-start.2 = (f32[512]{0:T(512)S(1)}, f32[512]{0:T(512)}, u32[]{:S(2)}) copy-start(f32[512]{0:T(512)} %param.11) | copy-start | bytes 6148
  0.0 2.3 %copy-start.8 = (s32[2]{0:T(128)S(1)}, s32[2]{0:T(128)}, u32[]{:S(2)}) copy-start(s32[2]{0:T(128)} %sc.3) | copy-start | bytes 28
  0.0 2.3 %copy-start.7 = (s32[2]{0:T(128)S(1)}, s32[2]{0:T(128)}, u32[]{:S(2)}) copy-start(s32[2]{0:T(128)} %bo.3) | copy-start | bytes 28
  0.0 2.2 %copy-start.6 = (s32[16]{0:T(128)S(1)}, s32[16]{0:T(128)}, u32[]{:S(2)}) copy-start(s32[16]{0:T(128)} %fco.3) | copy-start | bytes 196
  0.0 2.2 %copy-start.5 = (f32[2]{0:T(128)S(1)}, f32[2]{0:T(128)}, u32[]{:S(2)}) copy-start(f32[2]{0:T(128)} %w_terms.3) | copy-start | bytes 28
  0.0 2.2 %copy-start.4 = (s32[2]{0:T(128)S(1)}, s32[2]{0:T(128)}, u32[]{:S(2)}) copy-start(s32[2]{0:T(128)} %sro.1) | copy-start | bytes 28
  0.0 2.2 %copy-start.3 = (s32[16]{0:T(128)S(1)}, s32[16]{0:T(128)}, u32[]{:S(2)}) copy-start(s32[16]{0:T(128)} %fro.1) | copy-start | bytes 196
  0.1 2.2 %copy-start.1 = (f32[512]{0:T(512)S(1)}, f32[512]{0:T(512)}, u32[]{:S(2)}) copy-start(f32[512]{0:T(512)} %param.10) | copy-start | bytes 6148
  1.7 5.4 %collective-permute-start.1 = (f32[2,512,512]{2,1,0:T(8,128)S(1)}, f32[2,512,512]{2,1,0:T(8,128)S(1)}, u32[]{:S(2)}, u32[]{:S(2)}) collective-permute-start(f32[2,512,512]{2,1,0:T(8,128)S(1)} %convert_element_type.3), channel_id=1, source_target_pairs={{0,1},{1,0},{2,3},{3,2},{4,5},{5,4},{6,7},{7,6},{8,9},{9,8},{10,11... | collective-permute-start | bytes 6291464 | tf_op jit(solution)/shard_map/ppermute | solution.py:252
  1.8 4.1 %collective-permute-start = (f32[1,512]{1,0:T(1,128)S(1)}, f32[1,512]{1,0:T(1,128)S(1)}, u32[]{:S(2)}, u32[]{:S(2)}) collective-permute-start(f32[1,512]{1,0:T(1,128)S(1)} %bitcast.3), channel_id=1, source_target_pairs={{0,1},{1,0},{2,3},{3,2},{4,5},{5,4},{6,7},{7,6},{8,9},{9,8},{10,11... | collective-permute-start | bytes 6152 | tf_op jit(solution)/shard_map/ppermute | solution.py:251
  9.6 9.3 %collective-permute-start.2 = (f32[256,512]{1,0:T(8,128)S(1)}, f32[256,512]{1,0:T(8,128)S(1)}, u32[]{:S(2)}, u32[]{:S(2)}) collective-permute-start(f32[256,512]{1,0:T(8,128)S(1)} %get-tuple-element.22), channel_id=1, source_target_pairs={{0,2},{1,7},{2,0},{3,5},{4,6},{5,3},{6,4},{7,1},{8,10},{9,15},{10,... | collective-permute-start | bytes 1572872 | tf_op jit(solution)/shard_map/ppermute | solution.py:181
  11.1 14.8 %collective-permute-start.3 = (f32[256,512]{1,0:T(8,128)S(1)}, f32[256,512]{1,0:T(8,128)S(1)}, u32[]{:S(2)}, u32[]{:S(2)}) collective-permute-start(f32[256,512]{1,0:T(8,128)S(1)} %get-tuple-element.23), channel_id=1, source_target_pairs={{0,16},{1,49},{2,18},{3,51},{4,20},{5,53},{6,22},{7,55},{8,24},{9,... | collective-permute-start | bytes 1572872 | tf_op jit(solution)/shard_map/ppermute | solution.py:181
  12.7 13.2 %collective-permute-start.4 = (f32[256,512]{1,0:T(8,128)S(1)}, f32[256,512]{1,0:T(8,128)S(1)}, u32[]{:S(2)}, u32[]{:S(2)}) collective-permute-start(f32[256,512]{1,0:T(8,128)S(1)} %get-tuple-element.24), channel_id=1, source_target_pairs={{0,18},{1,55},{2,16},{3,53},{4,22},{5,51},{6,20},{7,49},{8,26},{9,... | collective-permute-start | bytes 1572872 | tf_op jit(solution)/shard_map/ppermute | solution.py:181
  26.1 6.3 %collective-permute-start.5 = (f32[128,256]{1,0:T(8,128)S(1)}, f32[128,256]{1,0:T(8,128)S(1)}, u32[]{:S(2)}, u32[]{:S(2)}) collective-permute-start(f32[128,256]{1,0:T(8,128)S(1)} %get-tuple-element.26), channel_id=1, source_target_pairs={{0,6},{1,3},{2,4},{3,1},{4,2},{5,7},{6,0},{7,5},{8,14},{9,11},{10,... | collective-permute-start | bytes 393224 | tf_op jit(solution)/shard_map/ppermute | solution.py:181
  28.4 6.2 %collective-permute-start.6 = (f32[128,256]{1,0:T(8,128)S(1)}, f32[128,256]{1,0:T(8,128)S(1)}, u32[]{:S(2)}, u32[]{:S(2)}) collective-permute-start(f32[128,256]{1,0:T(8,128)S(1)} %get-tuple-element.27), channel_id=1, source_target_pairs={{0,48},{1,17},{2,50},{3,19},{4,52},{5,21},{6,54},{7,23},{8,56},{9,... | collective-permute-start | bytes 393224 | tf_op jit(solution)/shard_map/ppermute | solution.py:181
  31.3 8.3 %collective-permute-start.7 = (f32[128,256]{1,0:T(8,128)S(1)}, f32[128,256]{1,0:T(8,128)S(1)}, u32[]{:S(2)}, u32[]{:S(2)}) collective-permute-start(f32[128,256]{1,0:T(8,128)S(1)} %get-tuple-element.28), channel_id=1, source_target_pairs={{0,54},{1,19},{2,52},{3,17},{4,50},{5,23},{6,48},{7,21},{8,62},{9,... | collective-permute-start | bytes 393224 | tf_op jit(solution)/shard_map/ppermute | solution.py:181

commit v4 on v3

--- a/solution.py
+++ b/solution.py
@@ -82,75 +82,65 @@
     return jnp.where(sub == 0, values[0], values[1])
 
 
-def column_factors(at, w_terms, bo, sc, offset, window):
+def column_factors(at, w_terms, bo, sc, offset):
     g = offset + lax.broadcasted_iota(jnp.int32, (1, F), 1)
     i = lax.broadcasted_iota(jnp.int32, (16, F), 0)
     x = near(at["x"], i >> 3, (i >> 2) & 1, at["c"])
     sub = (i >> 1) & 1
-    zl = i & 1
     band = per_sub(sub, [bo[sc[k]] for k in range(2)])
-    coarse = turn(phase_index(g, band + ((zl * 4 + x) * 2 + at["c"]) * 32))
+    coarse = turn(phase_index(g, band + (((i & 1) * 4 + x) * 2 + at["c"]) * 32))
     waves = [chirp(w_terms[sc[k]], g) for k in range(2)]
-    wave = [per_sub(sub, [v[part] * window for v in waves]) for part in range(2)]
-    coarse = times(coarse, wave)
+    wave = [per_sub(sub, [v[part] for v in waves]) for part in range(2)]
     fine = turn((g * lax.broadcasted_iota(jnp.int32, (32, F), 0)) & (IMAGE - 1))
-    return coarse, fine
-
-
-def column_table(factors, t):
+    return times(coarse, wave), fine
+
+
+def column_table(factors, t, table):
     coarse, fine = factors
-    first, second = [], []
     for zl in range(2):
         row = 2 * t + zl
         re, im = outer([v[row : row + 1] for v in coarse], fine)
-        first += [re, im]
-        second += [-im, re]
-    return [jnp.concatenate(v, axis=0).astype(bf16) for v in (first, second)]
-
-
-def own_kernel(w_terms, fro, fco, bo, sro, sc, image, wrow, wcol, rt, g_out, w1, w2):
+        first, second = pl.ds(t * 128 + zl * 64, 32), pl.ds(t * 128 + zl * 64 + 32, 32)
+        table[first, pl.ds(0, F)] = re.astype(bf16)
+        table[second, pl.ds(0, F)] = im.astype(bf16)
+        table[first, pl.ds(F, F)] = (-im).astype(bf16)
+        table[second, pl.ds(F, F)] = re.astype(bf16)
+
+
+def own_kernel(w_terms, fro, fco, bo, sro, sc, image, wrow, wcol, rt, g_out, other, table):
     at = ids()
     me = (at["zl"] * 4 + at["x"]) * 2 + at["c"]
-    factors = column_factors(at, w_terms, bo, sc, fco[me], wcol[...])
-    for t in range(8):
-        rows = pl.ds(t * 128, 128)
-        w1[rows, :], w2[rows, :] = column_table(factors, t)
-    for n in range(4):
-        rows = pl.ds(n * 256, 256)
-        g_out[:, rows] = lax.dot_general(image[0], w1[rows, :], NT, preferred_element_type=f32) + lax.dot_general(
-            image[1], w2[rows, :], NT, preferred_element_type=f32
-        )
+    coarse, fine = column_factors(at, w_terms, bo, sc, fco[me])
+    factors = [v * wcol[...] for v in coarse], fine
+    factors_other = column_factors(at, w_terms, bo, sc, fco[me + 1 - 2 * at["c"]])
     g = fro[at["zh"] * 4 + at["y"]] + lax.broadcasted_iota(jnp.int32, (1, F), 1)
     i = lax.broadcasted_iota(jnp.int32, (16, F), 0)
     window = wrow[...] * (1.0 / 8192.0)
-    fine = turn((g * lax.broadcasted_iota(jnp.int32, (32, F), 0)) & (IMAGE - 1))
+    fine_rows = turn((g * lax.broadcasted_iota(jnp.int32, (32, F), 0)) & (IMAGE - 1))
     y = near(at["y"], i >> 3, (i >> 2) & 1, at["c"])
-    zh = i & 3
-    for k in range(2):
-        wave = [v * window for v in chirp(w_terms[sc[k]], g)]
-        coarse = times(turn(phase_index(g, sro[k] + (zh * 4 + y) * 32)), wave)
-        re, im = outer(coarse, fine)
-        rt[k, :, pl.ds(0, F)] = re.astype(bf16)
-        rt[k, :, pl.ds(F, F)] = im.astype(bf16)
-
-
-def other_kernel(w_terms, fco, bo, sc, wcol, w1, w2):
-    at = ids()
-    me = (at["zl"] * 4 + at["x"]) * 2 + (1 - at["c"])
-    factors = column_factors(at, w_terms, bo, sc, fco[me], wcol[...])
-    for t in range(8):
-        rows = pl.ds(t * 128, 128)
-        w1[rows, :], w2[rows, :] = column_table(factors, t)
-
-
-def sum_kernel(rt, g_own, w1, w2, image, keep, to_x, to_y, to_xy, gg, im):
-    im[0] = image[0].astype(bf16)
-    im[1] = image[1].astype(bf16)
+    whole = jnp.concatenate([image[0], image[1]], axis=1)
+    for n in range(4):
+        for t in (2 * n, 2 * n + 1):
+            column_table(factors, t, table)
+        rows = pl.ds(n * 256, 256)
+        g_out[:, rows] = lax.dot_general(whole, table[rows, :], NT, preferred_element_type=f32)
+        for t in (2 * n, 2 * n + 1):
+            column_table(factors_other, t, other)
+        k, half = n // 2, n % 2
+        if half == 0:
+            wave = [v * window for v in chirp(w_terms[sc[k]], g)]
+            coarse = times(turn(phase_index(g, sro[k] + ((i & 3) * 4 + y) * 32)), wave)
+        re, im = outer([v[half * 8 : half * 8 + 8] for v in coarse], fine_rows)
+        rt[k, pl.ds(half * 256, 256), pl.ds(0, F)] = re.astype(bf16)
+        rt[k, pl.ds(half * 256, 256), pl.ds(F, F)] = im.astype(bf16)
+
+
+def sum_kernel(rt, g_own, table, image, keep, to_x, to_y, to_xy, gg):
+    whole = jnp.concatenate([image[0], image[1]], axis=1).astype(bf16)
     imag = (lax.broadcasted_iota(jnp.int32, (F, 128), 1) & 32) == 32
     for n in range(4):
         rows = pl.ds(n * 256, 256)
-        g = g_own[:, rows] + lax.dot_general(im[0], w1[rows, :], NT, preferred_element_type=f32)
-        g = g + lax.dot_general(im[1], w2[rows, :], NT, preferred_element_type=f32)
+        g = g_own[:, rows] + lax.dot_general(whole, table[rows, :], NT, preferred_element_type=f32)
         for k in range(2):
             tile = g[:, k * 128 : k * 128 + 128]
             turned = jnp.where(imag, pltpu.roll(tile, 32, 1), -pltpu.roll(tile, 96, 1))
@@ -248,38 +238,32 @@
     params = pltpu.CompilerParams(vmem_limit_bytes=24 * 2**20)
     swap = [(0, 1), (1, 0)]
     window = wcol.reshape(1, F)
-    other_window = lax.ppermute(window, "c", swap)
-    other_image = lax.ppermute(image.astype(f32), "c", swap)
-    table = jax.ShapeDtypeStruct((2 * F, F), bf16)
-    rt, g_own = pl.pallas_call(
+    wide = image.astype(f32) * wcol
+    other_image = lax.ppermute(wide, "c", swap)
+    rt, g_own, other = pl.pallas_call(
         own_kernel,
-        out_shape=(jax.ShapeDtypeStruct((2, F, 2 * F), bf16), jax.ShapeDtypeStruct((F, 2 * F), f32)),
+        out_shape=(
+            jax.ShapeDtypeStruct((2, F, 2 * F), bf16),
+            jax.ShapeDtypeStruct((F, 2 * F), f32),
+            jax.ShapeDtypeStruct((2 * F, 2 * F), bf16),
+        ),
         in_specs=[smem] * 6 + [vmem] * 3,
-        out_specs=(vmem, vmem),
-        scratch_shapes=[pltpu.VMEM((2 * F, F), bf16)] * 2,
-        compiler_params=params,
-        cost_estimate=pl.CostEstimate(flops=2**30, bytes_accessed=4 * 2**20, transcendentals=0),
+        out_specs=(vmem, vmem, vmem),
+        scratch_shapes=[pltpu.VMEM((2 * F, 2 * F), bf16)],
+        compiler_params=params,
+        cost_estimate=pl.CostEstimate(flops=2**31, bytes_accessed=4 * 2**20, transcendentals=0),
         name="own_facet",
     )(w_terms, fro, fco, bo, sro, sc, image, wrow.reshape(1, F), window)
-    w1, w2 = pl.pallas_call(
-        other_kernel,
-        out_shape=(table, table),
-        in_specs=[smem] * 4 + [vmem],
-        out_specs=(vmem, vmem),
-        compiler_params=params,
-        cost_estimate=pl.CostEstimate(flops=2**22, bytes_accessed=2 * 2**20, transcendentals=0),
-        name="other_table",
-    )(w_terms, fco, bo, sc, other_window)
     pieces = pl.pallas_call(
         sum_kernel,
         out_shape=[jax.ShapeDtypeStruct((256, 512), f32)] * 4,
-        in_specs=[vmem] * 5,
+        in_specs=[vmem] * 4,
         out_specs=[vmem] * 4,
-        scratch_shapes=[pltpu.VMEM((2, 2 * F, F), bf16), pltpu.VMEM((2, F, F), bf16)],
+        scratch_shapes=[pltpu.VMEM((2, 2 * F, F), bf16)],
         compiler_params=params,
         cost_estimate=pl.CostEstimate(flops=2**31, bytes_accessed=9 * 2**20, transcendentals=0),
         name="two_stages",
-    )(rt, g_own, w1, w2, other_image)
+    )(rt, g_own, other, other_image)
     return spread(pieces)
 
 

time: 56.5 us -> 55.3 us (0.979)
  Pallas kernels: 7.96 us -> 7.23 us
    mul x0 -> x1, other arithmetic: none -> 1.59 us  [local(): wide = image.astype(f32) * wcol]
    convert_element_type x1 -> x0, other arithmetic: 1.58 us -> none  [local(): other_image = lax.ppermute(image.astype(f32), 'c', swap)]
    pallas_call x1 -> x0, Pallas kernels: 1.12 us -> none  [local(): pl.pallas_call(other_kernel, out_shape=(table, table), in_specs=[smem] *...]
  transfers between devices with their start and end apart: 8 -> 7, of which waited for: 6 -> 6; matrix products, arithmetic and copies ran while one was open for 0% -> 0% of each run, Pallas kernels for 8% -> 7%
where the time goes in v4:
time: 55.3 us; the launch traced here: 55.2 us
  waiting for transfers between devices  20.5 us (37%)
  blocking collectives  16 us (29%)
  starting transfers between devices  9.66 us (17%)
  Pallas kernels  7.23 us (13%)
  other arithmetic  1.59 us (3%)
    ppermute x6, waiting for transfers between devices, swapped(): return lax.ppermute(value, ('zh', 'y', 'zl', 'x', 'c'), perm)  20.3 us
    all_to_all x1, blocking collectives, spread(): blocks = lax.all_to_all(packed, ('zh', 'zl'), 0, 0, tiled=True)  16 us
    ppermute x6, starting transfers between devices, swapped(): return lax.ppermute(value, ('zh', 'y', 'zl', 'x', 'c'), perm)  9.57 us
    pallas_call x1, Pallas kernels, local(): pl.pallas_call(own_kernel, out_shape=(jax.ShapeDtypeStruct((2, F, 2 * F),...  3.8 us
    pallas_call x1, Pallas kernels, local(): pl.pallas_call(sum_kernel, out_shape=[jax.ShapeDtypeStruct((256, 512), f3...  2.48 us
    mul x1, other arithmetic, local(): wide = image.astype(f32) * wcol  1.59 us
  transfers between devices with their start and end apart: 7, of which 6 were waited for; matrix products, arithmetic and copies ran while one was open for 0% of the time, Pallas kernels for 7%

profile of v4, /device:TPU:32, one launch (start us, length us, event | category | flops | bytes accessed | tf_op | source)
XLA Modules:
  0.0 55.2 jit_solution(11564209419254859878)
XLA Ops:
  0.0 0.0 copy-start.1
  0.0 0.0 copy-start
  0.0 0.0 copy-start.8
  0.0 0.0 copy-start.7
  0.0 0.0 copy-start.6
  0.0 0.0 copy-start.5
  0.0 0.0 copy-start.4
  0.0 0.0 copy-start.3
  0.1 0.0 copy-start.2
  0.1 1.6 %convert_multiply_fusion = f32[2,512,512]{2,1,0:T(8,128)S(1)} fusion(bf16[2,512,512]{2,1,0:T(8,128)(2,1)} %image.1, f32[512]{0:T(512)} %param.11), kind=kLoop, calls=%fused_computation | loop fusion | flops 1048576 | bytes 3147776 | tf_op jit(solution)/shard_map/mul | solution.py:241
  1.7 0.1 collective-permute-start
  1.8 0.0 copy-done.1
  1.8 0.0 copy-done
  1.8 0.0 copy-done.8
  1.8 0.0 copy-done.7
  1.8 0.0 copy-done.6
  1.8 0.0 copy-done.5
  1.8 0.0 copy-done.4
  1.8 0.0 copy-done.3
  1.8 0.0 copy-done.2
  1.9 3.8 %own_facet.1 = (bf16[2,512,1024]{2,1,0:T(8,128)(2,1)S(1)}, f32[512,1024]{1,0:T(8,128)S(1)}, bf16[1024,1024]{1,0:T(8,128)(2,1)S(1)}) custom-call(f32[2]{0:T(128)S(1)} %copy-done.3, s32[16]{0:T(128)S(1)} %copy-done.4, s32[16]{0:T(128)S(1)} %copy-done.5, s32[2]{0:T(128)S(1)} %copy-done.6, s32[2]{0:T(128)S(1)} %copy-done.7, s32[2]{0:T(128)S(1)} %copy-done.8, ...), custom_call_target="tpu_custom_call" | custom-call | flops 2147483648 | bytes 4194304 | tf_op jit(solution)/shard_map/own_facet/pallas_call | solution.py:243
  5.7 0.2 collective-permute-done.image
  5.9 2.5 %two_stages.1 = (f32[256,512]{1,0:T(8,128)S(1)}, f32[256,512]{1,0:T(8,128)S(1)}, f32[256,512]{1,0:T(8,128)S(1)}, f32[256,512]{1,0:T(8,128)S(1)}) custom-call(bf16[2,512,1024]{2,1,0:T(8,128)(2,1)S(1)} %get-tuple-element.16.rt, f32[512,1024]{1,0:T(8,128)S(1)} %get-tuple-element.17.g_own, bf16[1024,1024]{1,0:T(8,128)(2,1)S(1)} %get-tuple-element.18.table, ...), custom_call_target="tpu_custom_call" | custom-call | flops 2147483648 | bytes 9437184 | tf_op jit(solution)/shard_map/two_stages/pallas_call | solution.py:257
  8.4 1.6 %collective-permute-start.1 = (f32[256,512]{1,0:T(8,128)S(1)}, f32[256,512]{1,0:T(8,128)S(1)}, u32[]{:S(2)}, u32[]{:S(2)}) collective-permute-start(f32[256,512]{1,0:T(8,128)S(1)} %get-tuple-element.20), channel_id=1, source_target_pairs={{0,2},{1,7},{2,0},{3,5},{4,6},{5,3},{6,4},{7,1},{8,10},{9,15},{10,... | collective-permute-start | bytes 1572872 | tf_op jit(solution)/shard_map/ppermute | solution.py:171
  10.0 1.6 %collective-permute-start.2 = (f32[256,512]{1,0:T(8,128)S(1)}, f32[256,512]{1,0:T(8,128)S(1)}, u32[]{:S(2)}, u32[]{:S(2)}) collective-permute-start(f32[256,512]{1,0:T(8,128)S(1)} %get-tuple-element.21), channel_id=1, source_target_pairs={{0,16},{1,49},{2,18},{3,51},{4,20},{5,53},{6,22},{7,55},{8,24},{9,... | collective-permute-start | bytes 1572872 | tf_op jit(solution)/shard_map/ppermute | solution.py:171
  11.6 0.4 collective-permute-start.3
  12.0 5.7 %collective-permute-done.1.by_x = f32[256,512]{1,0:T(8,128)S(1)} collective-permute-done((f32[256,512]{1,0:T(8,128)S(1)}, f32[256,512]{1,0:T(8,128)S(1)}, u32[]{:S(2)}, u32[]{:S(2)}) %collective-permute-start.1) | collective-permute-done | bytes 524320 | tf_op jit(solution)/shard_map/ppermute | solution.py:171
  17.7 7.1 %collective-permute-done.2.by_y = f32[256,512]{1,0:T(8,128)S(1)} collective-permute-done((f32[256,512]{1,0:T(8,128)S(1)}, f32[256,512]{1,0:T(8,128)S(1)}, u32[]{:S(2)}, u32[]{:S(2)}) %collective-permute-start.2) | collective-permute-done | bytes 524320 | tf_op jit(solution)/shard_map/ppermute | solution.py:171
  24.8 0.0 collective-permute-done.3.by_xy
  24.8 0.1 cut.1
  24.9 2.4 %collective-permute-start.4 = (f32[128,256]{1,0:T(8,128)S(1)}, f32[128,256]{1,0:T(8,128)S(1)}, u32[]{:S(2)}, u32[]{:S(2)}) collective-permute-start(f32[128,256]{1,0:T(8,128)S(1)} %get-tuple-element.24), channel_id=1, source_target_pairs={{0,6},{1,3},{2,4},{3,1},{4,2},{5,7},{6,0},{7,5},{8,14},{9,11},{10,... | collective-permute-start | bytes 393224 | tf_op jit(solution)/shard_map/ppermute | solution.py:171
  27.3 2.8 %collective-permute-start.5 = (f32[128,256]{1,0:T(8,128)S(1)}, f32[128,256]{1,0:T(8,128)S(1)}, u32[]{:S(2)}, u32[]{:S(2)}) collective-permute-start(f32[128,256]{1,0:T(8,128)S(1)} %get-tuple-element.25), channel_id=1, source_target_pairs={{0,48},{1,17},{2,50},{3,19},{4,52},{5,21},{6,54},{7,23},{8,56},{9,... | collective-permute-start | bytes 393224 | tf_op jit(solution)/shard_map/ppermute | solution.py:171
  30.1 0.8 %collective-permute-start.6 = (f32[128,256]{1,0:T(8,128)S(1)}, f32[128,256]{1,0:T(8,128)S(1)}, u32[]{:S(2)}, u32[]{:S(2)}) collective-permute-start(f32[128,256]{1,0:T(8,128)S(1)} %get-tuple-element.26), channel_id=1, source_target_pairs={{0,54},{1,19},{2,52},{3,17},{4,50},{5,23},{6,48},{7,21},{8,62},{9,... | collective-permute-start | bytes 393224 | tf_op jit(solution)/shard_map/ppermute | solution.py:171
  30.9 0.3 collective-permute-done.4.by_x
  31.2 2.3 %collective-permute-done.5.by_y = f32[128,256]{1,0:T(8,128)S(1)} collective-permute-done((f32[128,256]{1,0:T(8,128)S(1)}, f32[128,256]{1,0:T(8,128)S(1)}, u32[]{:S(2)}, u32[]{:S(2)}) %collective-permute-start.5) | collective-permute-done | bytes 131104 | tf_op jit(solution)/shard_map/ppermute | solution.py:171
  33.5 4.9 %collective-permute-done.6.by_xy = f32[128,256]{1,0:T(8,128)S(1)} collective-permute-done((f32[128,256]{1,0:T(8,128)S(1)}, f32[128,256]{1,0:T(8,128)S(1)}, u32[]{:S(2)}, u32[]{:S(2)}) %collective-permute-start.6) | collective-permute-done | bytes 131104 | tf_op jit(solution)/shard_map/ppermute | solution.py:171
  38.4 0.1 pack.1
  38.5 16.0 %all_to_all.5.pieces = f32[8,32,128]{2,1,0:T(8,128)S(1)} all-to-all(f32[8,32,128]{2,1,0:T(8,128)S(1)} %pack.1), channel_id=1, replica_groups=mesh['zh'=4,'y'=4,'zl'=2,'x'=4,'c'=2] {'zh','zl'}, dimensions={0} | all-to-all | bytes 262144 | tf_op jit(solution)/shard_map/all_to_all | solution.py:224
  54.5 0.7 %last_sum.1 = f32[2,2,32,32]{3,2,1,0:T(8,128)} custom-call(f32[8,32,128]{2,1,0:T(8,128)S(1)} %all_to_all.5.pieces), custom_call_target="tpu_custom_call" | custom-call | tf_op jit(solution)/shard_map/last_sum/pallas_call | solution.py:225
Async XLA Ops:
  0.0 1.8 %copy-start.1 = (f32[512]{0:T(512)S(1)}, f32[512]{0:T(512)}, u32[]{:S(2)}) copy-start(f32[512]{0:T(512)} %param.11) | copy-start | bytes 6148
  0.0 1.8 %copy-start = (bf16[2,512,512]{2,1,0:T(8,128)(2,1)S(1)}, bf16[2,512,512]{2,1,0:T(8,128)(2,1)}, u32[]{:S(2)}) copy-start(bf16[2,512,512]{2,1,0:T(8,128)(2,1)} %image.1) | copy-start | bytes 3145732
  0.0 1.8 %copy-start.8 = (s32[2]{0:T(128)S(1)}, s32[2]{0:T(128)}, u32[]{:S(2)}) copy-start(s32[2]{0:T(128)} %sc.1) | copy-start | bytes 28
  0.0 1.8 %copy-start.7 = (s32[2]{0:T(128)S(1)}, s32[2]{0:T(128)}, u32[]{:S(2)}) copy-start(s32[2]{0:T(128)} %sro.1) | copy-start | bytes 28
  0.0 1.8 %copy-start.6 = (s32[2]{0:T(128)S(1)}, s32[2]{0:T(128)}, u32[]{:S(2)}) copy-start(s32[2]{0:T(128)} %bo.1) | copy-start | bytes 28
  0.0 1.8 %copy-start.5 = (s32[16]{0:T(128)S(1)}, s32[16]{0:T(128)}, u32[]{:S(2)}) copy-start(s32[16]{0:T(128)} %fco.1) | copy-start | bytes 196
  0.0 1.8 %copy-start.4 = (s32[16]{0:T(128)S(1)}, s32[16]{0:T(128)}, u32[]{:S(2)}) copy-start(s32[16]{0:T(128)} %fro.1) | copy-start | bytes 196
  0.0 1.8 %copy-start.3 = (f32[2]{0:T(128)S(1)}, f32[2]{0:T(128)}, u32[]{:S(2)}) copy-start(f32[2]{0:T(128)} %w_terms.1) | copy-start | bytes 28
  0.1 1.8 %copy-start.2 = (f32[512]{0:T(512)S(1)}, f32[512]{0:T(512)}, u32[]{:S(2)}) copy-start(f32[512]{0:T(512)} %param.10) | copy-start | bytes 6148
  1.7 4.2 %collective-permute-start = (f32[2,512,512]{2,1,0:T(8,128)S(1)}, f32[2,512,512]{2,1,0:T(8,128)S(1)}, u32[]{:S(2)}, u32[]{:S(2)}) collective-permute-start(f32[2,512,512]{2,1,0:T(8,128)S(1)} %convert_multiply_fusion), channel_id=1, source_target_pairs={{0,1},{1,0},{2,3},{3,2},{4,5},{5,4},{6,7},{7,6},{8,9},{9,8},{10,11... | collective-permute-start | bytes 6291464 | tf_op jit(solution)/shard_map/ppermute | solution.py:242
  8.4 9.3 %collective-permute-start.1 = (f32[256,512]{1,0:T(8,128)S(1)}, f32[256,512]{1,0:T(8,128)S(1)}, u32[]{:S(2)}, u32[]{:S(2)}) collective-permute-start(f32[256,512]{1,0:T(8,128)S(1)} %get-tuple-element.20), channel_id=1, source_target_pairs={{0,2},{1,7},{2,0},{3,5},{4,6},{5,3},{6,4},{7,1},{8,10},{9,15},{10,... | collective-permute-start | bytes 1572872 | tf_op jit(solution)/shard_map/ppermute | solution.py:171
  10.0 14.8 %collective-permute-start.2 = (f32[256,512]{1,0:T(8,128)S(1)}, f32[256,512]{1,0:T(8,128)S(1)}, u32[]{:S(2)}, u32[]{:S(2)}) collective-permute-start(f32[256,512]{1,0:T(8,128)S(1)} %get-tuple-element.21), channel_id=1, source_target_pairs={{0,16},{1,49},{2,18},{3,51},{4,20},{5,53},{6,22},{7,55},{8,24},{9,... | collective-permute-start | bytes 1572872 | tf_op jit(solution)/shard_map/ppermute | solution.py:171
  11.6 13.2 %collective-permute-start.3 = (f32[256,512]{1,0:T(8,128)S(1)}, f32[256,512]{1,0:T(8,128)S(1)}, u32[]{:S(2)}, u32[]{:S(2)}) collective-permute-start(f32[256,512]{1,0:T(8,128)S(1)} %get-tuple-element.22), channel_id=1, source_target_pairs={{0,18},{1,55},{2,16},{3,53},{4,22},{5,51},{6,20},{7,49},{8,26},{9,... | collective-permute-start | bytes 1572872 | tf_op jit(solution)/shard_map/ppermute | solution.py:171
  24.9 6.3 %collective-permute-start.4 = (f32[128,256]{1,0:T(8,128)S(1)}, f32[128,256]{1,0:T(8,128)S(1)}, u32[]{:S(2)}, u32[]{:S(2)}) collective-permute-start(f32[128,256]{1,0:T(8,128)S(1)} %get-tuple-element.24), channel_id=1, source_target_pairs={{0,6},{1,3},{2,4},{3,1},{4,2},{5,7},{6,0},{7,5},{8,14},{9,11},{10,... | collective-permute-start | bytes 393224 | tf_op jit(solution)/shard_map/ppermute | solution.py:171
  27.3 6.2 %collective-permute-start.5 = (f32[128,256]{1,0:T(8,128)S(1)}, f32[128,256]{1,0:T(8,128)S(1)}, u32[]{:S(2)}, u32[]{:S(2)}) collective-permute-start(f32[128,256]{1,0:T(8,128)S(1)} %get-tuple-element.25), channel_id=1, source_target_pairs={{0,48},{1,17},{2,50},{3,19},{4,52},{5,21},{6,54},{7,23},{8,56},{9,... | collective-permute-start | bytes 393224 | tf_op jit(solution)/shard_map/ppermute | solution.py:171
  30.1 8.3 %collective-permute-start.6 = (f32[128,256]{1,0:T(8,128)S(1)}, f32[128,256]{1,0:T(8,128)S(1)}, u32[]{:S(2)}, u32[]{:S(2)}) collective-permute-start(f32[128,256]{1,0:T(8,128)S(1)} %get-tuple-element.26), channel_id=1, source_target_pairs={{0,54},{1,19},{2,52},{3,17},{4,50},{5,23},{6,48},{7,21},{8,62},{9,... | collective-permute-start | bytes 393224 | tf_op jit(solution)/shard_map/ppermute | solution.py:171

commit v5 on v4

--- a/solution.py
+++ b/solution.py
@@ -1,3 +1,4 @@
+import functools
 import itertools
 import math
 
@@ -85,8 +86,8 @@
 def column_factors(at, w_terms, bo, sc, offset):
     g = offset + lax.broadcasted_iota(jnp.int32, (1, F), 1)
     i = lax.broadcasted_iota(jnp.int32, (16, F), 0)
-    x = near(at["x"], i >> 3, (i >> 2) & 1, at["c"])
-    sub = (i >> 1) & 1
+    x = near(at["x"], (i >> 2) & 1, (i >> 1) & 1, at["c"])
+    sub = i >> 3
     band = per_sub(sub, [bo[sc[k]] for k in range(2)])
     coarse = turn(phase_index(g, band + (((i & 1) * 4 + x) * 2 + at["c"]) * 32))
     waves = [chirp(w_terms[sc[k]], g) for k in range(2)]
@@ -135,26 +136,27 @@
         rt[k, pl.ds(half * 256, 256), pl.ds(F, F)] = im.astype(bf16)
 
 
-def sum_kernel(rt, g_own, table, image, keep, to_x, to_y, to_xy, gg):
+def sum_kernel(k, rt, g_own, table, image, gg, to_x, to_y, to_xy):
     whole = jnp.concatenate([image[0], image[1]], axis=1).astype(bf16)
     imag = (lax.broadcasted_iota(jnp.int32, (F, 128), 1) & 32) == 32
-    for n in range(4):
-        rows = pl.ds(n * 256, 256)
+    for n in range(2):
+        rows = pl.ds(k * F + n * 256, 256)
         g = g_own[:, rows] + lax.dot_general(whole, table[rows, :], NT, preferred_element_type=f32)
-        for k in range(2):
-            tile = g[:, k * 128 : k * 128 + 128]
+        for low in range(2):
+            tile = g[:, low * 128 : low * 128 + 128]
             turned = jnp.where(imag, pltpu.roll(tile, 32, 1), -pltpu.roll(tile, 96, 1))
-            cols = pl.ds(n * 128, 128)
-            gg[k, pl.ds(0, F), cols] = tile.astype(bf16)
-            gg[k, pl.ds(F, F), cols] = turned.astype(bf16)
-    for k in range(2):
-        for half in range(2):
-            s = lax.dot_general(rt[k], gg[k, :, pl.ds(half * 256, 256)], NN, preferred_element_type=f32)
-            for low in range(2):
-                tile = s[:, low * 128 : low * 128 + 128]
-                cols = pl.ds(low * 256 + k * 128, 128)
-                (to_x if half else keep)[:, cols] = tile[:256]
-                (to_xy if half else to_y)[:, cols] = tile[256:]
+            cols = pl.ds(n * 256 + low * 128, 128)
+            gg[pl.ds(0, F), cols] = tile.astype(bf16)
+            gg[pl.ds(F, F), cols] = turned.astype(bf16)
+    s = lax.dot_general(rt[k], gg[:, pl.ds(256, 256)], NN, preferred_element_type=f32)
+    to_x[...] = s[:256]
+    to_xy[...] = s[256:]
+    to_y[...] = lax.dot_general(rt[k, pl.ds(256, 256), :], gg[:, pl.ds(0, 256)], NN, preferred_element_type=f32)
+
+
+def keep_kernel(rt, zero, one, keep_zero, keep_one):
+    for k, (gg, keep) in enumerate(((zero, keep_zero), (one, keep_one))):
+        keep[...] = lax.dot_general(rt[k, pl.ds(0, 256), :], gg[:, pl.ds(0, 256)], NN, preferred_element_type=f32)
 
 
 def swapped(value, axes, second):
@@ -175,12 +177,15 @@
     return [pieces[0]] + [swapped(v, axes, second) for v, axes in zip(pieces[1:], ("x", "y", "xy"))]
 
 
-def cut_kernel(own, by_x, by_y, by_xy, keep, to_x, to_y, to_xy):
-    for y in range(2):
-        for x in range(2):
-            rows, cols = pl.ds(y * 128, 128), pl.ds(x * 256, 256)
-            total = (own[rows, cols] + by_x[rows, cols]) + (by_y[rows, cols] + by_xy[rows, cols])
-            ((keep, to_x), (to_y, to_xy))[y][x][...] = total
+def cut_kernel(*refs):
+    ins, out = refs[:8], refs[8:]
+    for k in range(2):
+        own, by_x, by_y, by_xy = ins[4 * k : 4 * k + 4]
+        for y in range(2):
+            for x in range(2):
+                rows, cols = pl.ds(y * 128, 128), pl.ds(x * 128, 128)
+                total = (own[rows, cols] + by_x[rows, cols]) + (by_y[rows, cols] + by_xy[rows, cols])
+                out[2 * y + x][:, pl.ds(k * 128, 128)] = total
 
 
 def pack_kernel(own, by_x, by_y, by_xy, out):
@@ -208,11 +213,11 @@
     pieces = pl.pallas_call(
         cut_kernel,
         out_shape=[jax.ShapeDtypeStruct((128, 256), f32)] * 4,
-        in_specs=[vmem] * 4,
+        in_specs=[vmem] * 8,
         out_specs=[vmem] * 4,
         compiler_params=params,
         name="cut",
-    )(*arrived(pieces, 0))
+    )(*arrived(pieces[0], 0), *arrived(pieces[1], 0))
     packed = pl.pallas_call(
         pack_kernel,
         out_shape=jax.ShapeDtypeStruct((8, 32, 128), f32),
@@ -254,16 +259,29 @@
         cost_estimate=pl.CostEstimate(flops=2**31, bytes_accessed=4 * 2**20, transcendentals=0),
         name="own_facet",
     )(w_terms, fro, fco, bo, sro, sc, image, wrow.reshape(1, F), window)
-    pieces = pl.pallas_call(
-        sum_kernel,
-        out_shape=[jax.ShapeDtypeStruct((256, 512), f32)] * 4,
-        in_specs=[vmem] * 4,
-        out_specs=[vmem] * 4,
-        scratch_shapes=[pltpu.VMEM((2, 2 * F, F), bf16)],
-        compiler_params=params,
-        cost_estimate=pl.CostEstimate(flops=2**31, bytes_accessed=9 * 2**20, transcendentals=0),
-        name="two_stages",
-    )(rt, g_own, other, other_image)
+    piece = jax.ShapeDtypeStruct((256, 256), f32)
+    (zero, *sent_zero), (one, *sent_one) = [
+        pl.pallas_call(
+            functools.partial(sum_kernel, k),
+            out_shape=[jax.ShapeDtypeStruct((2 * F, F), bf16)] + [piece] * 3,
+            in_specs=[vmem] * 4,
+            out_specs=[vmem] * 4,
+            compiler_params=params,
+            cost_estimate=pl.CostEstimate(flops=2**30, bytes_accessed=5 * 2**20, transcendentals=0),
+            name=f"two_stages_{k}",
+        )(rt, g_own, other, other_image)
+        for k in range(2)
+    ]
+    keep_zero, keep_one = pl.pallas_call(
+        keep_kernel,
+        out_shape=[piece] * 2,
+        in_specs=[vmem] * 3,
+        out_specs=[vmem] * 2,
+        compiler_params=params,
+        cost_estimate=pl.CostEstimate(flops=2**28, bytes_accessed=3 * 2**20, transcendentals=0),
+        name="keep",
+    )(rt, zero, one)
+    pieces = [keep_zero, *sent_zero], [keep_one, *sent_one]
     return spread(pieces)
 
 

time: 55.3 us -> 54.4 us (0.984)
  waiting for transfers between devices: 20.5 us -> 14.7 us
  starting transfers between devices: 9.66 us -> 13.5 us
  Pallas kernels: 7.23 us -> 8.31 us
    ppermute x6 -> x9, waiting for transfers between devices: 20.3 us -> 14.5 us  [swapped(): return lax.ppermute(value, ('zh', 'y', 'zl', 'x', 'c'), perm)]
    ppermute x6 -> x9, starting transfers between devices: 9.57 us -> 13.4 us  [swapped(): return lax.ppermute(value, ('zh', 'y', 'zl', 'x', 'c'), perm)]
    pallas_call x1 -> x3, Pallas kernels: 2.48 us -> 3.56 us  [the longest x2 3.13 us: local(): pl.pallas_call(functools.partial(sum_kernel, k), out_shape=[jax.ShapeDtyp...]
  transfers between devices with their start and end apart: 7 -> 10, of which waited for: 6 -> 7; matrix products, arithmetic and copies ran while one was open for 0% -> 0% of each run, Pallas kernels for 7% -> 11%
where the time goes in v5:
time: 54.4 us; the launch traced here: 54.3 us
  blocking collectives  16 us (29%)
  waiting for transfers between devices  14.7 us (27%)
  starting transfers between devices  13.5 us (25%)
  Pallas kernels  8.31 us (15%)
  other arithmetic  1.59 us (3%)
    all_to_all x1, blocking collectives, spread(): blocks = lax.all_to_all(packed, ('zh', 'zl'), 0, 0, tiled=True)  16 us
    ppermute x9, waiting for transfers between devices, swapped(): return lax.ppermute(value, ('zh', 'y', 'zl', 'x', 'c'), perm)  14.5 us
    ppermute x9, starting transfers between devices, swapped(): return lax.ppermute(value, ('zh', 'y', 'zl', 'x', 'c'), perm)  13.4 us
    pallas_call x1, Pallas kernels, local(): pl.pallas_call(own_kernel, out_shape=(jax.ShapeDtypeStruct((2, F, 2 * F),...  3.82 us
    pallas_call x2, Pallas kernels, local(): pl.pallas_call(functools.partial(sum_kernel, k), out_shape=[jax.ShapeDtyp...  3.13 us
    mul x1, other arithmetic, local(): wide = image.astype(f32) * wcol  1.59 us
  transfers between devices with their start and end apart: 10, of which 7 were waited for; matrix products, arithmetic and copies ran while one was open for 0% of the time, Pallas kernels for 11%

profile of v5, /device:TPU:32, one launch (start us, length us, event | category | flops | bytes accessed | tf_op | source)
XLA Modules:
  0.0 54.3 jit_solution(18018286348753495636)
XLA Ops:
  0.0 0.0 copy-start.1
  0.0 0.0 copy-start
  0.0 0.0 copy-start.8
  0.0 0.0 copy-start.7
  0.0 0.0 copy-start.6
  0.0 0.0 copy-start.5
  0.0 0.0 copy-start.4
  0.0 0.0 copy-start.3
  0.1 0.0 copy-start.2
  0.1 1.6 %convert_multiply_fusion = f32[2,512,512]{2,1,0:T(8,128)S(1)} fusion(bf16[2,512,512]{2,1,0:T(8,128)(2,1)} %image.1, f32[512]{0:T(512)} %param.11), kind=kLoop, calls=%fused_computation | loop fusion | flops 1048576 | bytes 3147776 | tf_op jit(solution)/shard_map/mul | solution.py:246
  1.7 0.1 collective-permute-start
  1.8 0.0 copy-done.1
  1.8 0.0 copy-done
  1.8 0.0 copy-done.8
  1.8 0.0 copy-done.7
  1.8 0.0 copy-done.6
  1.8 0.0 copy-done.5
  1.8 0.0 copy-done.4
  1.8 0.0 copy-done.3
  1.8 0.0 copy-done.2
  1.9 3.8 %own_facet.1 = (bf16[2,512,1024]{2,1,0:T(8,128)(2,1)S(1)}, f32[512,1024]{1,0:T(8,128)S(1)}, bf16[1024,1024]{1,0:T(8,128)(2,1)S(1)}) custom-call(f32[2]{0:T(128)S(1)} %copy-done.3, s32[16]{0:T(128)S(1)} %copy-done.4, s32[16]{0:T(128)S(1)} %copy-done.5, s32[2]{0:T(128)S(1)} %copy-done.6, s32[2]{0:T(128)S(1)} %copy-done.7, s32[2]{0:T(128)S(1)} %copy-done.8, ...), custom_call_target="tpu_custom_call" | custom-call | flops 2147483648 | bytes 4194304 | tf_op jit(solution)/shard_map/own_facet/pallas_call | solution.py:248
  5.7 0.2 collective-permute-done.image
  5.9 1.6 %two_stages_1.1 = (bf16[1024,512]{1,0:T(8,128)(2,1)S(1)}, f32[256,256]{1,0:T(8,128)S(1)}, f32[256,256]{1,0:T(8,128)S(1)}, f32[256,256]{1,0:T(8,128)S(1)}) custom-call(bf16[2,512,1024]{2,1,0:T(8,128)(2,1)S(1)} %get-tuple-element.22.rt, f32[512,1024]{1,0:T(8,128)S(1)} %get-tuple-element.23.g_own, bf16[1024,1024]{1,0:T(8,128)(2,1)S(1)} %get-tuple-element.24.table, ...), custom_call_target="tpu_custom_call" | custom-call | flops 1073741824 | bytes 5242880 | tf_op jit(solution)/shard_map/two_stages_1/pallas_call | solution.py:264
  7.5 1.6 %collective-permute-start.4 = (f32[256,256]{1,0:T(8,128)S(1)}, f32[256,256]{1,0:T(8,128)S(1)}, u32[]{:S(2)}, u32[]{:S(2)}) collective-permute-start(f32[256,256]{1,0:T(8,128)S(1)} %get-tuple-element.32), channel_id=1, source_target_pairs={{0,2},{1,7},{2,0},{3,5},{4,6},{5,3},{6,4},{7,1},{8,10},{9,15},{10,... | collective-permute-start | bytes 786440 | tf_op jit(solution)/shard_map/ppermute | solution.py:173
  9.1 1.6 %collective-permute-start.5 = (f32[256,256]{1,0:T(8,128)S(1)}, f32[256,256]{1,0:T(8,128)S(1)}, u32[]{:S(2)}, u32[]{:S(2)}) collective-permute-start(f32[256,256]{1,0:T(8,128)S(1)} %get-tuple-element.33), channel_id=1, source_target_pairs={{0,16},{1,49},{2,18},{3,51},{4,20},{5,53},{6,22},{7,55},{8,24},{9,... | collective-permute-start | bytes 786440 | tf_op jit(solution)/shard_map/ppermute | solution.py:173
  10.6 0.4 collective-permute-start.6
  11.1 1.6 %two_stages_0.1 = (bf16[1024,512]{1,0:T(8,128)(2,1)S(1)}, f32[256,256]{1,0:T(8,128)S(1)}, f32[256,256]{1,0:T(8,128)S(1)}, f32[256,256]{1,0:T(8,128)S(1)}) custom-call(bf16[2,512,1024]{2,1,0:T(8,128)(2,1)S(1)} %get-tuple-element.22.rt, f32[512,1024]{1,0:T(8,128)S(1)} %get-tuple-element.23.g_own, bf16[1024,1024]{1,0:T(8,128)(2,1)S(1)} %get-tuple-element.24.table, ...), custom_call_target="tpu_custom_call" | custom-call | flops 1073741824 | bytes 5242880 | tf_op jit(solution)/shard_map/two_stages_0/pallas_call | solution.py:264
  12.6 1.6 %collective-permute-start.1 = (f32[256,256]{1,0:T(8,128)S(1)}, f32[256,256]{1,0:T(8,128)S(1)}, u32[]{:S(2)}, u32[]{:S(2)}) collective-permute-start(f32[256,256]{1,0:T(8,128)S(1)} %get-tuple-element.28), channel_id=1, source_target_pairs={{0,2},{1,7},{2,0},{3,5},{4,6},{5,3},{6,4},{7,1},{8,10},{9,15},{10,... | collective-permute-start | bytes 786440 | tf_op jit(solution)/shard_map/ppermute | solution.py:173
  14.2 1.6 %collective-permute-start.2 = (f32[256,256]{1,0:T(8,128)S(1)}, f32[256,256]{1,0:T(8,128)S(1)}, u32[]{:S(2)}, u32[]{:S(2)}) collective-permute-start(f32[256,256]{1,0:T(8,128)S(1)} %get-tuple-element.29), channel_id=1, source_target_pairs={{0,16},{1,49},{2,18},{3,51},{4,20},{5,53},{6,22},{7,55},{8,24},{9,... | collective-permute-start | bytes 786440 | tf_op jit(solution)/shard_map/ppermute | solution.py:173
  15.8 0.0 collective-permute-done.4.refs_5_
  15.8 0.7 %collective-permute-start.3 = (f32[256,256]{1,0:T(8,128)S(1)}, f32[256,256]{1,0:T(8,128)S(1)}, u32[]{:S(2)}, u32[]{:S(2)}) collective-permute-start(f32[256,256]{1,0:T(8,128)S(1)} %get-tuple-element.30), channel_id=1, source_target_pairs={{0,18},{1,55},{2,16},{3,53},{4,22},{5,51},{6,20},{7,49},{8,26},{9,... | collective-permute-start | bytes 786440 | tf_op jit(solution)/shard_map/ppermute | solution.py:173
  16.4 0.4 keep.1
  16.9 1.4 %collective-permute-done.5.refs_6_ = f32[256,256]{1,0:T(8,128)S(1)} collective-permute-done((f32[256,256]{1,0:T(8,128)S(1)}, f32[256,256]{1,0:T(8,128)S(1)}, u32[]{:S(2)}, u32[]{:S(2)}) %collective-permute-start.5) | collective-permute-done | bytes 262176 | tf_op jit(solution)/shard_map/ppermute | solution.py:173
  18.2 0.0 collective-permute-done.6.refs_7_
  18.2 1.5 %collective-permute-done.1.refs_1_ = f32[256,256]{1,0:T(8,128)S(1)} collective-permute-done((f32[256,256]{1,0:T(8,128)S(1)}, f32[256,256]{1,0:T(8,128)S(1)}, u32[]{:S(2)}, u32[]{:S(2)}) %collective-permute-start.1) | collective-permute-done | bytes 262176 | tf_op jit(solution)/shard_map/ppermute | solution.py:173
  19.8 4.1 %collective-permute-done.2.refs_2_ = f32[256,256]{1,0:T(8,128)S(1)} collective-permute-done((f32[256,256]{1,0:T(8,128)S(1)}, f32[256,256]{1,0:T(8,128)S(1)}, u32[]{:S(2)}, u32[]{:S(2)}) %collective-permute-start.2) | collective-permute-done | bytes 262176 | tf_op jit(solution)/shard_map/ppermute | solution.py:173
  23.9 0.0 collective-permute-done.3.refs_3_
  23.9 0.1 cut.1
  24.0 2.4 %collective-permute-start.7 = (f32[128,256]{1,0:T(8,128)S(1)}, f32[128,256]{1,0:T(8,128)S(1)}, u32[]{:S(2)}, u32[]{:S(2)}) collective-permute-start(f32[128,256]{1,0:T(8,128)S(1)} %get-tuple-element.36), channel_id=1, source_target_pairs={{0,6},{1,3},{2,4},{3,1},{4,2},{5,7},{6,0},{7,5},{8,14},{9,11},{10,... | collective-permute-start | bytes 393224 | tf_op jit(solution)/shard_map/ppermute | solution.py:173
  26.3 2.8 %collective-permute-start.8 = (f32[128,256]{1,0:T(8,128)S(1)}, f32[128,256]{1,0:T(8,128)S(1)}, u32[]{:S(2)}, u32[]{:S(2)}) collective-permute-start(f32[128,256]{1,0:T(8,128)S(1)} %get-tuple-element.37), channel_id=1, source_target_pairs={{0,48},{1,17},{2,50},{3,19},{4,52},{5,21},{6,54},{7,23},{8,56},{9,... | collective-permute-start | bytes 393224 | tf_op jit(solution)/shard_map/ppermute | solution.py:173
  29.2 0.8 %collective-permute-start.9 = (f32[128,256]{1,0:T(8,128)S(1)}, f32[128,256]{1,0:T(8,128)S(1)}, u32[]{:S(2)}, u32[]{:S(2)}) collective-permute-start(f32[128,256]{1,0:T(8,128)S(1)} %get-tuple-element.38), channel_id=1, source_target_pairs={{0,54},{1,19},{2,52},{3,17},{4,50},{5,23},{6,48},{7,21},{8,62},{9,... | collective-permute-start | bytes 393224 | tf_op jit(solution)/shard_map/ppermute | solution.py:173
  30.0 0.3 collective-permute-done.7.by_x
  30.2 2.3 %collective-permute-done.8.by_y = f32[128,256]{1,0:T(8,128)S(1)} collective-permute-done((f32[128,256]{1,0:T(8,128)S(1)}, f32[128,256]{1,0:T(8,128)S(1)}, u32[]{:S(2)}, u32[]{:S(2)}) %collective-permute-start.8) | collective-permute-done | bytes 131104 | tf_op jit(solution)/shard_map/ppermute | solution.py:173
  32.5 4.9 %collective-permute-done.9.by_xy = f32[128,256]{1,0:T(8,128)S(1)} collective-permute-done((f32[128,256]{1,0:T(8,128)S(1)}, f32[128,256]{1,0:T(8,128)S(1)}, u32[]{:S(2)}, u32[]{:S(2)}) %collective-permute-start.9) | collective-permute-done | bytes 131104 | tf_op jit(solution)/shard_map/ppermute | solution.py:173
  37.5 0.1 pack.1
  37.6 16.0 %all_to_all.5.pieces = f32[8,32,128]{2,1,0:T(8,128)S(1)} all-to-all(f32[8,32,128]{2,1,0:T(8,128)S(1)} %pack.1), channel_id=1, replica_groups=mesh['zh'=4,'y'=4,'zl'=2,'x'=4,'c'=2] {'zh','zl'}, dimensions={0} | all-to-all | bytes 262144 | tf_op jit(solution)/shard_map/all_to_all | solution.py:229
  53.6 0.7 %last_sum.1 = f32[2,2,32,32]{3,2,1,0:T(8,128)} custom-call(f32[8,32,128]{2,1,0:T(8,128)S(1)} %all_to_all.5.pieces), custom_call_target="tpu_custom_call" | custom-call | tf_op jit(solution)/shard_map/last_sum/pallas_call | solution.py:230
Async XLA Ops:
  0.0 1.8 %copy-start.1 = (f32[512]{0:T(512)S(1)}, f32[512]{0:T(512)}, u32[]{:S(2)}) copy-start(f32[512]{0:T(512)} %param.11) | copy-start | bytes 6148
  0.0 1.8 %copy-start = (bf16[2,512,512]{2,1,0:T(8,128)(2,1)S(1)}, bf16[2,512,512]{2,1,0:T(8,128)(2,1)}, u32[]{:S(2)}) copy-start(bf16[2,512,512]{2,1,0:T(8,128)(2,1)} %image.1) | copy-start | bytes 3145732
  0.0 1.8 %copy-start.8 = (s32[2]{0:T(128)S(1)}, s32[2]{0:T(128)}, u32[]{:S(2)}) copy-start(s32[2]{0:T(128)} %sc.1) | copy-start | bytes 28
  0.0 1.8 %copy-start.7 = (s32[2]{0:T(128)S(1)}, s32[2]{0:T(128)}, u32[]{:S(2)}) copy-start(s32[2]{0:T(128)} %sro.1) | copy-start | bytes 28
  0.0 1.8 %copy-start.6 = (s32[2]{0:T(128)S(1)}, s32[2]{0:T(128)}, u32[]{:S(2)}) copy-start(s32[2]{0:T(128)} %bo.1) | copy-start | bytes 28
  0.0 1.8 %copy-start.5 = (s32[16]{0:T(128)S(1)}, s32[16]{0:T(128)}, u32[]{:S(2)}) copy-start(s32[16]{0:T(128)} %fco.1) | copy-start | bytes 196
  0.0 1.8 %copy-start.4 = (s32[16]{0:T(128)S(1)}, s32[16]{0:T(128)}, u32[]{:S(2)}) copy-start(s32[16]{0:T(128)} %fro.1) | copy-start | bytes 196
  0.0 1.8 %copy-start.3 = (f32[2]{0:T(128)S(1)}, f32[2]{0:T(128)}, u32[]{:S(2)}) copy-start(f32[2]{0:T(128)} %w_terms.1) | copy-start | bytes 28
  0.1 1.8 %copy-start.2 = (f32[512]{0:T(512)S(1)}, f32[512]{0:T(512)}, u32[]{:S(2)}) copy-start(f32[512]{0:T(512)} %param.10) | copy-start | bytes 6148
  1.7 4.2 %collective-permute-start = (f32[2,512,512]{2,1,0:T(8,128)S(1)}, f32[2,512,512]{2,1,0:T(8,128)S(1)}, u32[]{:S(2)}, u32[]{:S(2)}) collective-permute-start(f32[2,512,512]{2,1,0:T(8,128)S(1)} %convert_multiply_fusion), channel_id=1, source_target_pairs={{0,1},{1,0},{2,3},{3,2},{4,5},{5,4},{6,7},{7,6},{8,9},{9,8},{10,11... | collective-permute-start | bytes 6291464 | tf_op jit(solution)/shard_map/ppermute | solution.py:247
  7.5 8.3 %collective-permute-start.4 = (f32[256,256]{1,0:T(8,128)S(1)}, f32[256,256]{1,0:T(8,128)S(1)}, u32[]{:S(2)}, u32[]{:S(2)}) collective-permute-start(f32[256,256]{1,0:T(8,128)S(1)} %get-tuple-element.32), channel_id=1, source_target_pairs={{0,2},{1,7},{2,0},{3,5},{4,6},{5,3},{6,4},{7,1},{8,10},{9,15},{10,... | collective-permute-start | bytes 786440 | tf_op jit(solution)/shard_map/ppermute | solution.py:173
  9.1 9.2 %collective-permute-start.5 = (f32[256,256]{1,0:T(8,128)S(1)}, f32[256,256]{1,0:T(8,128)S(1)}, u32[]{:S(2)}, u32[]{:S(2)}) collective-permute-start(f32[256,256]{1,0:T(8,128)S(1)} %get-tuple-element.33), channel_id=1, source_target_pairs={{0,16},{1,49},{2,18},{3,51},{4,20},{5,53},{6,22},{7,55},{8,24},{9,... | collective-permute-start | bytes 786440 | tf_op jit(solution)/shard_map/ppermute | solution.py:173
  10.6 7.6 %collective-permute-start.6 = (f32[256,256]{1,0:T(8,128)S(1)}, f32[256,256]{1,0:T(8,128)S(1)}, u32[]{:S(2)}, u32[]{:S(2)}) collective-permute-start(f32[256,256]{1,0:T(8,128)S(1)} %get-tuple-element.34), channel_id=1, source_target_pairs={{0,18},{1,55},{2,16},{3,53},{4,22},{5,51},{6,20},{7,49},{8,26},{9,... | collective-permute-start | bytes 786440 | tf_op jit(solution)/shard_map/ppermute | solution.py:173
  12.6 7.1 %collective-permute-start.1 = (f32[256,256]{1,0:T(8,128)S(1)}, f32[256,256]{1,0:T(8,128)S(1)}, u32[]{:S(2)}, u32[]{:S(2)}) collective-permute-start(f32[256,256]{1,0:T(8,128)S(1)} %get-tuple-element.28), channel_id=1, source_target_pairs={{0,2},{1,7},{2,0},{3,5},{4,6},{5,3},{6,4},{7,1},{8,10},{9,15},{10,... | collective-permute-start | bytes 786440 | tf_op jit(solution)/shard_map/ppermute | solution.py:173
  14.2 9.7 %collective-permute-start.2 = (f32[256,256]{1,0:T(8,128)S(1)}, f32[256,256]{1,0:T(8,128)S(1)}, u32[]{:S(2)}, u32[]{:S(2)}) collective-permute-start(f32[256,256]{1,0:T(8,128)S(1)} %get-tuple-element.29), channel_id=1, source_target_pairs={{0,16},{1,49},{2,18},{3,51},{4,20},{5,53},{6,22},{7,55},{8,24},{9,... | collective-permute-start | bytes 786440 | tf_op jit(solution)/shard_map/ppermute | solution.py:173
  15.8 8.1 %collective-permute-start.3 = (f32[256,256]{1,0:T(8,128)S(1)}, f32[256,256]{1,0:T(8,128)S(1)}, u32[]{:S(2)}, u32[]{:S(2)}) collective-permute-start(f32[256,256]{1,0:T(8,128)S(1)} %get-tuple-element.30), channel_id=1, source_target_pairs={{0,18},{1,55},{2,16},{3,53},{4,22},{5,51},{6,20},{7,49},{8,26},{9,... | collective-permute-start | bytes 786440 | tf_op jit(solution)/shard_map/ppermute | solution.py:173
  24.0 6.3 %collective-permute-start.7 = (f32[128,256]{1,0:T(8,128)S(1)}, f32[128,256]{1,0:T(8,128)S(1)}, u32[]{:S(2)}, u32[]{:S(2)}) collective-permute-start(f32[128,256]{1,0:T(8,128)S(1)} %get-tuple-element.36), channel_id=1, source_target_pairs={{0,6},{1,3},{2,4},{3,1},{4,2},{5,7},{6,0},{7,5},{8,14},{9,11},{10,... | collective-permute-start | bytes 393224 | tf_op jit(solution)/shard_map/ppermute | solution.py:173
  26.3 6.2 %collective-permute-start.8 = (f32[128,256]{1,0:T(8,128)S(1)}, f32[128,256]{1,0:T(8,128)S(1)}, u32[]{:S(2)}, u32[]{:S(2)}) collective-permute-start(f32[128,256]{1,0:T(8,128)S(1)} %get-tuple-element.37), channel_id=1, source_target_pairs={{0,48},{1,17},{2,50},{3,19},{4,52},{5,21},{6,54},{7,23},{8,56},{9,... | collective-permute-start | bytes 393224 | tf_op jit(solution)/shard_map/ppermute | solution.py:173
  29.2 8.3 %collective-permute-start.9 = (f32[128,256]{1,0:T(8,128)S(1)}, f32[128,256]{1,0:T(8,128)S(1)}, u32[]{:S(2)}, u32[]{:S(2)}) collective-permute-start(f32[128,256]{1,0:T(8,128)S(1)} %get-tuple-element.38), channel_id=1, source_target_pairs={{0,54},{1,19},{2,52},{3,17},{4,50},{5,23},{6,48},{7,21},{8,62},{9,... | collective-permute-start | bytes 393224 | tf_op jit(solution)/shard_map/ppermute | solution.py:173

commit v6 on v5

--- a/solution.py
+++ b/solution.py
@@ -136,8 +136,8 @@
         rt[k, pl.ds(half * 256, 256), pl.ds(F, F)] = im.astype(bf16)
 
 
-def sum_kernel(k, rt, g_own, table, image, gg, to_x, to_y, to_xy):
-    whole = jnp.concatenate([image[0], image[1]], axis=1).astype(bf16)
+def sum_kernel(k, rt, g_own, table, real, imaginary, gg, to_x, to_y, to_xy):
+    whole = jnp.concatenate([real[...], imaginary[...]], axis=1).astype(bf16)
     imag = (lax.broadcasted_iota(jnp.int32, (F, 128), 1) & 32) == 32
     for n in range(2):
         rows = pl.ds(k * F + n * 256, 256)
@@ -243,8 +243,8 @@
     params = pltpu.CompilerParams(vmem_limit_bytes=24 * 2**20)
     swap = [(0, 1), (1, 0)]
     window = wcol.reshape(1, F)
-    wide = image.astype(f32) * wcol
-    other_image = lax.ppermute(wide, "c", swap)
+    wide = [image[part].astype(f32) * wcol for part in range(2)]
+    other_real, other_imag = [lax.ppermute(v, "c", swap) for v in wide]
     rt, g_own, other = pl.pallas_call(
         own_kernel,
         out_shape=(
@@ -264,12 +264,12 @@
         pl.pallas_call(
             functools.partial(sum_kernel, k),
             out_shape=[jax.ShapeDtypeStruct((2 * F, F), bf16)] + [piece] * 3,
-            in_specs=[vmem] * 4,
+            in_specs=[vmem] * 5,
             out_specs=[vmem] * 4,
             compiler_params=params,
             cost_estimate=pl.CostEstimate(flops=2**30, bytes_accessed=5 * 2**20, transcendentals=0),
             name=f"two_stages_{k}",
-        )(rt, g_own, other, other_image)
+        )(rt, g_own, other, other_real, other_imag)
         for k in range(2)
     ]
     keep_zero, keep_one = pl.pallas_call(

time: 54.4 us -> 54.6 us (level)
  transfers between devices with their start and end apart: 10 -> 11, of which waited for: 7 -> 6; matrix products, arithmetic and copies ran while one was open for 0% -> 0% of each run, Pallas kernels for 11% -> 11%
where the time goes in v6:
time: 54.6 us; the launch traced here: 54.5 us
  blocking collectives  16 us (29%)
  waiting for transfers between devices  14.5 us (27%)
  starting transfers between devices  14 us (26%)
  Pallas kernels  8.31 us (15%)
  other arithmetic  1.57 us (3%)
    all_to_all x1, blocking collectives, spread(): blocks = lax.all_to_all(packed, ('zh', 'zl'), 0, 0, tiled=True)  16 us
    ppermute x9, waiting for transfers between devices, swapped(): return lax.ppermute(value, ('zh', 'y', 'zl', 'x', 'c'), perm)  14.5 us
    ppermute x9, starting transfers between devices, swapped(): return lax.ppermute(value, ('zh', 'y', 'zl', 'x', 'c'), perm)  13.4 us
    pallas_call x1, Pallas kernels, local(): pl.pallas_call(own_kernel, out_shape=(jax.ShapeDtypeStruct((2, F, 2 * F),...  3.81 us
    pallas_call x2, Pallas kernels, local(): pl.pallas_call(functools.partial(sum_kernel, k), out_shape=[jax.ShapeDtyp...  3.14 us
    mul x1, other arithmetic, local(): wide = [image[part].astype(f32) * wcol for part in range(2)]  1.57 us
  transfers between devices with their start and end apart: 11, of which 6 were waited for; matrix products, arithmetic and copies ran while one was open for 0% of the time, Pallas kernels for 11%

profile of v6, /device:TPU:32, one launch (start us, length us, event | category | flops | bytes accessed | tf_op | source)
XLA Modules:
  0.0 54.5 jit_solution(15628549694765792297)
XLA Ops:
  0.0 0.0 copy-start.1
  0.0 0.0 copy-start
  0.0 0.0 copy-start.7
  0.0 0.0 copy-start.6
  0.0 0.0 copy-start.5
  0.0 0.0 copy-start.4
  0.0 0.0 copy-start.3
  0.1 0.0 copy-start.2
  0.1 1.6 %convert_multiply_fusion = (f32[512,512]{1,0:T(8,128)S(1)}, f32[512,512]{1,0:T(8,128)S(1)}) fusion(bf16[2,512,512]{2,1,0:T(8,128)(2,1)} %image.1, f32[512]{0:T(512)} %param.11), kind=kLoop, calls=%fused_computation | loop fusion | flops 1048576 | bytes 3147776 | tf_op jit(solution)/shard_map/mul | solution.py:246
  1.6 0.1 collective-permute-start.1
  1.7 0.5 collective-permute-start
  2.2 0.0 copy-done.1
  2.2 0.0 copy-done
  2.2 0.0 copy-done.8
  2.2 0.0 copy-done.7
  2.3 0.0 copy-done.6
  2.3 0.0 copy-done.5
  2.3 0.0 copy-done.4
  2.3 0.0 copy-done.3
  2.3 0.0 copy-done.2
  2.3 3.8 %own_facet.1 = (bf16[2,512,1024]{2,1,0:T(8,128)(2,1)S(1)}, f32[512,1024]{1,0:T(8,128)S(1)}, bf16[1024,1024]{1,0:T(8,128)(2,1)S(1)}) custom-call(f32[2]{0:T(128)S(1)} %copy-done.3, s32[16]{0:T(128)S(1)} %copy-done.4, s32[16]{0:T(128)S(1)} %copy-done.5, s32[2]{0:T(128)S(1)} %copy-done.6, s32[2]{0:T(128)S(1)} %copy-done.7, s32[2]{0:T(128)S(1)} %copy-done.8, ...), custom_call_target="tpu_custom_call" | custom-call | flops 2147483648 | bytes 4194304 | tf_op jit(solution)/shard_map/own_facet/pallas_call | solution.py:248
  6.1 0.0 collective-permute-done.1.imaginary
  6.1 0.0 collective-permute-done.real
  6.1 1.6 %two_stages_1.1 = (bf16[1024,512]{1,0:T(8,128)(2,1)S(1)}, f32[256,256]{1,0:T(8,128)S(1)}, f32[256,256]{1,0:T(8,128)S(1)}, f32[256,256]{1,0:T(8,128)S(1)}) custom-call(bf16[2,512,1024]{2,1,0:T(8,128)(2,1)S(1)} %get-tuple-element.22.rt, f32[512,1024]{1,0:T(8,128)S(1)} %get-tuple-element.23.g_own, bf16[1024,1024]{1,0:T(8,128)(2,1)S(1)} %get-tuple-element.24.table, ...), custom_call_target="tpu_custom_call" | custom-call | flops 1073741824 | bytes 5242880 | tf_op jit(solution)/shard_map/two_stages_1/pallas_call | solution.py:264
  7.7 1.6 %collective-permute-start.5 = (f32[256,256]{1,0:T(8,128)S(1)}, f32[256,256]{1,0:T(8,128)S(1)}, u32[]{:S(2)}, u32[]{:S(2)}) collective-permute-start(f32[256,256]{1,0:T(8,128)S(1)} %get-tuple-element.32), channel_id=1, source_target_pairs={{0,2},{1,7},{2,0},{3,5},{4,6},{5,3},{6,4},{7,1},{8,10},{9,15},{10,... | collective-permute-start | bytes 786440 | tf_op jit(solution)/shard_map/ppermute | solution.py:173
  9.3 1.6 %collective-permute-start.6 = (f32[256,256]{1,0:T(8,128)S(1)}, f32[256,256]{1,0:T(8,128)S(1)}, u32[]{:S(2)}, u32[]{:S(2)}) collective-permute-start(f32[256,256]{1,0:T(8,128)S(1)} %get-tuple-element.33), channel_id=1, source_target_pairs={{0,16},{1,49},{2,18},{3,51},{4,20},{5,53},{6,22},{7,55},{8,24},{9,... | collective-permute-start | bytes 786440 | tf_op jit(solution)/shard_map/ppermute | solution.py:173
  10.9 0.4 collective-permute-start.7
  11.3 1.6 %two_stages_0.1 = (bf16[1024,512]{1,0:T(8,128)(2,1)S(1)}, f32[256,256]{1,0:T(8,128)S(1)}, f32[256,256]{1,0:T(8,128)S(1)}, f32[256,256]{1,0:T(8,128)S(1)}) custom-call(bf16[2,512,1024]{2,1,0:T(8,128)(2,1)S(1)} %get-tuple-element.22.rt, f32[512,1024]{1,0:T(8,128)S(1)} %get-tuple-element.23.g_own, bf16[1024,1024]{1,0:T(8,128)(2,1)S(1)} %get-tuple-element.24.table, ...), custom_call_target="tpu_custom_call" | custom-call | flops 1073741824 | bytes 5242880 | tf_op jit(solution)/shard_map/two_stages_0/pallas_call | solution.py:264
  12.9 1.6 %collective-permute-start.2 = (f32[256,256]{1,0:T(8,128)S(1)}, f32[256,256]{1,0:T(8,128)S(1)}, u32[]{:S(2)}, u32[]{:S(2)}) collective-permute-start(f32[256,256]{1,0:T(8,128)S(1)} %get-tuple-element.28), channel_id=1, source_target_pairs={{0,2},{1,7},{2,0},{3,5},{4,6},{5,3},{6,4},{7,1},{8,10},{9,15},{10,... | collective-permute-start | bytes 786440 | tf_op jit(solution)/shard_map/ppermute | solution.py:173
  14.4 1.6 %collective-permute-start.3 = (f32[256,256]{1,0:T(8,128)S(1)}, f32[256,256]{1,0:T(8,128)S(1)}, u32[]{:S(2)}, u32[]{:S(2)}) collective-permute-start(f32[256,256]{1,0:T(8,128)S(1)} %get-tuple-element.29), channel_id=1, source_target_pairs={{0,16},{1,49},{2,18},{3,51},{4,20},{5,53},{6,22},{7,55},{8,24},{9,... | collective-permute-start | bytes 786440 | tf_op jit(solution)/shard_map/ppermute | solution.py:173
  16.0 0.0 collective-permute-done.5.refs_5_
  16.0 0.7 %collective-permute-start.4 = (f32[256,256]{1,0:T(8,128)S(1)}, f32[256,256]{1,0:T(8,128)S(1)}, u32[]{:S(2)}, u32[]{:S(2)}) collective-permute-start(f32[256,256]{1,0:T(8,128)S(1)} %get-tuple-element.30), channel_id=1, source_target_pairs={{0,18},{1,55},{2,16},{3,53},{4,22},{5,51},{6,20},{7,49},{8,26},{9,... | collective-permute-start | bytes 786440 | tf_op jit(solution)/shard_map/ppermute | solution.py:173
  16.7 0.4 keep.1
  17.1 1.3 %collective-permute-done.6.refs_6_ = f32[256,256]{1,0:T(8,128)S(1)} collective-permute-done((f32[256,256]{1,0:T(8,128)S(1)}, f32[256,256]{1,0:T(8,128)S(1)}, u32[]{:S(2)}, u32[]{:S(2)}) %collective-permute-start.6) | collective-permute-done | bytes 262176 | tf_op jit(solution)/shard_map/ppermute | solution.py:173
  18.5 0.0 collective-permute-done.7.refs_7_
  18.5 1.5 %collective-permute-done.2.refs_1_ = f32[256,256]{1,0:T(8,128)S(1)} collective-permute-done((f32[256,256]{1,0:T(8,128)S(1)}, f32[256,256]{1,0:T(8,128)S(1)}, u32[]{:S(2)}, u32[]{:S(2)}) %collective-permute-start.2) | collective-permute-done | bytes 262176 | tf_op jit(solution)/shard_map/ppermute | solution.py:173
  20.0 4.1 %collective-permute-done.3.refs_2_ = f32[256,256]{1,0:T(8,128)S(1)} collective-permute-done((f32[256,256]{1,0:T(8,128)S(1)}, f32[256,256]{1,0:T(8,128)S(1)}, u32[]{:S(2)}, u32[]{:S(2)}) %collective-permute-start.3) | collective-permute-done | bytes 262176 | tf_op jit(solution)/shard_map/ppermute | solution.py:173
  24.1 0.0 collective-permute-done.4.refs_3_
  24.1 0.1 cut.1
  24.2 2.4 %collective-permute-start.8 = (f32[128,256]{1,0:T(8,128)S(1)}, f32[128,256]{1,0:T(8,128)S(1)}, u32[]{:S(2)}, u32[]{:S(2)}) collective-permute-start(f32[128,256]{1,0:T(8,128)S(1)} %get-tuple-element.36), channel_id=1, source_target_pairs={{0,6},{1,3},{2,4},{3,1},{4,2},{5,7},{6,0},{7,5},{8,14},{9,11},{10,... | collective-permute-start | bytes 393224 | tf_op jit(solution)/shard_map/ppermute | solution.py:173
  26.6 2.8 %collective-permute-start.9 = (f32[128,256]{1,0:T(8,128)S(1)}, f32[128,256]{1,0:T(8,128)S(1)}, u32[]{:S(2)}, u32[]{:S(2)}) collective-permute-start(f32[128,256]{1,0:T(8,128)S(1)} %get-tuple-element.37), channel_id=1, source_target_pairs={{0,48},{1,17},{2,50},{3,19},{4,52},{5,21},{6,54},{7,23},{8,56},{9,... | collective-permute-start | bytes 393224 | tf_op jit(solution)/shard_map/ppermute | solution.py:173
  29.4 0.8 %collective-permute-start.10 = (f32[128,256]{1,0:T(8,128)S(1)}, f32[128,256]{1,0:T(8,128)S(1)}, u32[]{:S(2)}, u32[]{:S(2)}) collective-permute-start(f32[128,256]{1,0:T(8,128)S(1)} %get-tuple-element.38), channel_id=1, source_target_pairs={{0,54},{1,19},{2,52},{3,17},{4,50},{5,23},{6,48},{7,21},{8,62},{9,... | collective-permute-start | bytes 393224 | tf_op jit(solution)/shard_map/ppermute | solution.py:173
  30.2 0.3 collective-permute-done.8.by_x
  30.5 2.3 %collective-permute-done.9.by_y = f32[128,256]{1,0:T(8,128)S(1)} collective-permute-done((f32[128,256]{1,0:T(8,128)S(1)}, f32[128,256]{1,0:T(8,128)S(1)}, u32[]{:S(2)}, u32[]{:S(2)}) %collective-permute-start.9) | collective-permute-done | bytes 131104 | tf_op jit(solution)/shard_map/ppermute | solution.py:173
  32.8 4.9 %collective-permute-done.10.by_xy = f32[128,256]{1,0:T(8,128)S(1)} collective-permute-done((f32[128,256]{1,0:T(8,128)S(1)}, f32[128,256]{1,0:T(8,128)S(1)}, u32[]{:S(2)}, u32[]{:S(2)}) %collective-permute-start.10) | collective-permute-done | bytes 131104 | tf_op jit(solution)/shard_map/ppermute | solution.py:173
  37.7 0.1 pack.1
  37.8 16.0 %all_to_all.5.pieces = f32[8,32,128]{2,1,0:T(8,128)S(1)} all-to-all(f32[8,32,128]{2,1,0:T(8,128)S(1)} %pack.1), channel_id=1, replica_groups=mesh['zh'=4,'y'=4,'zl'=2,'x'=4,'c'=2] {'zh','zl'}, dimensions={0} | all-to-all | bytes 262144 | tf_op jit(solution)/shard_map/all_to_all | solution.py:229
  53.8 0.7 %last_sum.1 = f32[2,2,32,32]{3,2,1,0:T(8,128)} custom-call(f32[8,32,128]{2,1,0:T(8,128)S(1)} %all_to_all.5.pieces), custom_call_target="tpu_custom_call" | custom-call | tf_op jit(solution)/shard_map/last_sum/pallas_call | solution.py:230
  (1 shorter events, 0.0 us)
Async XLA Ops:
  0.0 2.2 %copy-start.1 = (f32[512]{0:T(512)S(1)}, f32[512]{0:T(512)}, u32[]{:S(2)}) copy-start(f32[512]{0:T(512)} %param.11) | copy-start | bytes 6148
  0.0 2.2 %copy-start = (bf16[2,512,512]{2,1,0:T(8,128)(2,1)S(1)}, bf16[2,512,512]{2,1,0:T(8,128)(2,1)}, u32[]{:S(2)}) copy-start(bf16[2,512,512]{2,1,0:T(8,128)(2,1)} %image.1) | copy-start | bytes 3145732
  0.0 2.2 %copy-start.8 = (s32[2]{0:T(128)S(1)}, s32[2]{0:T(128)}, u32[]{:S(2)}) copy-start(s32[2]{0:T(128)} %sc.1) | copy-start | bytes 28
  0.0 2.2 %copy-start.7 = (s32[2]{0:T(128)S(1)}, s32[2]{0:T(128)}, u32[]{:S(2)}) copy-start(s32[2]{0:T(128)} %sro.1) | copy-start | bytes 28
  0.0 2.2 %copy-start.6 = (s32[2]{0:T(128)S(1)}, s32[2]{0:T(128)}, u32[]{:S(2)}) copy-start(s32[2]{0:T(128)} %bo.1) | copy-start | bytes 28
  0.0 2.2 %copy-start.5 = (s32[16]{0:T(128)S(1)}, s32[16]{0:T(128)}, u32[]{:S(2)}) copy-start(s32[16]{0:T(128)} %fco.1) | copy-start | bytes 196
  0.0 2.2 %copy-start.4 = (s32[16]{0:T(128)S(1)}, s32[16]{0:T(128)}, u32[]{:S(2)}) copy-start(s32[16]{0:T(128)} %fro.1) | copy-start | bytes 196
  0.0 2.2 %copy-start.3 = (f32[2]{0:T(128)S(1)}, f32[2]{0:T(128)}, u32[]{:S(2)}) copy-start(f32[2]{0:T(128)} %w_terms.1) | copy-start | bytes 28
  0.1 2.2 %copy-start.2 = (f32[512]{0:T(512)S(1)}, f32[512]{0:T(512)}, u32[]{:S(2)}) copy-start(f32[512]{0:T(512)} %param.10) | copy-start | bytes 6148
  1.6 4.5 %collective-permute-start.1 = (f32[512,512]{1,0:T(8,128)S(1)}, f32[512,512]{1,0:T(8,128)S(1)}, u32[]{:S(2)}, u32[]{:S(2)}) collective-permute-start(f32[512,512]{1,0:T(8,128)S(1)} %get-tuple-element.39), channel_id=1, source_target_pairs={{0,1},{1,0},{2,3},{3,2},{4,5},{5,4},{6,7},{7,6},{8,9},{9,8},{10,11... | collective-permute-start | bytes 3145736 | tf_op jit(solution)/shard_map/ppermute | solution.py:247
  1.7 4.4 %collective-permute-start = (f32[512,512]{1,0:T(8,128)S(1)}, f32[512,512]{1,0:T(8,128)S(1)}, u32[]{:S(2)}, u32[]{:S(2)}) collective-permute-start(f32[512,512]{1,0:T(8,128)S(1)} %get-tuple-element.40), channel_id=1, source_target_pairs={{0,1},{1,0},{2,3},{3,2},{4,5},{5,4},{6,7},{7,6},{8,9},{9,8},{10,11... | collective-permute-start | bytes 3145736 | tf_op jit(solution)/shard_map/ppermute | solution.py:247
  7.7 8.3 %collective-permute-start.5 = (f32[256,256]{1,0:T(8,128)S(1)}, f32[256,256]{1,0:T(8,128)S(1)}, u32[]{:S(2)}, u32[]{:S(2)}) collective-permute-start(f32[256,256]{1,0:T(8,128)S(1)} %get-tuple-element.32), channel_id=1, source_target_pairs={{0,2},{1,7},{2,0},{3,5},{4,6},{5,3},{6,4},{7,1},{8,10},{9,15},{10,... | collective-permute-start | bytes 786440 | tf_op jit(solution)/shard_map/ppermute | solution.py:173
  9.3 9.2 %collective-permute-start.6 = (f32[256,256]{1,0:T(8,128)S(1)}, f32[256,256]{1,0:T(8,128)S(1)}, u32[]{:S(2)}, u32[]{:S(2)}) collective-permute-start(f32[256,256]{1,0:T(8,128)S(1)} %get-tuple-element.33), channel_id=1, source_target_pairs={{0,16},{1,49},{2,18},{3,51},{4,20},{5,53},{6,22},{7,55},{8,24},{9,... | collective-permute-start | bytes 786440 | tf_op jit(solution)/shard_map/ppermute | solution.py:173
  10.9 7.6 %collective-permute-start.7 = (f32[256,256]{1,0:T(8,128)S(1)}, f32[256,256]{1,0:T(8,128)S(1)}, u32[]{:S(2)}, u32[]{:S(2)}) collective-permute-start(f32[256,256]{1,0:T(8,128)S(1)} %get-tuple-element.34), channel_id=1, source_target_pairs={{0,18},{1,55},{2,16},{3,53},{4,22},{5,51},{6,20},{7,49},{8,26},{9,... | collective-permute-start | bytes 786440 | tf_op jit(solution)/shard_map/ppermute | solution.py:173
  12.9 7.1 %collective-permute-start.2 = (f32[256,256]{1,0:T(8,128)S(1)}, f32[256,256]{1,0:T(8,128)S(1)}, u32[]{:S(2)}, u32[]{:S(2)}) collective-permute-start(f32[256,256]{1,0:T(8,128)S(1)} %get-tuple-element.28), channel_id=1, source_target_pairs={{0,2},{1,7},{2,0},{3,5},{4,6},{5,3},{6,4},{7,1},{8,10},{9,15},{10,... | collective-permute-start | bytes 786440 | tf_op jit(solution)/shard_map/ppermute | solution.py:173
  14.4 9.7 %collective-permute-start.3 = (f32[256,256]{1,0:T(8,128)S(1)}, f32[256,256]{1,0:T(8,128)S(1)}, u32[]{:S(2)}, u32[]{:S(2)}) collective-permute-start(f32[256,256]{1,0:T(8,128)S(1)} %get-tuple-element.29), channel_id=1, source_target_pairs={{0,16},{1,49},{2,18},{3,51},{4,20},{5,53},{6,22},{7,55},{8,24},{9,... | collective-permute-start | bytes 786440 | tf_op jit(solution)/shard_map/ppermute | solution.py:173
  16.0 8.1 %collective-permute-start.4 = (f32[256,256]{1,0:T(8,128)S(1)}, f32[256,256]{1,0:T(8,128)S(1)}, u32[]{:S(2)}, u32[]{:S(2)}) collective-permute-start(f32[256,256]{1,0:T(8,128)S(1)} %get-tuple-element.30), channel_id=1, source_target_pairs={{0,18},{1,55},{2,16},{3,53},{4,22},{5,51},{6,20},{7,49},{8,26},{9,... | collective-permute-start | bytes 786440 | tf_op jit(solution)/shard_map/ppermute | solution.py:173
  24.2 6.3 %collective-permute-start.8 = (f32[128,256]{1,0:T(8,128)S(1)}, f32[128,256]{1,0:T(8,128)S(1)}, u32[]{:S(2)}, u32[]{:S(2)}) collective-permute-start(f32[128,256]{1,0:T(8,128)S(1)} %get-tuple-element.36), channel_id=1, source_target_pairs={{0,6},{1,3},{2,4},{3,1},{4,2},{5,7},{6,0},{7,5},{8,14},{9,11},{10,... | collective-permute-start | bytes 393224 | tf_op jit(solution)/shard_map/ppermute | solution.py:173
  26.6 6.2 %collective-permute-start.9 = (f32[128,256]{1,0:T(8,128)S(1)}, f32[128,256]{1,0:T(8,128)S(1)}, u32[]{:S(2)}, u32[]{:S(2)}) collective-permute-start(f32[128,256]{1,0:T(8,128)S(1)} %get-tuple-element.37), channel_id=1, source_target_pairs={{0,48},{1,17},{2,50},{3,19},{4,52},{5,21},{6,54},{7,23},{8,56},{9,... | collective-permute-start | bytes 393224 | tf_op jit(solution)/shard_map/ppermute | solution.py:173
  29.4 8.3 %collective-permute-start.10 = (f32[128,256]{1,0:T(8,128)S(1)}, f32[128,256]{1,0:T(8,128)S(1)}, u32[]{:S(2)}, u32[]{:S(2)}) collective-permute-start(f32[128,256]{1,0:T(8,128)S(1)} %get-tuple-element.38), channel_id=1, source_target_pairs={{0,54},{1,19},{2,52},{3,17},{4,50},{5,23},{6,48},{7,21},{8,62},{9,... | collective-permute-start | bytes 393224 | tf_op jit(solution)/shard_map/ppermute | solution.py:173
